TPU v7x, 512 devices: a whole 4x4x16 slice. The times are simulated.
512 devices in a mesh: head: 8 (over z_hi, core), inner: 16 (over x, y), outer: 4 (over z_lo).
Axes of the slice: x: 4, y: 4, z: 16 (z_hi: 4, z_lo: 4; z = z_hi * 4 + z_lo), core: 2. Of those that a mesh axis runs over, the one named last changes fastest.
Arguments:
- queries: bfloat16 [8192, 8192], P(('inner', 'outer', 'head')), may hold values from -6 to 6
- key_head_rows: bfloat16 [8192, 1024], P(('inner', 'outer', 'head')), may hold values from -6 to 6
- value_head_rows: bfloat16 [8192, 1024], P(('inner', 'outer', 'head')), may hold values from -0.59765625 to 0.59765625
- output_gradient: bfloat16 [8192, 8192], P(('inner', 'outer', 'head')), may hold values from -6 to 6
- support_values: bfloat16 [8192, 8192], P(('inner', 'outer', 'head')), may hold values from -6 to 6
- thresholds: bfloat16 [8192, 64], P(('inner', 'outer', 'head')), may hold values from 0.3984375 to 1.1953125
- gate_row_sums: bfloat16 [8192, 64], P(('inner', 'outer', 'head')), may hold values from 10 to 100
- token_pos: int32 [8192], replicated, may hold values from 0 to 8191, as said below
- block_mask: int32 [64, 64], replicated, may hold values from 0 to 1, as said below
Outputs:
- grad_queries: bfloat16 [8192, 8192], P(('inner', 'outer', 'head'))
- key_gradient: bfloat16 [8192, 1024], P(('inner', 'outer', 'head'))
- value_gradient: bfloat16 [8192, 1024], P(('inner', 'outer', 'head'))
Inputs may be any that keep to these rules, and one draw needn't show every extreme that they name: `token_pos`: A permutation of the 8192 positions in which each aligned run of 128 stored rows holds 128 consecutive positions in increasing order, the first a multiple of 128. `block_mask`: entry [a, b] is 1 where queries of position block a may see keys of position block b; the diagonal is 1.
All inputs are finite; a program needn't handle non-finite values.
Results may differ from a plain program's by a relative error of at most 0.005.
Values may be sent and summed in bfloat16 or wider, within the bound.
No kernel may reach another device: no remote copies, remote signals or barrier semaphores. Data moves between devices by JAX's collectives and lax.ppermute only.
A program may use at most 64 MiB of HBM per device.

v0:
```python
import jax
import jax.numpy as jnp
from jax import lax
from jax.sharding import PartitionSpec as P

QUERY_HEADS = 64
KEY_HEADS = 8
HEAD_WIDTH = 128
BLK = 128
GROUP = 8


def from_behind(value, axis, steps):
    count = lax.axis_size(axis)
    pairs = [(source, (source + steps) % count) for source in range(count)]
    return lax.ppermute(value, axis, pairs)


def local(
    queries,
    key_head_rows,
    value_head_rows,
    output_gradient,
    support_values,
    thresholds,
    gate_row_sums,
    token_pos,
    block_mask,
):
    preceding_rows = queries.shape[0]
    score_scale = HEAD_WIDTH ** (-0.5)
    local_query, local_grad, local_support, local_thresh, local_sums, local_keys, local_values = (
        lax.all_to_all(
            queries.reshape(preceding_rows, QUERY_HEADS, HEAD_WIDTH),
            "head",
            split_axis=1,
            concat_axis=0,
            tiled=True,
        ),
        lax.all_to_all(
            output_gradient.reshape(preceding_rows, QUERY_HEADS, HEAD_WIDTH),
            "head",
            split_axis=1,
            concat_axis=0,
            tiled=True,
        ),
        lax.all_to_all(
            support_values.reshape(preceding_rows, QUERY_HEADS, HEAD_WIDTH),
            "head",
            split_axis=1,
            concat_axis=0,
            tiled=True,
        ),
        lax.all_to_all(thresholds, "head", split_axis=1, concat_axis=0, tiled=True),
        lax.all_to_all(gate_row_sums, "head", split_axis=1, concat_axis=0, tiled=True),
        lax.all_to_all(
            key_head_rows.reshape(preceding_rows, KEY_HEADS, HEAD_WIDTH),
            "head",
            split_axis=1,
            concat_axis=0,
            tiled=True,
        ),
        lax.all_to_all(
            value_head_rows.reshape(preceding_rows, KEY_HEADS, HEAD_WIDTH),
            "head",
            split_axis=1,
            concat_axis=0,
            tiled=True,
        ),
    )
    tokens = local_query.shape[0]
    kv_heads = local_keys.shape[1]
    query_blocks = local_query.reshape(tokens, kv_heads, GROUP, HEAD_WIDTH)
    grad_blocks = local_grad.reshape(tokens, kv_heads, GROUP, HEAD_WIDTH)
    row_inner_product = jnp.einsum(
        "thd,thd->th", local_grad, local_support, preferred_element_type=jnp.float32
    )
    offset_average = jnp.transpose(
        (row_inner_product / local_sums.astype(jnp.float32)).reshape(tokens, kv_heads, GROUP),
        (1, 2, 0),
    )
    thresh_heads = jnp.transpose(
        local_thresh.astype(jnp.float32).reshape(tokens, kv_heads, GROUP), (1, 2, 0)
    )
    block_ids = token_pos[::BLK] // BLK
    blocks_dev = tokens // BLK
    inner_size = lax.axis_size("inner")
    outer_size = lax.axis_size("outer")
    inner_index = lax.axis_index("inner")
    outer_index = lax.axis_index("outer")
    own_context = inner_index * outer_size + outer_index
    offsets = jnp.arange(BLK, dtype=jnp.int32)

    def visit_tile(totals, key_now, value_now, piece_no, context, key_blk, query_blk):
        query_block_id = block_ids[own_context * blocks_dev + query_blk]
        key_block_id = block_ids[context * blocks_dev + key_blk]
        active = (block_mask[query_block_id, key_block_id] == 1) & (key_block_id <= query_block_id)

        def compute(inner_totals):
            query_gradient, grad_key, grad_value = inner_totals
            key_row = piece_no * tokens + key_blk * BLK
            key_part = lax.dynamic_slice_in_dim(key_now, key_row, BLK, 0)
            value_part = lax.dynamic_slice_in_dim(value_now, key_row, BLK, 0)
            thresh_part = thresh_heads[..., None]
            mean_part = offset_average[..., None]
            allowed = (key_block_id * BLK + offsets)[None, :] <= (query_block_id * BLK + offsets)[
                :, None
            ]
            scores = (
                jnp.einsum(
                    "ikgd,jkd->kgij", query_blocks, key_part, preferred_element_type=jnp.float32
                )
                * score_scale
            )
            gate_value = jnp.where(allowed, jnp.maximum(0.5 * scores - thresh_part, 0.0), 0.0)
            dprob = jnp.einsum(
                "ikgd,jkd->kgij", grad_blocks, value_part, preferred_element_type=jnp.float32
            )
            dscore = (score_scale * gate_value * (dprob - mean_part)).astype(jnp.bfloat16)
            prob_low = (gate_value * gate_value).astype(jnp.bfloat16)
            query_update = query_gradient + jnp.einsum(
                "kgij,jkd->ikgd", dscore, key_part, preferred_element_type=jnp.float32
            )
            key_update = lax.dynamic_slice_in_dim(grad_key, key_row, BLK, 0) + jnp.einsum(
                "kgij,ikgd->jkd", dscore, query_blocks, preferred_element_type=jnp.float32
            )
            value_update = lax.dynamic_slice_in_dim(grad_value, key_row, BLK, 0) + jnp.einsum(
                "kgij,ikgd->jkd", prob_low, grad_blocks, preferred_element_type=jnp.float32
            )
            query_gradient = query_update
            grad_key = lax.dynamic_update_slice_in_dim(grad_key, key_update, key_row, 0)
            grad_value = lax.dynamic_update_slice_in_dim(grad_value, value_update, key_row, 0)
            return (query_gradient, grad_key, grad_value)

        def unchanged(inner_totals):
            return inner_totals

        return lax.cond(active, compute, unchanged, totals)

    key_all, value_all = (
        lax.all_gather(local_keys, "outer", axis=0, tiled=True),
        lax.all_gather(local_values, "outer", axis=0, tiled=True),
    )

    def context_inner(cycle_step, piece_no):
        return (inner_index - cycle_step) % inner_size * outer_size + piece_no

    def rotate_keys_inner(key_now, value_now):
        return from_behind((key_now, value_now), "inner", 1)

    def rotate_grads_inner(grad_key, grad_value):
        return from_behind((grad_key, grad_value), "inner", 1)

    per_step = outer_size * blocks_dev * blocks_dev
    zero_keys = jnp.zeros(key_all.shape, jnp.float32)
    zero_query = jnp.zeros(query_blocks.shape, jnp.float32)

    def one_step(cycle_step, state):
        key_now, value_now, query_gradient, grad_key, grad_value = state

        def visit(tile_no, totals):
            piece_no = tile_no // (blocks_dev * blocks_dev)
            key_blk = tile_no // blocks_dev % blocks_dev
            query_blk = tile_no % blocks_dev
            return visit_tile(
                totals,
                key_now,
                value_now,
                piece_no,
                context_inner(cycle_step, piece_no),
                key_blk,
                query_blk,
            )

        query_gradient, grad_key, grad_value = lax.fori_loop(
            0, per_step, visit, (query_gradient, grad_key, grad_value)
        )
        key_now, value_now = rotate_keys_inner(key_now, value_now)
        grad_key, grad_value = rotate_grads_inner(grad_key, grad_value)
        return (key_now, value_now, query_gradient, grad_key, grad_value)

    final_state = lax.fori_loop(
        0, inner_size, one_step, (key_all, value_all, zero_query, zero_keys, zero_keys)
    )
    query_gradient = final_state[2]
    grad_key = final_state[3]
    grad_value = final_state[4]
    own_keys, own_values = (
        lax.psum_scatter(grad_key, "outer", scatter_dimension=0, tiled=True),
        lax.psum_scatter(grad_value, "outer", scatter_dimension=0, tiled=True),
    )
    query_low = query_gradient.astype(jnp.bfloat16).reshape(tokens, kv_heads * GROUP, HEAD_WIDTH)
    back_query, backward_keys, backward_values = (
        lax.all_to_all(query_low, "head", split_axis=0, concat_axis=1, tiled=True),
        lax.all_to_all(
            own_keys.astype(jnp.bfloat16), "head", split_axis=0, concat_axis=1, tiled=True
        ),
        lax.all_to_all(
            own_values.astype(jnp.bfloat16), "head", split_axis=0, concat_axis=1, tiled=True
        ),
    )
    return (
        back_query.reshape(preceding_rows, QUERY_HEADS * HEAD_WIDTH),
        backward_keys.reshape(preceding_rows, KEY_HEADS * HEAD_WIDTH),
        backward_values.reshape(preceding_rows, KEY_HEADS * HEAD_WIDTH),
    )


def solution(mesh):
    return jax.shard_map(
        local,
        mesh=mesh,
        in_specs=(
            P(("inner", "outer", "head"), None),
            P(("inner", "outer", "head"), None),
            P(("inner", "outer", "head"), None),
            P(("inner", "outer", "head"), None),
            P(("inner", "outer", "head"), None),
            P(("inner", "outer", "head"), None),
            P(("inner", "outer", "head"), None),
            P(),
            P(),
        ),
        out_specs=(
            P(("inner", "outer", "head"), None),
            P(("inner", "outer", "head"), None),
            P(("inner", "outer", "head"), None),
        ),
        check_vma=False,
    )
```

profile of v0, /device:TPU:37, one launch (start us, length us, event | category | flops | bytes accessed | tf_op | source)
XLA Modules:
  0.0 1086.1 jit_solution(17363772127892574176)
XLA Ops:
  8.6 15.0 %all-to-all-start.6 = ((bf16[16,8,8]{0,2,1:T(8,128)(2,1)}), bf16[16,8,8]{0,2,1:T(8,128)(2,1)S(1)}, u32[]{:S(2)}, u32[]{:S(2)}) async-start(bf16[16,8,8]{0,2,1:T(8,128)(2,1)} %bitcast.50), calls=%async_computation.6 | async-start | bytes 32768 | tf_op jit(solution)/shard_map/all_to_all | solution.py:55
  24.3 11.2 %all-to-all-done.6 = bf16[16,8,8]{0,2,1:T(8,128)(2,1)S(1)} async-done(((bf16[16,8,8]{0,2,1:T(8,128)(2,1)}), bf16[16,8,8]{0,2,1:T(8,128)(2,1)S(1)}, u32[]{:S(2)}, u32[]{:S(2)}) %all-to-all-start.6) | async-done | bytes 2080 | tf_op jit(solution)/shard_map/all_to_all | solution.py:55
  35.5 4.0 all-to-all-start.3
  40.1 11.3 %all-to-all-done.3 = bf16[16,8,8]{0,2,1:T(8,128)(2,1)S(1)} async-done(((bf16[16,8,8]{0,2,1:T(8,128)(2,1)}), bf16[16,8,8]{0,2,1:T(8,128)(2,1)S(1)}, u32[]{:S(2)}, u32[]{:S(2)}) %all-to-all-start.3) | async-done | bytes 2080 | tf_op jit(solution)/shard_map/all_to_all | solution.py:54
  51.4 4.0 all-to-all-start
  56.0 11.4 %all-to-all-done = bf16[16,8,128]{2,0,1:T(8,128)(2,1)S(1)} async-done(((bf16[16,8,128]{2,0,1:T(8,128)(2,1)}), bf16[16,8,128]{2,0,1:T(8,128)(2,1)S(1)}, u32[]{:S(2)}, u32[]{:S(2)}) %all-to-all-start) | async-done | bytes 32800 | tf_op jit(solution)/shard_map/all_to_all | solution.py:56
  67.3 4.0 all-to-all-start.1
  72.1 11.2 %all-to-all-done.1 = bf16[16,8,128]{2,0,1:T(8,128)(2,1)S(1)} async-done(((bf16[16,8,128]{2,0,1:T(8,128)(2,1)}), bf16[16,8,128]{2,0,1:T(8,128)(2,1)S(1)}, u32[]{:S(2)}, u32[]{:S(2)}) %all-to-all-start.1) | async-done | bytes 32800 | tf_op jit(solution)/shard_map/all_to_all | solution.py:63
  83.3 4.1 all-to-all-start.4
  88.2 18.8 %all-to-all-done.4 = bf16[16,64,128]{2,0,1:T(8,128)(2,1)S(1)} async-done(((bf16[16,64,128]{2,0,1:T(8,128)(2,1)}), bf16[16,64,128]{2,0,1:T(8,128)(2,1)S(1)}, u32[]{:S(2)}, u32[]{:S(2)}) %all-to-all-start.4) | async-done | bytes 262176 | tf_op jit(solution)/shard_map/all_to_all | solution.py:40
  106.9 5.0 all-to-all-start.5
  112.7 18.6 %all-to-all-done.5 = bf16[16,64,128]{2,0,1:T(8,128)(2,1)S(1)} async-done(((bf16[16,64,128]{2,0,1:T(8,128)(2,1)}), bf16[16,64,128]{2,0,1:T(8,128)(2,1)S(1)}, u32[]{:S(2)}, u32[]{:S(2)}) %all-to-all-start.5) | async-done | bytes 262176 | tf_op jit(solution)/shard_map/all_to_all | solution.py:47
  131.4 7.1 all-to-all-start.2
  142.1 13.5 %all_gather.6 = bf16[512,1,128]{2,0,1:T(8,128)(2,1)S(1)} all-gather(bf16[128,1,128]{2,0,1:T(8,128)(2,1)S(1)} %bitcast.202), channel_id=1, replica_groups=mesh['head'=8,'inner'=16,'outer'=4] {'outer'}, dimensions={0}, use_global_device_ids=true | all-gather | bytes 163840 | tf_op jit(solution)/shard_map/all_gather | solution.py:141
  155.5 10.2 all_gather.7
  166.5 797.3 %while.84 = (s32[]{:T(128)}, bf16[512,1,128]{2,0,1:T(8,128)(2,1)S(1)}, bf16[512,1,128]{2,0,1:T(8,128)(2,1)S(1)}, f32[128,1,8,128]{0,3,2,1:T(8,128)S(1)}, f32[512...) while((s32[]{:T(128)}, ...), condition=%wide.region_5.6_spmd.clone.clone, body=%wide.region_0.5_spmd.clone.clone.sunk | while | flops 169263392 | bytes 9581283 | solution.py:182
  166.6 30.9 %while.85 = (s32[]{:T(128)}, f32[128,1,8,128]{0,3,2,1:T(8,128)S(1)}, f32[512,1,128]{2,0,1:T(8,128)S(1)}, f32[512,1,128]{2,0,1:T(8,128)S(1)}, s32[]{:T(128)}, /*i...) while((s32[]{:T(128)}, ...), condition=%wide.region_4.4_spmd.clone, body=%wide.region_1.3_spmd.clone.sunk | while | flops 169263376 | bytes 4861505 | solution.py:175
  197.5 5.8 collective-permute-start.2
  209.1 6.1 collective-permute-done.3
  220.3 23.1 %while.85 = (s32[]{:T(128)}, f32[128,1,8,128]{0,3,2,1:T(8,128)S(1)}, f32[512,1,128]{2,0,1:T(8,128)S(1)}, f32[512,1,128]{2,0,1:T(8,128)S(1)}, s32[]{:T(128)}, /*i...) while((s32[]{:T(128)}, ...), condition=%wide.region_4.4_spmd.clone, body=%wide.region_1.3_spmd.clone.sunk | while | flops 169263376 | bytes 4861505 | solution.py:175
  243.4 8.5 collective-permute-start.2
  264.2 28.3 %while.85 = (s32[]{:T(128)}, f32[128,1,8,128]{0,3,2,1:T(8,128)S(1)}, f32[512,1,128]{2,0,1:T(8,128)S(1)}, f32[512,1,128]{2,0,1:T(8,128)S(1)}, s32[]{:T(128)}, /*i...) while((s32[]{:T(128)}, ...), condition=%wide.region_4.4_spmd.clone, body=%wide.region_1.3_spmd.clone.sunk | while | flops 169263376 | bytes 4861505 | solution.py:175
  292.5 4.7 collective-permute-start.2
  312.8 30.9 %while.85 = (s32[]{:T(128)}, f32[128,1,8,128]{0,3,2,1:T(8,128)S(1)}, f32[512,1,128]{2,0,1:T(8,128)S(1)}, f32[512,1,128]{2,0,1:T(8,128)S(1)}, s32[]{:T(128)}, /*i...) while((s32[]{:T(128)}, ...), condition=%wide.region_4.4_spmd.clone, body=%wide.region_1.3_spmd.clone.sunk | while | flops 169263376 | bytes 4861505 | solution.py:175
  347.5 7.2 collective-permute-start
  358.1 6.2 collective-permute-done.1
  364.4 25.7 %while.85 = (s32[]{:T(128)}, f32[128,1,8,128]{0,3,2,1:T(8,128)S(1)}, f32[512,1,128]{2,0,1:T(8,128)S(1)}, f32[512,1,128]{2,0,1:T(8,128)S(1)}, s32[]{:T(128)}, /*i...) while((s32[]{:T(128)}, ...), condition=%wide.region_4.4_spmd.clone, body=%wide.region_1.3_spmd.clone.sunk | while | flops 169263376 | bytes 4861505 | solution.py:175
  390.1 7.9 collective-permute-start.2
  400.0 6.1 collective-permute-start
  406.1 3.6 collective-permute-start.1
  410.3 5.3 collective-permute-done.1
  415.7 28.3 %while.85 = (s32[]{:T(128)}, f32[128,1,8,128]{0,3,2,1:T(8,128)S(1)}, f32[512,1,128]{2,0,1:T(8,128)S(1)}, f32[512,1,128]{2,0,1:T(8,128)S(1)}, s32[]{:T(128)}, /*i...) while((s32[]{:T(128)}, ...), condition=%wide.region_4.4_spmd.clone, body=%wide.region_1.3_spmd.clone.sunk | while | flops 169263376 | bytes 4861505 | solution.py:175
  444.0 7.2 collective-permute-start.2
  465.7 28.3 %while.85 = (s32[]{:T(128)}, f32[128,1,8,128]{0,3,2,1:T(8,128)S(1)}, f32[512,1,128]{2,0,1:T(8,128)S(1)}, f32[512,1,128]{2,0,1:T(8,128)S(1)}, s32[]{:T(128)}, /*i...) while((s32[]{:T(128)}, ...), condition=%wide.region_4.4_spmd.clone, body=%wide.region_1.3_spmd.clone.sunk | while | flops 169263376 | bytes 4861505 | solution.py:175
  494.1 8.4 collective-permute-start.2
  515.6 28.3 %while.85 = (s32[]{:T(128)}, f32[128,1,8,128]{0,3,2,1:T(8,128)S(1)}, f32[512,1,128]{2,0,1:T(8,128)S(1)}, f32[512,1,128]{2,0,1:T(8,128)S(1)}, s32[]{:T(128)}, /*i...) while((s32[]{:T(128)}, ...), condition=%wide.region_4.4_spmd.clone, body=%wide.region_1.3_spmd.clone.sunk | while | flops 169263376 | bytes 4861505 | solution.py:175
  543.9 3.8 collective-permute-start.2
  549.9 4.7 collective-permute-start
  564.2 25.7 %while.85 = (s32[]{:T(128)}, f32[128,1,8,128]{0,3,2,1:T(8,128)S(1)}, f32[512,1,128]{2,0,1:T(8,128)S(1)}, f32[512,1,128]{2,0,1:T(8,128)S(1)}, s32[]{:T(128)}, /*i...) while((s32[]{:T(128)}, ...), condition=%wide.region_4.4_spmd.clone, body=%wide.region_1.3_spmd.clone.sunk | while | flops 169263376 | bytes 4861505 | solution.py:175
  589.9 9.4 collective-permute-start.2
  612.9 30.9 %while.85 = (s32[]{:T(128)}, f32[128,1,8,128]{0,3,2,1:T(8,128)S(1)}, f32[512,1,128]{2,0,1:T(8,128)S(1)}, f32[512,1,128]{2,0,1:T(8,128)S(1)}, s32[]{:T(128)}, /*i...) while((s32[]{:T(128)}, ...), condition=%wide.region_4.4_spmd.clone, body=%wide.region_1.3_spmd.clone.sunk | while | flops 169263376 | bytes 4861505 | solution.py:175
  643.7 6.3 collective-permute-start.2
  655.9 5.3 collective-permute-done.3
  666.3 28.3 %while.85 = (s32[]{:T(128)}, f32[128,1,8,128]{0,3,2,1:T(8,128)S(1)}, f32[512,1,128]{2,0,1:T(8,128)S(1)}, f32[512,1,128]{2,0,1:T(8,128)S(1)}, s32[]{:T(128)}, /*i...) while((s32[]{:T(128)}, ...), condition=%wide.region_4.4_spmd.clone, body=%wide.region_1.3_spmd.clone.sunk | while | flops 169263376 | bytes 4861505 | solution.py:175
  703.9 4.2 collective-permute-done.3
  713.8 23.1 %while.85 = (s32[]{:T(128)}, f32[128,1,8,128]{0,3,2,1:T(8,128)S(1)}, f32[512,1,128]{2,0,1:T(8,128)S(1)}, f32[512,1,128]{2,0,1:T(8,128)S(1)}, s32[]{:T(128)}, /*i...) while((s32[]{:T(128)}, ...), condition=%wide.region_4.4_spmd.clone, body=%wide.region_1.3_spmd.clone.sunk | while | flops 169263376 | bytes 4861505 | solution.py:175
  736.9 10.4 collective-permute-start.2
  753.1 5.6 collective-permute-done.3
  764.3 28.3 %while.85 = (s32[]{:T(128)}, f32[128,1,8,128]{0,3,2,1:T(8,128)S(1)}, f32[512,1,128]{2,0,1:T(8,128)S(1)}, f32[512,1,128]{2,0,1:T(8,128)S(1)}, s32[]{:T(128)}, /*i...) while((s32[]{:T(128)}, ...), condition=%wide.region_4.4_spmd.clone, body=%wide.region_1.3_spmd.clone.sunk | while | flops 169263376 | bytes 4861505 | solution.py:175
  801.9 4.6 collective-permute-done.3
  812.1 28.3 %while.85 = (s32[]{:T(128)}, f32[128,1,8,128]{0,3,2,1:T(8,128)S(1)}, f32[512,1,128]{2,0,1:T(8,128)S(1)}, f32[512,1,128]{2,0,1:T(8,128)S(1)}, s32[]{:T(128)}, /*i...) while((s32[]{:T(128)}, ...), condition=%wide.region_4.4_spmd.clone, body=%wide.region_1.3_spmd.clone.sunk | while | flops 169263376 | bytes 4861505 | solution.py:175
  850.5 4.5 collective-permute-done.3
  860.7 30.9 %while.85 = (s32[]{:T(128)}, f32[128,1,8,128]{0,3,2,1:T(8,128)S(1)}, f32[512,1,128]{2,0,1:T(8,128)S(1)}, f32[512,1,128]{2,0,1:T(8,128)S(1)}, s32[]{:T(128)}, /*i...) while((s32[]{:T(128)}, ...), condition=%wide.region_4.4_spmd.clone, body=%wide.region_1.3_spmd.clone.sunk | while | flops 169263376 | bytes 4861505 | solution.py:175
  900.8 3.6 collective-permute-done.3
  910.1 30.9 %while.85 = (s32[]{:T(128)}, f32[128,1,8,128]{0,3,2,1:T(8,128)S(1)}, f32[512,1,128]{2,0,1:T(8,128)S(1)}, f32[512,1,128]{2,0,1:T(8,128)S(1)}, s32[]{:T(128)}, /*i...) while((s32[]{:T(128)}, ...), condition=%wide.region_4.4_spmd.clone, body=%wide.region_1.3_spmd.clone.sunk | while | flops 169263376 | bytes 4861505 | solution.py:175
  948.6 4.8 collective-permute-done.2
  953.4 4.7 collective-permute-done.3
  965.3 27.1 %reduce-scatter.3.cloned.1.call-done = f32[128,1,128]{2,1,0:T(1,128)} async-done(((f32[512,1,128]{2,1,0:T(1,128)}), f32[128,1,128]{2,1,0:T(1,128)}) %reduce-scatter.3.cloned.1.call-update) | async-done | bytes 65552 | tf_op jit(solution)/shard_map/reduce_scatter | solution.py:189
  995.3 14.1 %all-to-all-start.8 = ((bf16[8,2,1024]{2,1,0:T(2,128)(2,1)}), bf16[8,2,1024]{2,1,0:T(2,128)(2,1)S(1)}, u32[]{:S(2)}, u32[]{:S(2)}) async-start(bf16[8,2,1024]{2,1,0:T(2,128)(2,1)} %reshape.129), calls=%async_computation.9 | async-start | bytes 65536 | tf_op jit(solution)/shard_map/all_to_all | solution.py:195
  1009.4 15.8 %reduce-scatter.5.cloned.1.call-done = f32[128,1,128]{2,1,0:T(1,128)} async-done(((f32[512,1,128]{2,1,0:T(1,128)}), f32[128,1,128]{2,1,0:T(1,128)}) %reduce-scatter.5.cloned.1.call-update) | async-done | bytes 65552 | tf_op jit(solution)/shard_map/reduce_scatter | solution.py:190
  1027.6 13.5 %all-to-all-start.9 = ((bf16[8,2,1024]{2,1,0:T(2,128)(2,1)}), bf16[8,2,1024]{2,1,0:T(2,128)(2,1)S(1)}, u32[]{:S(2)}, u32[]{:S(2)}) async-start(bf16[8,2,1024]{2,1,0:T(2,128)(2,1)} %reshape.131), calls=%async_computation.11 | async-start | bytes 65536 | tf_op jit(solution)/shard_map/all_to_all | solution.py:198
  1042.0 11.1 %all-to-all-done.9 = bf16[8,2,1024]{2,1,0:T(2,128)(2,1)S(1)} async-done(((bf16[8,2,1024]{2,1,0:T(2,128)(2,1)}), bf16[8,2,1024]{2,1,0:T(2,128)(2,1)S(1)}, u32[]{:S(2)}, u32[]{:S(2)}) %all-to-all-start.9) | async-done | bytes 32800 | tf_op jit(solution)/shard_map/all_to_all | solution.py:198
  1053.1 4.0 all-to-all-start.7
  1057.9 20.4 %all-to-all-done.7 = bf16[128,8,128]{2,1,0:T(8,128)(2,1)S(1)} async-done(((bf16[128,8,128]{2,1,0:T(8,128)(2,1)}), bf16[128,8,128]{2,1,0:T(8,128)(2,1)S(1)}, u32[]{:S(2)}, u32[]{:S(2)}) %all-to-all-start.7) | async-done | bytes 262176 | tf_op jit(solution)/shard_map/all_to_all | solution.py:194
  (658 shorter events, 459.8 us)
Async XLA Ops:
  8.6 26.9 %all-to-all-start.6 = ((bf16[16,8,8]{0,2,1:T(8,128)(2,1)}), bf16[16,8,8]{0,2,1:T(8,128)(2,1)S(1)}, u32[]{:S(2)}, u32[]{:S(2)}) async-start(bf16[16,8,8]{0,2,1:T(8,128)(2,1)} %bitcast.50), calls=%async_computation.6 | async-start | bytes 32768 | tf_op jit(solution)/shard_map/all_to_all | solution.py:55
  35.5 15.9 %all-to-all-start.3 = ((bf16[16,8,8]{0,2,1:T(8,128)(2,1)}), bf16[16,8,8]{0,2,1:T(8,128)(2,1)S(1)}, u32[]{:S(2)}, u32[]{:S(2)}) async-start(bf16[16,8,8]{0,2,1:T(8,128)(2,1)} %bitcast.36), calls=%async_computation.3 | async-start | bytes 32768 | tf_op jit(solution)/shard_map/all_to_all | solution.py:54
  51.4 15.9 %all-to-all-start = ((bf16[16,8,128]{2,0,1:T(8,128)(2,1)}), bf16[16,8,128]{2,0,1:T(8,128)(2,1)S(1)}, u32[]{:S(2)}, u32[]{:S(2)}) async-start(bf16[16,8,128]{2,0,1:T(8,128)(2,1)} %copy_bitcast_fusion.7), calls=%async_computation | async-start | bytes 65536 | tf_op jit(solution)/shard_map/all_to_all | solution.py:56
  67.3 16.0 %all-to-all-start.1 = ((bf16[16,8,128]{2,0,1:T(8,128)(2,1)}), bf16[16,8,128]{2,0,1:T(8,128)(2,1)S(1)}, u32[]{:S(2)}, u32[]{:S(2)}) async-start(bf16[16,8,128]{2,0,1:T(8,128)(2,1)} %copy_bitcast_fusion.6), calls=%async_computation.1 | async-start | bytes 65536 | tf_op jit(solution)/shard_map/all_to_all | solution.py:63
  83.3 23.6 %all-to-all-start.4 = ((bf16[16,64,128]{2,0,1:T(8,128)(2,1)}), bf16[16,64,128]{2,0,1:T(8,128)(2,1)S(1)}, u32[]{:S(2)}, u32[]{:S(2)}) async-start(bf16[16,64,128]{2,0,1:T(8,128)(2,1)} %copy_bitcast_fusion.2), calls=%async_computation.4 | async-start | bytes 524288 | tf_op jit(solution)/shard_map/all_to_all | solution.py:40
  106.9 24.4 %all-to-all-start.5 = ((bf16[16,64,128]{2,0,1:T(8,128)(2,1)}), bf16[16,64,128]{2,0,1:T(8,128)(2,1)S(1)}, u32[]{:S(2)}, u32[]{:S(2)}) async-start(bf16[16,64,128]{2,0,1:T(8,128)(2,1)} %copy_bitcast_fusion.1), calls=%async_computation.5 | async-start | bytes 524288 | tf_op jit(solution)/shard_map/all_to_all | solution.py:47
  131.4 34.9 %all-to-all-start.2 = ((bf16[16,64,128]{2,0,1:T(8,128)(2,1)}), bf16[16,64,128]{2,0,1:T(8,128)(2,1)S(1)}, u32[]{:S(2)}, u32[]{:S(2)}) async-start(bf16[16,64,128]{2,0,1:T(8,128)(2,1)} %copy_bitcast_fusion.3), calls=%async_computation.2 | async-start | bytes 524288 | tf_op jit(solution)/shard_map/all_to_all | solution.py:33
  138.5 853.9 %reduce-scatter.3.cloned.1.call-start = ((), (), s32[]{:S(2)}) async-start(), calls=%async_computation.12 | async-start | bytes 327680 | tf_op jit(solution)/shard_map/reduce_scatter | solution.py:189
  197.5 11.6 %collective-permute-start.2 = (f32[512,1,128]{2,0,1:T(8,128)S(1)}, f32[512,1,128]{2,0,1:T(8,128)S(1)}, u32[]{:S(2)}, u32[]{:S(2)}) collective-permute-start(f32[512,1,128]{2,0,1:T(8,128)S(1)} %get-tuple-element.1639), channel_id=1, source_target_pairs={{0,4},{4,8},{8,12},{12,16},{16,20},{20,24},{24,28},{28,32},{32,36}... | collective-permute-start | bytes 786440 | tf_op jit(solution)/shard_map/while/body/eval_jaxpr/ppermute | solution.py:16
  203.2 11.9 %collective-permute-start.3 = (f32[512,1,128]{2,0,1:T(8,128)S(1)}, f32[512,1,128]{2,0,1:T(8,128)S(1)}, u32[]{:S(2)}, u32[]{:S(2)}) collective-permute-start(f32[512,1,128]{2,0,1:T(8,128)S(1)} %get-tuple-element.1640), channel_id=1, source_target_pairs={{0,4},{4,8},{8,12},{12,16},{16,20},{20,24},{24,28},{28,32},{32,36}... | collective-permute-start | bytes 786440 | tf_op jit(solution)/shard_map/while/body/eval_jaxpr/ppermute | solution.py:16
  205.2 12.2 %collective-permute-start = (bf16[512,1,128]{2,0,1:T(8,128)(2,1)S(1)}, bf16[512,1,128]{2,0,1:T(8,128)(2,1)S(1)}, u32[]{:S(2)}, u32[]{:S(2)}) collective-permute-start(bf16[512,1,128]{2,0,1:T(8,128)(2,1)S(1)} %get-tuple-element.1805), channel_id=1, source_target_pairs={{0,4},{4,8},{8,12},{12,16},{16,20},{20,24},{24,28},{28,32},{32,36}... | collective-permute-start | bytes 393224 | tf_op jit(solution)/shard_map/while/body/eval_jaxpr/ppermute | solution.py:16
  207.1 13.1 %collective-permute-start.1 = (bf16[512,1,128]{2,0,1:T(8,128)(2,1)S(1)}, bf16[512,1,128]{2,0,1:T(8,128)(2,1)S(1)}, u32[]{:S(2)}, u32[]{:S(2)}) collective-permute-start(bf16[512,1,128]{2,0,1:T(8,128)(2,1)S(1)} %get-tuple-element.1815), channel_id=1, source_target_pairs={{0,4},{4,8},{8,12},{12,16},{16,20},{20,24},{24,28},{28,32},{32,36}... | collective-permute-start | bytes 393224 | tf_op jit(solution)/shard_map/while/body/eval_jaxpr/ppermute | solution.py:16
  243.4 14.8 %collective-permute-start.2 = (f32[512,1,128]{2,0,1:T(8,128)S(1)}, f32[512,1,128]{2,0,1:T(8,128)S(1)}, u32[]{:S(2)}, u32[]{:S(2)}) collective-permute-start(f32[512,1,128]{2,0,1:T(8,128)S(1)} %get-tuple-element.1639), channel_id=1, source_target_pairs={{0,4},{4,8},{8,12},{12,16},{16,20},{20,24},{24,28},{28,32},{32,36}... | collective-permute-start | bytes 786440 | tf_op jit(solution)/shard_map/while/body/eval_jaxpr/ppermute | solution.py:16
  292.5 11.8 %collective-permute-start.2 = (f32[512,1,128]{2,0,1:T(8,128)S(1)}, f32[512,1,128]{2,0,1:T(8,128)S(1)}, u32[]{:S(2)}, u32[]{:S(2)}) collective-permute-start(f32[512,1,128]{2,0,1:T(8,128)S(1)} %get-tuple-element.1639), channel_id=1, source_target_pairs={{0,4},{4,8},{8,12},{12,16},{16,20},{20,24},{24,28},{28,32},{32,36}... | collective-permute-start | bytes 786440 | tf_op jit(solution)/shard_map/while/body/eval_jaxpr/ppermute | solution.py:16
  297.2 10.0 collective-permute-start.3
  299.1 10.8 collective-permute-start
  301.0 11.7 %collective-permute-start.1 = (bf16[512,1,128]{2,0,1:T(8,128)(2,1)S(1)}, bf16[512,1,128]{2,0,1:T(8,128)(2,1)S(1)}, u32[]{:S(2)}, u32[]{:S(2)}) collective-permute-start(bf16[512,1,128]{2,0,1:T(8,128)(2,1)S(1)} %get-tuple-element.1815), channel_id=1, source_target_pairs={{0,4},{4,8},{8,12},{12,16},{16,20},{20,24},{24,28},{28,32},{32,36}... | collective-permute-start | bytes 393224 | tf_op jit(solution)/shard_map/while/body/eval_jaxpr/ppermute | solution.py:16
  343.6 13.0 %collective-permute-start.2 = (f32[512,1,128]{2,0,1:T(8,128)S(1)}, f32[512,1,128]{2,0,1:T(8,128)S(1)}, u32[]{:S(2)}, u32[]{:S(2)}) collective-permute-start(f32[512,1,128]{2,0,1:T(8,128)S(1)} %get-tuple-element.1639), channel_id=1, source_target_pairs={{0,4},{4,8},{8,12},{12,16},{16,20},{20,24},{24,28},{28,32},{32,36}... | collective-permute-start | bytes 786440 | tf_op jit(solution)/shard_map/while/body/eval_jaxpr/ppermute | solution.py:16
  345.6 11.1 %collective-permute-start.3 = (f32[512,1,128]{2,0,1:T(8,128)S(1)}, f32[512,1,128]{2,0,1:T(8,128)S(1)}, u32[]{:S(2)}, u32[]{:S(2)}) collective-permute-start(f32[512,1,128]{2,0,1:T(8,128)S(1)} %get-tuple-element.1640), channel_id=1, source_target_pairs={{0,4},{4,8},{8,12},{12,16},{16,20},{20,24},{24,28},{28,32},{32,36}... | collective-permute-start | bytes 786440 | tf_op jit(solution)/shard_map/while/body/eval_jaxpr/ppermute | solution.py:16
  347.5 10.6 collective-permute-start
  354.7 9.6 collective-permute-start.1
  390.1 19.6 %collective-permute-start.2 = (f32[512,1,128]{2,0,1:T(8,128)S(1)}, f32[512,1,128]{2,0,1:T(8,128)S(1)}, u32[]{:S(2)}, u32[]{:S(2)}) collective-permute-start(f32[512,1,128]{2,0,1:T(8,128)S(1)} %get-tuple-element.1639), channel_id=1, source_target_pairs={{0,4},{4,8},{8,12},{12,16},{16,20},{20,24},{24,28},{28,32},{32,36}... | collective-permute-start | bytes 786440 | tf_op jit(solution)/shard_map/while/body/eval_jaxpr/ppermute | solution.py:16
  398.0 11.7 %collective-permute-start.3 = (f32[512,1,128]{2,0,1:T(8,128)S(1)}, f32[512,1,128]{2,0,1:T(8,128)S(1)}, u32[]{:S(2)}, u32[]{:S(2)}) collective-permute-start(f32[512,1,128]{2,0,1:T(8,128)S(1)} %get-tuple-element.1640), channel_id=1, source_target_pairs={{0,4},{4,8},{8,12},{12,16},{16,20},{20,24},{24,28},{28,32},{32,36}... | collective-permute-start | bytes 786440 | tf_op jit(solution)/shard_map/while/body/eval_jaxpr/ppermute | solution.py:16
  400.0 10.3 collective-permute-start
  406.1 9.6 collective-permute-start.1
  444.0 14.1 %collective-permute-start.2 = (f32[512,1,128]{2,0,1:T(8,128)S(1)}, f32[512,1,128]{2,0,1:T(8,128)S(1)}, u32[]{:S(2)}, u32[]{:S(2)}) collective-permute-start(f32[512,1,128]{2,0,1:T(8,128)S(1)} %get-tuple-element.1639), channel_id=1, source_target_pairs={{0,4},{4,8},{8,12},{12,16},{16,20},{20,24},{24,28},{28,32},{32,36}... | collective-permute-start | bytes 786440 | tf_op jit(solution)/shard_map/while/body/eval_jaxpr/ppermute | solution.py:16
  456.2 9.5 collective-permute-start.1
  494.1 14.2 %collective-permute-start.2 = (f32[512,1,128]{2,0,1:T(8,128)S(1)}, f32[512,1,128]{2,0,1:T(8,128)S(1)}, u32[]{:S(2)}, u32[]{:S(2)}) collective-permute-start(f32[512,1,128]{2,0,1:T(8,128)S(1)} %get-tuple-element.1639), channel_id=1, source_target_pairs={{0,4},{4,8},{8,12},{12,16},{16,20},{20,24},{24,28},{28,32},{32,36}... | collective-permute-start | bytes 786440 | tf_op jit(solution)/shard_map/while/body/eval_jaxpr/ppermute | solution.py:16
  543.9 12.6 %collective-permute-start.2 = (f32[512,1,128]{2,0,1:T(8,128)S(1)}, f32[512,1,128]{2,0,1:T(8,128)S(1)}, u32[]{:S(2)}, u32[]{:S(2)}) collective-permute-start(f32[512,1,128]{2,0,1:T(8,128)S(1)} %get-tuple-element.1639), channel_id=1, source_target_pairs={{0,4},{4,8},{8,12},{12,16},{16,20},{20,24},{24,28},{28,32},{32,36}... | collective-permute-start | bytes 786440 | tf_op jit(solution)/shard_map/while/body/eval_jaxpr/ppermute | solution.py:16
  547.7 10.3 collective-permute-start.3
  549.9 10.9 %collective-permute-start = (bf16[512,1,128]{2,0,1:T(8,128)(2,1)S(1)}, bf16[512,1,128]{2,0,1:T(8,128)(2,1)S(1)}, u32[]{:S(2)}, u32[]{:S(2)}) collective-permute-start(bf16[512,1,128]{2,0,1:T(8,128)(2,1)S(1)} %get-tuple-element.1805), channel_id=1, source_target_pairs={{0,4},{4,8},{8,12},{12,16},{16,20},{20,24},{24,28},{28,32},{32,36}... | collective-permute-start | bytes 393224 | tf_op jit(solution)/shard_map/while/body/eval_jaxpr/ppermute | solution.py:16
  554.5 9.6 collective-permute-start.1
  589.9 15.2 %collective-permute-start.2 = (f32[512,1,128]{2,0,1:T(8,128)S(1)}, f32[512,1,128]{2,0,1:T(8,128)S(1)}, u32[]{:S(2)}, u32[]{:S(2)}) collective-permute-start(f32[512,1,128]{2,0,1:T(8,128)S(1)} %get-tuple-element.1639), channel_id=1, source_target_pairs={{0,4},{4,8},{8,12},{12,16},{16,20},{20,24},{24,28},{28,32},{32,36}... | collective-permute-start | bytes 786440 | tf_op jit(solution)/shard_map/while/body/eval_jaxpr/ppermute | solution.py:16
  599.3 9.3 collective-permute-start.3
  603.2 9.7 collective-permute-start.1
  643.7 12.1 %collective-permute-start.2 = (f32[512,1,128]{2,0,1:T(8,128)S(1)}, f32[512,1,128]{2,0,1:T(8,128)S(1)}, u32[]{:S(2)}, u32[]{:S(2)}) collective-permute-start(f32[512,1,128]{2,0,1:T(8,128)S(1)} %get-tuple-element.1639), channel_id=1, source_target_pairs={{0,4},{4,8},{8,12},{12,16},{16,20},{20,24},{24,28},{28,32},{32,36}... | collective-permute-start | bytes 786440 | tf_op jit(solution)/shard_map/while/body/eval_jaxpr/ppermute | solution.py:16
  650.0 11.1 %collective-permute-start.3 = (f32[512,1,128]{2,0,1:T(8,128)S(1)}, f32[512,1,128]{2,0,1:T(8,128)S(1)}, u32[]{:S(2)}, u32[]{:S(2)}) collective-permute-start(f32[512,1,128]{2,0,1:T(8,128)S(1)} %get-tuple-element.1640), channel_id=1, source_target_pairs={{0,4},{4,8},{8,12},{12,16},{16,20},{20,24},{24,28},{28,32},{32,36}... | collective-permute-start | bytes 786440 | tf_op jit(solution)/shard_map/while/body/eval_jaxpr/ppermute | solution.py:16
  652.0 11.5 %collective-permute-start = (bf16[512,1,128]{2,0,1:T(8,128)(2,1)S(1)}, bf16[512,1,128]{2,0,1:T(8,128)(2,1)S(1)}, u32[]{:S(2)}, u32[]{:S(2)}) collective-permute-start(bf16[512,1,128]{2,0,1:T(8,128)(2,1)S(1)} %get-tuple-element.1805), channel_id=1, source_target_pairs={{0,4},{4,8},{8,12},{12,16},{16,20},{20,24},{24,28},{28,32},{32,36}... | collective-permute-start | bytes 393224 | tf_op jit(solution)/shard_map/while/body/eval_jaxpr/ppermute | solution.py:16
  653.9 12.4 %collective-permute-start.1 = (bf16[512,1,128]{2,0,1:T(8,128)(2,1)S(1)}, bf16[512,1,128]{2,0,1:T(8,128)(2,1)S(1)}, u32[]{:S(2)}, u32[]{:S(2)}) collective-permute-start(bf16[512,1,128]{2,0,1:T(8,128)(2,1)S(1)} %get-tuple-element.1815), channel_id=1, source_target_pairs={{0,4},{4,8},{8,12},{12,16},{16,20},{20,24},{24,28},{28,32},{32,36}... | collective-permute-start | bytes 393224 | tf_op jit(solution)/shard_map/while/body/eval_jaxpr/ppermute | solution.py:16
  696.6 11.5 %collective-permute-start.3 = (f32[512,1,128]{2,0,1:T(8,128)S(1)}, f32[512,1,128]{2,0,1:T(8,128)S(1)}, u32[]{:S(2)}, u32[]{:S(2)}) collective-permute-start(f32[512,1,128]{2,0,1:T(8,128)S(1)} %get-tuple-element.1640), channel_id=1, source_target_pairs={{0,4},{4,8},{8,12},{12,16},{16,20},{20,24},{24,28},{28,32},{32,36}... | collective-permute-start | bytes 786440 | tf_op jit(solution)/shard_map/while/body/eval_jaxpr/ppermute | solution.py:16
  698.5 12.4 %collective-permute-start = (bf16[512,1,128]{2,0,1:T(8,128)(2,1)S(1)}, bf16[512,1,128]{2,0,1:T(8,128)(2,1)S(1)}, u32[]{:S(2)}, u32[]{:S(2)}) collective-permute-start(bf16[512,1,128]{2,0,1:T(8,128)(2,1)S(1)} %get-tuple-element.1805), channel_id=1, source_target_pairs={{0,4},{4,8},{8,12},{12,16},{16,20},{20,24},{24,28},{28,32},{32,36}... | collective-permute-start | bytes 393224 | tf_op jit(solution)/shard_map/while/body/eval_jaxpr/ppermute | solution.py:16
  700.4 13.3 %collective-permute-start.1 = (bf16[512,1,128]{2,0,1:T(8,128)(2,1)S(1)}, bf16[512,1,128]{2,0,1:T(8,128)(2,1)S(1)}, u32[]{:S(2)}, u32[]{:S(2)}) collective-permute-start(bf16[512,1,128]{2,0,1:T(8,128)(2,1)S(1)} %get-tuple-element.1815), channel_id=1, source_target_pairs={{0,4},{4,8},{8,12},{12,16},{16,20},{20,24},{24,28},{28,32},{32,36}... | collective-permute-start | bytes 393224 | tf_op jit(solution)/shard_map/while/body/eval_jaxpr/ppermute | solution.py:16
  736.9 16.2 %collective-permute-start.2 = (f32[512,1,128]{2,0,1:T(8,128)S(1)}, f32[512,1,128]{2,0,1:T(8,128)S(1)}, u32[]{:S(2)}, u32[]{:S(2)}) collective-permute-start(f32[512,1,128]{2,0,1:T(8,128)S(1)} %get-tuple-element.1639), channel_id=1, source_target_pairs={{0,4},{4,8},{8,12},{12,16},{16,20},{20,24},{24,28},{28,32},{32,36}... | collective-permute-start | bytes 786440 | tf_op jit(solution)/shard_map/while/body/eval_jaxpr/ppermute | solution.py:16
  747.3 11.4 %collective-permute-start.3 = (f32[512,1,128]{2,0,1:T(8,128)S(1)}, f32[512,1,128]{2,0,1:T(8,128)S(1)}, u32[]{:S(2)}, u32[]{:S(2)}) collective-permute-start(f32[512,1,128]{2,0,1:T(8,128)S(1)} %get-tuple-element.1640), channel_id=1, source_target_pairs={{0,4},{4,8},{8,12},{12,16},{16,20},{20,24},{24,28},{28,32},{32,36}... | collective-permute-start | bytes 786440 | tf_op jit(solution)/shard_map/while/body/eval_jaxpr/ppermute | solution.py:16
  749.2 12.2 %collective-permute-start = (bf16[512,1,128]{2,0,1:T(8,128)(2,1)S(1)}, bf16[512,1,128]{2,0,1:T(8,128)(2,1)S(1)}, u32[]{:S(2)}, u32[]{:S(2)}) collective-permute-start(bf16[512,1,128]{2,0,1:T(8,128)(2,1)S(1)} %get-tuple-element.1805), channel_id=1, source_target_pairs={{0,4},{4,8},{8,12},{12,16},{16,20},{20,24},{24,28},{28,32},{32,36}... | collective-permute-start | bytes 393224 | tf_op jit(solution)/shard_map/while/body/eval_jaxpr/ppermute | solution.py:16
  751.2 13.1 %collective-permute-start.1 = (bf16[512,1,128]{2,0,1:T(8,128)(2,1)S(1)}, bf16[512,1,128]{2,0,1:T(8,128)(2,1)S(1)}, u32[]{:S(2)}, u32[]{:S(2)}) collective-permute-start(bf16[512,1,128]{2,0,1:T(8,128)(2,1)S(1)} %get-tuple-element.1815), channel_id=1, source_target_pairs={{0,4},{4,8},{8,12},{12,16},{16,20},{20,24},{24,28},{28,32},{32,36}... | collective-permute-start | bytes 393224 | tf_op jit(solution)/shard_map/while/body/eval_jaxpr/ppermute | solution.py:16
  794.6 11.9 %collective-permute-start.3 = (f32[512,1,128]{2,0,1:T(8,128)S(1)}, f32[512,1,128]{2,0,1:T(8,128)S(1)}, u32[]{:S(2)}, u32[]{:S(2)}) collective-permute-start(f32[512,1,128]{2,0,1:T(8,128)S(1)} %get-tuple-element.1640), channel_id=1, source_target_pairs={{0,4},{4,8},{8,12},{12,16},{16,20},{20,24},{24,28},{28,32},{32,36}... | collective-permute-start | bytes 786440 | tf_op jit(solution)/shard_map/while/body/eval_jaxpr/ppermute | solution.py:16
  796.8 12.5 %collective-permute-start = (bf16[512,1,128]{2,0,1:T(8,128)(2,1)S(1)}, bf16[512,1,128]{2,0,1:T(8,128)(2,1)S(1)}, u32[]{:S(2)}, u32[]{:S(2)}) collective-permute-start(bf16[512,1,128]{2,0,1:T(8,128)(2,1)S(1)} %get-tuple-element.1805), channel_id=1, source_target_pairs={{0,4},{4,8},{8,12},{12,16},{16,20},{20,24},{24,28},{28,32},{32,36}... | collective-permute-start | bytes 393224 | tf_op jit(solution)/shard_map/while/body/eval_jaxpr/ppermute | solution.py:16
  798.7 13.4 %collective-permute-start.1 = (bf16[512,1,128]{2,0,1:T(8,128)(2,1)S(1)}, bf16[512,1,128]{2,0,1:T(8,128)(2,1)S(1)}, u32[]{:S(2)}, u32[]{:S(2)}) collective-permute-start(bf16[512,1,128]{2,0,1:T(8,128)(2,1)S(1)} %get-tuple-element.1815), channel_id=1, source_target_pairs={{0,4},{4,8},{8,12},{12,16},{16,20},{20,24},{24,28},{28,32},{32,36}... | collective-permute-start | bytes 393224 | tf_op jit(solution)/shard_map/while/body/eval_jaxpr/ppermute | solution.py:16
  840.4 10.1 collective-permute-start.2
  843.5 11.6 %collective-permute-start.3 = (f32[512,1,128]{2,0,1:T(8,128)S(1)}, f32[512,1,128]{2,0,1:T(8,128)S(1)}, u32[]{:S(2)}, u32[]{:S(2)}) collective-permute-start(f32[512,1,128]{2,0,1:T(8,128)S(1)} %get-tuple-element.1640), channel_id=1, source_target_pairs={{0,4},{4,8},{8,12},{12,16},{16,20},{20,24},{24,28},{28,32},{32,36}... | collective-permute-start | bytes 786440 | tf_op jit(solution)/shard_map/while/body/eval_jaxpr/ppermute | solution.py:16
  845.4 12.4 %collective-permute-start = (bf16[512,1,128]{2,0,1:T(8,128)(2,1)S(1)}, bf16[512,1,128]{2,0,1:T(8,128)(2,1)S(1)}, u32[]{:S(2)}, u32[]{:S(2)}) collective-permute-start(bf16[512,1,128]{2,0,1:T(8,128)(2,1)S(1)} %get-tuple-element.1805), channel_id=1, source_target_pairs={{0,4},{4,8},{8,12},{12,16},{16,20},{20,24},{24,28},{28,32},{32,36}... | collective-permute-start | bytes 393224 | tf_op jit(solution)/shard_map/while/body/eval_jaxpr/ppermute | solution.py:16
  847.3 13.3 %collective-permute-start.1 = (bf16[512,1,128]{2,0,1:T(8,128)(2,1)S(1)}, bf16[512,1,128]{2,0,1:T(8,128)(2,1)S(1)}, u32[]{:S(2)}, u32[]{:S(2)}) collective-permute-start(bf16[512,1,128]{2,0,1:T(8,128)(2,1)S(1)} %get-tuple-element.1815), channel_id=1, source_target_pairs={{0,4},{4,8},{8,12},{12,16},{16,20},{20,24},{24,28},{28,32},{32,36}... | collective-permute-start | bytes 393224 | tf_op jit(solution)/shard_map/while/body/eval_jaxpr/ppermute | solution.py:16
  893.5 10.9 %collective-permute-start.3 = (f32[512,1,128]{2,0,1:T(8,128)S(1)}, f32[512,1,128]{2,0,1:T(8,128)S(1)}, u32[]{:S(2)}, u32[]{:S(2)}) collective-permute-start(f32[512,1,128]{2,0,1:T(8,128)S(1)} %get-tuple-element.1640), channel_id=1, source_target_pairs={{0,4},{4,8},{8,12},{12,16},{16,20},{20,24},{24,28},{28,32},{32,36}... | collective-permute-start | bytes 786440 | tf_op jit(solution)/shard_map/while/body/eval_jaxpr/ppermute | solution.py:16
  895.4 11.8 %collective-permute-start = (bf16[512,1,128]{2,0,1:T(8,128)(2,1)S(1)}, bf16[512,1,128]{2,0,1:T(8,128)(2,1)S(1)}, u32[]{:S(2)}, u32[]{:S(2)}) collective-permute-start(bf16[512,1,128]{2,0,1:T(8,128)(2,1)S(1)} %get-tuple-element.1805), channel_id=1, source_target_pairs={{0,4},{4,8},{8,12},{12,16},{16,20},{20,24},{24,28},{28,32},{32,36}... | collective-permute-start | bytes 393224 | tf_op jit(solution)/shard_map/while/body/eval_jaxpr/ppermute | solution.py:16
  897.3 12.7 %collective-permute-start.1 = (bf16[512,1,128]{2,0,1:T(8,128)(2,1)S(1)}, bf16[512,1,128]{2,0,1:T(8,128)(2,1)S(1)}, u32[]{:S(2)}, u32[]{:S(2)}) collective-permute-start(bf16[512,1,128]{2,0,1:T(8,128)(2,1)S(1)} %get-tuple-element.1815), channel_id=1, source_target_pairs={{0,4},{4,8},{8,12},{12,16},{16,20},{20,24},{24,28},{28,32},{32,36}... | collective-permute-start | bytes 393224 | tf_op jit(solution)/shard_map/while/body/eval_jaxpr/ppermute | solution.py:16
  940.9 12.5 %collective-permute-start.2 = (f32[512,1,128]{2,0,1:T(8,128)S(1)}, f32[512,1,128]{2,0,1:T(8,128)S(1)}, u32[]{:S(2)}, u32[]{:S(2)}) collective-permute-start(f32[512,1,128]{2,0,1:T(8,128)S(1)} %get-tuple-element.1639), channel_id=1, source_target_pairs={{0,4},{4,8},{8,12},{12,16},{16,20},{20,24},{24,28},{28,32},{32,36}... | collective-permute-start | bytes 786440 | tf_op jit(solution)/shard_map/while/body/eval_jaxpr/ppermute | solution.py:16
  942.9 15.3 %collective-permute-start.3 = (f32[512,1,128]{2,0,1:T(8,128)S(1)}, f32[512,1,128]{2,0,1:T(8,128)S(1)}, u32[]{:S(2)}, u32[]{:S(2)}) collective-permute-start(f32[512,1,128]{2,0,1:T(8,128)S(1)} %get-tuple-element.1640), channel_id=1, source_target_pairs={{0,4},{4,8},{8,12},{12,16},{16,20},{20,24},{24,28},{28,32},{32,36}... | collective-permute-start | bytes 786440 | tf_op jit(solution)/shard_map/while/body/eval_jaxpr/ppermute | solution.py:16
  944.8 16.2 %collective-permute-start = (bf16[512,1,128]{2,0,1:T(8,128)(2,1)S(1)}, bf16[512,1,128]{2,0,1:T(8,128)(2,1)S(1)}, u32[]{:S(2)}, u32[]{:S(2)}) collective-permute-start(bf16[512,1,128]{2,0,1:T(8,128)(2,1)S(1)} %get-tuple-element.1805), channel_id=1, source_target_pairs={{0,4},{4,8},{8,12},{12,16},{16,20},{20,24},{24,28},{28,32},{32,36}... | collective-permute-start | bytes 393224 | tf_op jit(solution)/shard_map/while/body/eval_jaxpr/ppermute | solution.py:16
  946.7 17.1 %collective-permute-start.1 = (bf16[512,1,128]{2,0,1:T(8,128)(2,1)S(1)}, bf16[512,1,128]{2,0,1:T(8,128)(2,1)S(1)}, u32[]{:S(2)}, u32[]{:S(2)}) collective-permute-start(bf16[512,1,128]{2,0,1:T(8,128)(2,1)S(1)} %get-tuple-element.1815), channel_id=1, source_target_pairs={{0,4},{4,8},{8,12},{12,16},{16,20},{20,24},{24,28},{28,32},{32,36}... | collective-permute-start | bytes 393224 | tf_op jit(solution)/shard_map/while/body/eval_jaxpr/ppermute | solution.py:16
  964.5 60.7 %reduce-scatter.5.cloned.1.call-start = ((), (), s32[]{:S(2)}) async-start(), calls=%async_computation.13 | async-start | bytes 327680 | tf_op jit(solution)/shard_map/reduce_scatter | solution.py:190
  995.3 32.3 %all-to-all-start.8 = ((bf16[8,2,1024]{2,1,0:T(2,128)(2,1)}), bf16[8,2,1024]{2,1,0:T(2,128)(2,1)S(1)}, u32[]{:S(2)}, u32[]{:S(2)}) async-start(bf16[8,2,1024]{2,1,0:T(2,128)(2,1)} %reshape.129), calls=%async_computation.9 | async-start | bytes 65536 | tf_op jit(solution)/shard_map/all_to_all | solution.py:195
  1027.6 25.5 %all-to-all-start.9 = ((bf16[8,2,1024]{2,1,0:T(2,128)(2,1)}), bf16[8,2,1024]{2,1,0:T(2,128)(2,1)S(1)}, u32[]{:S(2)}, u32[]{:S(2)}) async-start(bf16[8,2,1024]{2,1,0:T(2,128)(2,1)} %reshape.131), calls=%async_computation.11 | async-start | bytes 65536 | tf_op jit(solution)/shard_map/all_to_all | solution.py:198
  1053.1 25.2 %all-to-all-start.7 = ((bf16[128,8,128]{2,1,0:T(8,128)(2,1)}), bf16[128,8,128]{2,1,0:T(8,128)(2,1)S(1)}, u32[]{:S(2)}, u32[]{:S(2)}) async-start(bf16[128,8,128]{2,1,0:T(8,128)(2,1)} %bitcast.167), calls=%async_computation.7 | async-start | bytes 524288 | tf_op jit(solution)/shard_map/all_to_all | solution.py:194
  (20 other events, 258.6 us)
Sparse Core Ops, SparseCore 0:
  964.6 27.7 reduce-scatter.2
  996.0 29.1 reduce-scatter.4
where the time goes:
time: 1100 us; the launch traced here: 1090 us
  waiting for transfers between devices  309 us (28%)
  loops' own time  287 us (26%)
  starting transfers between devices  268 us (24%)
  local copies, waits for them, and re-layouts  139 us (13%)
  matrix products  36.6 us (3%)
  blocking collectives  23.7 us (2%)
  between operations  16.1 us (1%)
    another operation x16, loops' own time, one_step(): lax.fori_loop(0, per_step, visit, (query_gradient, grad_key, grad_value))  244 us
    ppermute x64, starting transfers between devices, from_behind(): return lax.ppermute(value, axis, pairs)  193 us
    ppermute x64, waiting for transfers between devices, from_behind(): return lax.ppermute(value, axis, pairs)  151 us
    dynamic_slice x64, local copies, waits for them, and re-layouts, visit_tile(): block_mask[query_block_id, key_block_id] == 1  83.7 us
    dynamic_slice x64, local copies, waits for them, and re-layouts, visit_tile(): key_block_id = block_ids[context * blocks_dev + key_blk]  41.9 us
    another operation x64, loops' own time, visit_tile(): return lax.cond(active, compute, unchanged, totals)  41.4 us
    reduce_scatter x1, waiting for transfers between devices, local(): lax.psum_scatter(grad_key, 'outer', scatter_dimension=0, tiled=True)  27.1 us
  transfers between devices with their start and end apart: 76, of which 62 were waited for; matrix products, arithmetic and copies ran while one was open for 1% of the time, Pallas kernels for 0%

commit v1 on v0

v1 whole, which is shorter than its diff:
```python
import functools

import jax
import jax.numpy as jnp
from jax import lax
from jax.experimental import pallas as pl
from jax.experimental.pallas import tpu as pltpu
from jax.sharding import Mesh, PartitionSpec as P

QUERY_HEADS = 64
KEY_HEADS = 8
HEAD_WIDTH = 128
BLK = 128
GROUP = 8
ROWS = 16
BATCH = 4
PIECE = 64
SCALE = HEAD_WIDTH ** (-0.5)
FAR = 1e30
STEPS = (0, 1, -1, 2)
TOKEN_AXES = ("x", "yh", "yl", "zlo", "zhi", "core")
PLANE = ("x", "yh", "yl")
KEY_AXES = ("x", "yl", "zhi")
VMEM = pltpu.VMEM
F32 = jnp.float32
BF16 = jnp.bfloat16


def vmem_call(kernel, out_shape, ins, **kw):
    return pl.pallas_call(
        kernel,
        out_shape=out_shape,
        in_specs=ins,
        out_specs=jax.tree.map(lambda _: pl.BlockSpec(memory_space=VMEM), out_shape),
        compiler_params=pltpu.CompilerParams(vmem_limit_bytes=48 << 20),
        **kw,
    )


WHOLE = pl.BlockSpec(memory_space=VMEM)
SCALARS = pl.BlockSpec(memory_space=pltpu.SMEM)


def pack_keys_kernel(k_ref, v_ref, out_ref):
    for head in range(KEY_HEADS):
        cols = slice(head * HEAD_WIDTH, (head + 1) * HEAD_WIDTH)
        key, value = k_ref[:, cols], v_ref[:, cols]
        for copy in range(4):
            out_ref[head * 4 + copy, 0] = key
            out_ref[head * 4 + copy, 1] = value


def pack_queries_kernel(q_ref, do_ref, sup_ref, thr_ref, sums_ref, out_ref):
    for head in range(KEY_HEADS):
        dests = [(head // 2) * 4 + yh * 2 + head % 2 for yh in range(2)]
        products = []
        for g in range(GROUP):
            n = head * GROUP + g
            cols = slice(n * HEAD_WIDTH, (n + 1) * HEAD_WIDTH)
            query, grad = q_ref[:, cols], do_ref[:, cols]
            for dest in dests:
                out_ref[dest, g] = query
                out_ref[dest, GROUP + g] = grad
            products.append(grad.astype(F32) * sup_ref[:, cols].astype(F32))
        row_dot = jnp.sum(jnp.concatenate(products, axis=0).T, axis=0, keepdims=True)
        mean = row_dot / sums_ref[head : head + 1, :]
        high = mean.astype(BF16).astype(F32)
        low = mean - high
        stats = jnp.concatenate(
            [thr_ref[head : head + 1, :], high, low, jnp.zeros((13, 128), F32)], axis=0
        ).astype(BF16)
        for dest in dests:
            out_ref[dest, 2 * GROUP] = stats


def attention_kernel(
    list_ref,
    count_ref,
    place_ref,
    qa_ref,
    qb_ref,
    kv0_ref,
    kv1_ref,
    kv2_ref,
    kv3_ref,
    dq_ref,
    g0_ref,
    g1_ref,
    g2_ref,
    g3_ref,
    k_s,
    v_s,
    bias_s,
    dk_s,
    dv_s,
    dqt_s,
):
    core, zhi = place_ref[0], place_ref[1]
    for c, ref in enumerate((kv0_ref, kv1_ref, kv2_ref, kv3_ref)):
        for b in range(8):
            k_s[c * 8 + b] = ref[b * 4 : b * 4 + 4, 0].reshape(PIECE, HEAD_WIDTH)
            v_s[c * 8 + b] = ref[b * 4 : b * 4 + 4, 1].reshape(PIECE, HEAD_WIDTH)
    dk_s[...] = jnp.zeros_like(dk_s)
    dv_s[...] = jnp.zeros_like(dv_s)
    row = lax.broadcasted_iota(jnp.int32, (PIECE, 256), 0)
    lane = lax.broadcasted_iota(jnp.int32, (PIECE, 256), 1)
    key_offset = (row >> 4) * 32 + core * 16 + (row & 15)
    query_core = jnp.where(lane < 128, core, 1 - core)
    query_offset = zhi * 32 + query_core * 16 + (lane & 15)
    bias_s[0] = jnp.zeros((PIECE, 256), F32)
    bias_s[1] = jnp.where(key_offset <= query_offset, 0.0, FAR)
    bias_s[2] = jnp.full((PIECE, 256), FAR, F32)

    def one_block(j, _):
        def rows(first):
            return jnp.concatenate(
                [ref[j, first : first + GROUP].reshape(128, HEAD_WIDTH) for ref in (qa_ref, qb_ref)],
                axis=0,
            )

        query, grad = rows(0), rows(GROUP)
        stats = jnp.concatenate(
            [ref[j, 2 * GROUP].astype(F32) for ref in (qa_ref, qb_ref)], axis=1
        )
        thresh = stats[0:1]
        mean = stats[1:2] + stats[2:3]
        query_t, grad_t = query.T, grad.T
        dqt_s[...] = jnp.zeros_like(dqt_s)

        def one_batch(step, _):
            entries = [list_ref[j * 32 + step * BATCH + u] for u in range(BATCH)]
            ids = [entry & 31 for entry in entries]
            keys = jnp.concatenate([k_s[i] for i in ids], axis=0)
            values = jnp.concatenate([v_s[i] for i in ids], axis=0)
            bias = jnp.concatenate([bias_s[entry >> 5] for entry in entries], axis=0)
            scores = jnp.dot(keys, query_t, preferred_element_type=F32)
            dprob = jnp.dot(values, grad_t, preferred_element_type=F32)
            gate = jnp.maximum(scores * (0.5 * SCALE) - thresh - bias, 0.0)
            probs = (gate * gate).astype(BF16)
            dscore = (SCALE * gate * (dprob - mean)).astype(BF16)
            dv = jnp.dot(probs, grad, preferred_element_type=F32)
            dk = jnp.dot(dscore, query, preferred_element_type=F32)
            dqt_s[...] += lax.dot_general(
                keys, dscore, (((0,), (0,)), ((), ())), preferred_element_type=F32
            )
            for u, i in enumerate(ids):
                dk_s[i] += dk[u * PIECE : (u + 1) * PIECE]
                dv_s[i] += dv[u * PIECE : (u + 1) * PIECE]
            return 0

        lax.fori_loop(0, (count_ref[j] + BATCH - 1) // BATCH, one_batch, 0)
        dq = dqt_s[...].T.astype(BF16)
        dq_ref[j, core] = dq[:128]
        dq_ref[j, 1 - core] = dq[128:]
        return 0

    lax.fori_loop(0, 16, one_block, 0)
    for c, ref in enumerate((g0_ref, g1_ref, g2_ref, g3_ref)):
        for b in range(8):
            ref[b * 4 : b * 4 + 4, 0] = dk_s[c * 8 + b].astype(BF16).reshape(4, ROWS, HEAD_WIDTH)
            ref[b * 4 : b * 4 + 4, 1] = dv_s[c * 8 + b].astype(BF16).reshape(4, ROWS, HEAD_WIDTH)


def sum_queries_kernel(in_ref, out_ref):
    for head in range(KEY_HEADS):
        parts = [
            in_ref[(((head // 2) * 2 + yh) * 2 + head % 2) * 2 + core].astype(F32)
            for yh in range(2)
            for core in range(2)
        ]
        total = ((parts[0] + parts[1]) + (parts[2] + parts[3])).astype(BF16)
        for g in range(GROUP):
            n = head * GROUP + g
            out_ref[:, n * HEAD_WIDTH : (n + 1) * HEAD_WIDTH] = total[g * ROWS : (g + 1) * ROWS]


def sum_keys_kernel(in_ref, dk_ref, dv_ref):
    for head in range(KEY_HEADS):
        cols = slice(head * HEAD_WIDTH, (head + 1) * HEAD_WIDTH)
        for kind, ref in enumerate((dk_ref, dv_ref)):
            parts = [in_ref[head * 4 + zhi, kind].astype(F32) for zhi in range(4)]
            ref[:, cols] = ((parts[0] + parts[1]) + (parts[2] + parts[3])).astype(BF16)


def exchange(value, axes):
    return lax.all_to_all(value, axes, split_axis=0, concat_axis=0, tiled=True)


def along_z(value, steps):
    pairs = [(z, (z + steps) % 16) for z in range(16)]
    return lax.ppermute(value, ("zhi", "zlo"), pairs)


def active_lists(token_pos, block_mask):
    yh, zlo = lax.axis_index("yh"), lax.axis_index("zlo")
    block_ids = token_pos.reshape(64, BLK)[:, 0] // BLK
    by_place = block_ids.reshape(16, 4)
    query_pos = lax.dynamic_index_in_dim(by_place, zlo, 1, keepdims=False)
    mine = lax.dynamic_index_in_dim(block_ids.reshape(4, 2, 2, 4), yh, 1, keepdims=False)
    key_pos = jnp.concatenate(
        [
            lax.dynamic_index_in_dim(mine, (zlo + step) % 4, 2, keepdims=False).reshape(8)
            for step in STEPS
        ]
    )
    span = jnp.arange(64, dtype=jnp.int32)
    pick_query = (query_pos[:, None] == span[None, :]).astype(BF16)
    pick_key = (key_pos[:, None] == span[None, :]).astype(BF16)
    seen = jnp.dot(
        jnp.dot(pick_query, (block_mask == 1).astype(BF16), preferred_element_type=F32).astype(BF16),
        pick_key.T,
        preferred_element_type=F32,
    )
    active = (seen > 0.5) & (key_pos[None, :] <= query_pos[:, None])
    same = key_pos[None, :] == query_pos[:, None]
    number = jnp.arange(32, dtype=jnp.int32)
    ones = active.astype(jnp.int32)
    before = jnp.sum(
        jnp.where(number[None, None, :] < number[None, :, None], ones[:, None, :], 0), axis=2
    )
    count = jnp.sum(ones, axis=1)
    code = number[None, :] + 32 * same.astype(jnp.int32)
    lists = jnp.sum(
        jnp.where(active[:, None, :] & (before[:, None, :] == number[None, :, None]), code[:, None, :], 0),
        axis=2,
    )
    lists = jnp.where(number[None, :] < count[:, None], lists, 64)
    return lists.reshape(512), count


def local(
    queries,
    key_head_rows,
    value_head_rows,
    output_gradient,
    support_values,
    thresholds,
    gate_row_sums,
    token_pos,
    block_mask,
):
    shape = jax.ShapeDtypeStruct
    send_keys = vmem_call(
        pack_keys_kernel, shape((32, 2, ROWS, HEAD_WIDTH), BF16), [WHOLE] * 2
    )(key_head_rows, value_head_rows)
    keys_own = exchange(send_keys, KEY_AXES)
    keys_near = [along_z(keys_own, -step) for step in STEPS[1:]]

    def by_head(stat):
        return stat.astype(F32).T.reshape(KEY_HEADS, GROUP * ROWS)

    send_queries = vmem_call(
        pack_queries_kernel, shape((16, 2 * GROUP + 1, ROWS, HEAD_WIDTH), BF16), [WHOLE] * 5
    )(queries, output_gradient, support_values, by_head(thresholds), by_head(gate_row_sums))
    send_queries, keys_own = lax.optimization_barrier((send_queries, keys_own))
    queries_own = exchange(send_queries, PLANE)
    queries_other = lax.ppermute(queries_own, "core", [(0, 1), (1, 0)])

    lists, count = active_lists(token_pos, block_mask)
    place = jnp.stack([lax.axis_index("core"), lax.axis_index("zhi")]).astype(jnp.int32)

    piece_shape = shape((32, 2, ROWS, HEAD_WIDTH), BF16)
    grad_query, *grad_keys = vmem_call(
        attention_kernel,
        [shape((16, 2, 128, HEAD_WIDTH), BF16)] + [piece_shape] * 4,
        [SCALARS] * 3 + [WHOLE] * 6,
        scratch_shapes=[
            VMEM((32, PIECE, HEAD_WIDTH), BF16),
            VMEM((32, PIECE, HEAD_WIDTH), BF16),
            VMEM((3, PIECE, 256), F32),
            VMEM((32, PIECE, HEAD_WIDTH), F32),
            VMEM((32, PIECE, HEAD_WIDTH), F32),
            VMEM((HEAD_WIDTH, 256), F32),
        ],
        cost_estimate=pl.CostEstimate(
            flops=10 * 256 * PIECE * HEAD_WIDTH * 256, bytes_accessed=8 << 20, transcendentals=0
        ),
    )(lists, count, place, queries_own, queries_other, keys_own, *keys_near)

    back_near = [along_z(grad, step) for grad, step in zip(grad_keys[1:], STEPS[1:])]
    back_query = exchange(grad_query.reshape(32, 128, HEAD_WIDTH), PLANE + ("core",))
    query_out = vmem_call(
        sum_queries_kernel, shape((ROWS, QUERY_HEADS * HEAD_WIDTH), BF16), [WHOLE]
    )(back_query)
    total = grad_keys[0].astype(F32)
    for part in back_near:
        total = total + part.astype(F32)
    back_keys = exchange(total.astype(BF16), KEY_AXES)
    key_shape = shape((ROWS, KEY_HEADS * HEAD_WIDTH), BF16)
    key_out, value_out = vmem_call(sum_keys_kernel, [key_shape, key_shape], [WHOLE])(back_keys)
    return query_out, key_out, value_out


def solution(mesh):
    parts = Mesh(
        mesh.devices.reshape(4, 2, 4, 2, 2, 4), ("zhi", "core", "x", "yh", "yl", "zlo")
    )
    rows = P(TOKEN_AXES, None)
    return jax.shard_map(
        local,
        mesh=parts,
        in_specs=(rows,) * 7 + (P(), P()),
        out_specs=(rows,) * 3,
        check_vma=False,
    )
```

time: 1100 us -> 191 us (0.17)
  the two profiles are of different devices: /device:TPU:37 before, /device:TPU:16 now
where the time goes in v1:
time: 191 us; the launch traced here: 190 us
  starting transfers between devices  74 us (39%)
  waiting for transfers between devices  70.1 us (37%)
  Pallas kernels  34.8 us (18%)
  local copies, waits for them, and re-layouts  6.11 us (3%)
  other arithmetic  3.56 us (2%)
    all_to_all x4, waiting for transfers between devices, exchange(): return lax.all_to_all(value, axes, split_axis=0, concat_axis=0, tiled=True)  45.7 us
    all_to_all x4, starting transfers between devices, exchange(): return lax.all_to_all(value, axes, split_axis=0, concat_axis=0, tiled=True)  40.1 us
    ppermute x6, starting transfers between devices, along_z(): return lax.ppermute(value, ('zhi', 'zlo'), pairs)  32 us
    pallas_call x1, Pallas kernels, local(): vmem_call(attention_kernel, [shape((16, 2, 128, HEAD_WIDTH), BF16)] + [pi...  31.3 us
    ppermute x6, waiting for transfers between devices, along_z(): return lax.ppermute(value, ('zhi', 'zlo'), pairs)  24.4 us
    unnamed x26, local copies, waits for them, and re-layouts  4.65 us
  transfers between devices with their start and end apart: 11, of which 8 were waited for; matrix products, arithmetic and copies ran while one was open for 3% of the time, Pallas kernels for 1%

profile of v1, /device:TPU:16, one launch (start us, length us, event | category | flops | bytes accessed | tf_op | source)
XLA Modules:
  0.0 189.8 jit_solution(12250079444502138585)
XLA Ops:
  0.6 0.0 copy-start.2
  0.6 0.0 copy-start.1
  0.7 0.0 copy-start
  0.7 0.0 copy-start.3
  0.7 0.8 copy-done.3
  1.5 0.8 copy-done.4
  2.2 0.7 shard_map.113
  3.0 18.7 %all-to-all-start = ((bf16[32,2,16,128]{3,2,1,0:T(8,128)(2,1)}), bf16[32,2,16,128]{3,2,1,0:T(8,128)(2,1)S(1)}, u32[]{:S(2)}, u32[]{:S(2)}) async-start(bf16[32,2,16,128]{3,2,1,0:T(8,128)(2,1)} %shard_map.113), calls=%async_computation | async-start | bytes 524288 | tf_op jit(solution)/shard_map/all_to_all | solution.py:186
  21.7 0.7 convert_bitcast_fusion
  22.3 0.1 copy.19
  22.4 0.1 reshape.120.sums_ref
  22.5 0.7 convert_bitcast_fusion.1
  23.2 0.1 copy.18
  23.3 0.1 reshape.118.thr_ref
  23.4 0.0 copy-done.2
  23.4 0.0 copy-done.1
  23.4 1.2 shard_map.112
  24.6 17.1 %all-to-all-done.kv0_ref = bf16[32,2,16,128]{3,2,1,0:T(8,128)(2,1)S(1)} async-done(((bf16[32,2,16,128]{3,2,1,0:T(8,128)(2,1)}), bf16[32,2,16,128]{3,2,1,0:T(8,128)(2,1)S(1)}, u32[]{:S(2)}, u32[]{:S(2)}) %all-to-all-start) | async-done | bytes 262176 | tf_op jit(solution)/shard_map/all_to_all | solution.py:186
  41.8 6.4 %all-to-all-start.1 = ((bf16[16,17,16,128]{3,2,1,0:T(8,128)(2,1)}), bf16[16,17,16,128]{3,2,1,0:T(8,128)(2,1)S(1)}, u32[]{:S(2)}, u32[]{:S(2)}) async-start(bf16[16,17,16,128]{3,2,1,0:T(8,128)(2,1)} %shard_map.112), calls=%async_computation.1 | async-start | bytes 2228224 | tf_op jit(solution)/shard_map/all_to_all | solution.py:186
  48.1 0.1 slice_reduce_fusion
  48.3 0.1 squeeze.14
  48.3 0.1 squeeze.15
  48.5 0.4 dynamic-slice_reduce_fusion.3
  49.0 0.1 reshape.108
  49.0 0.1 reshape.111
  49.1 0.1 reshape.110
  49.2 0.1 reshape.109
  49.3 0.2 fusion.7
  49.5 0.1 pad_add_fusion
  49.6 9.6 %all-to-all-done.1.qa_ref = bf16[16,17,16,128]{3,2,1,0:T(8,128)(2,1)S(1)} async-done(((bf16[16,17,16,128]{3,2,1,0:T(8,128)(2,1)}), bf16[16,17,16,128]{3,2,1,0:T(8,128)(2,1)S(1)}, u32[]{:S(2)}, u32[]{:S(2)}) %all-to-all-start.1) | async-done | bytes 1114144 | tf_op jit(solution)/shard_map/all_to_all | solution.py:186
  59.2 1.9 %collective-permute-start = (bf16[16,17,16,128]{3,2,1,0:T(8,128)(2,1)S(1)}, bf16[16,17,16,128]{3,2,1,0:T(8,128)(2,1)S(1)}, u32[]{:S(2)}, u32[]{:S(2)}) collective-permute-start(bf16[16,17,16,128]{3,2,1,0:T(8,128)(2,1)S(1)} %all-to-all-done.1.qa_ref), channel_id=1, source_target_pairs={{0,64},{64,0},{1,65},{65,1},{2,66},{66,2},{3,67},{67,3},{4,68},{68... | collective-permute-start | bytes 3342344 | tf_op jit(solution)/shard_map/ppermute | solution.py:257
  61.2 0.3 fusion.16
  61.5 0.1 convert_reduce_fusion.count_ref
  61.6 0.4 select_reduce_fusion.1
  61.9 0.1 select_add_fusion
  62.0 0.4 select_reduce_fusion
  62.4 9.4 %collective-permute-start.3 = (bf16[32,2,16,128]{3,2,1,0:T(8,128)(2,1)S(1)}, bf16[32,2,16,128]{3,2,1,0:T(8,128)(2,1)S(1)}, u32[]{:S(2)}, u32[]{:S(2)}) collective-permute-start(bf16[32,2,16,128]{3,2,1,0:T(8,128)(2,1)S(1)} %all-to-all-done.kv0_ref), channel_id=1, source_target_pairs={{0,386},{1,387},{2,0},{3,1},{128,2},{129,3},{130,128},{131,129},{2... | collective-permute-start | bytes 786440 | tf_op jit(solution)/shard_map/ppermute | solution.py:191
  71.7 1.9 %collective-permute-start.2 = (bf16[32,2,16,128]{3,2,1,0:T(8,128)(2,1)S(1)}, bf16[32,2,16,128]{3,2,1,0:T(8,128)(2,1)S(1)}, u32[]{:S(2)}, u32[]{:S(2)}) collective-permute-start(bf16[32,2,16,128]{3,2,1,0:T(8,128)(2,1)S(1)} %all-to-all-done.kv0_ref), channel_id=1, source_target_pairs={{0,1},{1,2},{2,3},{3,128},{128,129},{129,130},{130,131},{131,256},... | collective-permute-start | bytes 786440 | tf_op jit(solution)/shard_map/ppermute | solution.py:191
  73.7 5.1 %collective-permute-start.1 = (bf16[32,2,16,128]{3,2,1,0:T(8,128)(2,1)S(1)}, bf16[32,2,16,128]{3,2,1,0:T(8,128)(2,1)S(1)}, u32[]{:S(2)}, u32[]{:S(2)}) collective-permute-start(bf16[32,2,16,128]{3,2,1,0:T(8,128)(2,1)S(1)} %all-to-all-done.kv0_ref), channel_id=1, source_target_pairs={{0,387},{1,0},{2,1},{3,2},{128,3},{129,128},{130,129},{131,130},{2... | collective-permute-start | bytes 786440 | tf_op jit(solution)/shard_map/ppermute | solution.py:191
  78.8 0.1 fusion.10
  78.9 0.1 select_n.95.list_ref
  79.0 0.1 pad_add_fusion.1.place_ref
  79.0 5.7 %collective-permute-done.3.kv3_ref = bf16[32,2,16,128]{3,2,1,0:T(8,128)(2,1)S(1)} collective-permute-done((bf16[32,2,16,128]{3,2,1,0:T(8,128)(2,1)S(1)}, bf16[32,2,16,128]{3,2,1,0:T(8,128)(2,1)S(1)}, u32[]{:S(2)}, u32[]{:S(2)}) %collective-permute-start.3) | collective-permute-done | bytes 262176 | tf_op jit(solution)/shard_map/ppermute | solution.py:191
  84.7 0.0 collective-permute-done.2.kv2_ref
  84.7 4.9 %collective-permute-done.1.kv1_ref = bf16[32,2,16,128]{3,2,1,0:T(8,128)(2,1)S(1)} collective-permute-done((bf16[32,2,16,128]{3,2,1,0:T(8,128)(2,1)S(1)}, bf16[32,2,16,128]{3,2,1,0:T(8,128)(2,1)S(1)}, u32[]{:S(2)}, u32[]{:S(2)}) %collective-permute-start.1) | collective-permute-done | bytes 262176 | tf_op jit(solution)/shard_map/ppermute | solution.py:191
  89.6 0.7 copy-done.7
  90.3 0.0 collective-permute-done.qb_ref
  90.3 0.9 copy-done.8
  91.3 31.3 %shard_map.114 = (bf16[16,2,128,128]{3,2,1,0:T(8,128)(2,1)}, bf16[32,2,16,128]{3,2,1,0:T(8,128)(2,1)S(1)}, bf16[32,2,16,128]{3,2,1,0:T(8,128)(2,1)S(1)}, bf16[32...) custom-call(s32[512]{0:T(512)S(1)} %select_n.95.list_ref, s32[16]{0:T(128)S(1)} %convert_reduce_fusion.count_ref, ...), custom_call_target="tpu_custom_call" | custom-call | flops 5368709120 | bytes 8388608 | tf_op jit(solution)/shard_map/pallas_call | solution.py:263
  122.6 0.7 copy-done.5
  123.3 0.7 copy-done.9
  124.0 6.4 %all-to-all-start.2 = ((bf16[32,128,128]{2,1,0:T(8,128)(2,1)}), bf16[32,128,128]{2,1,0:T(8,128)(2,1)S(1)}, u32[]{:S(2)}, u32[]{:S(2)}) async-start(bf16[32,128,128]{2,1,0:T(8,128)(2,1)} %bitcast.5), calls=%async_computation.2 | async-start | bytes 2097152 | tf_op jit(solution)/shard_map/all_to_all | solution.py:186
  130.4 1.9 %collective-permute-start.4 = (bf16[32,2,16,128]{3,2,1,0:T(8,128)(2,1)S(1)}, bf16[32,2,16,128]{3,2,1,0:T(8,128)(2,1)S(1)}, u32[]{:S(2)}, u32[]{:S(2)}) collective-permute-start(bf16[32,2,16,128]{3,2,1,0:T(8,128)(2,1)S(1)} %copy-done.10), channel_id=1, source_target_pairs={{0,1},{1,2},{2,3},{3,128},{128,129},{129,130},{130,131},{131,256},... | collective-permute-start | bytes 786440 | tf_op jit(solution)/shard_map/ppermute | solution.py:191
  132.3 9.8 %collective-permute-start.5 = (bf16[32,2,16,128]{3,2,1,0:T(8,128)(2,1)S(1)}, bf16[32,2,16,128]{3,2,1,0:T(8,128)(2,1)S(1)}, u32[]{:S(2)}, u32[]{:S(2)}) collective-permute-start(bf16[32,2,16,128]{3,2,1,0:T(8,128)(2,1)S(1)} %copy-done.6), channel_id=1, source_target_pairs={{0,387},{1,0},{2,1},{3,2},{128,3},{129,128},{130,129},{131,130},{2... | collective-permute-start | bytes 786440 | tf_op jit(solution)/shard_map/ppermute | solution.py:191
  142.1 3.9 %collective-permute-start.6 = (bf16[32,2,16,128]{3,2,1,0:T(8,128)(2,1)S(1)}, bf16[32,2,16,128]{3,2,1,0:T(8,128)(2,1)S(1)}, u32[]{:S(2)}, u32[]{:S(2)}) collective-permute-start(bf16[32,2,16,128]{3,2,1,0:T(8,128)(2,1)S(1)} %get-tuple-element.18), channel_id=1, source_target_pairs={{0,2},{1,3},{2,128},{3,129},{128,130},{129,131},{130,256},{131,257... | collective-permute-start | bytes 786440 | tf_op jit(solution)/shard_map/ppermute | solution.py:191
  146.0 1.0 collective-permute-done.4
  147.0 0.9 collective-permute-done.5
  148.0 11.9 %collective-permute-done.6 = bf16[32,2,16,128]{3,2,1,0:T(8,128)(2,1)S(1)} collective-permute-done((bf16[32,2,16,128]{3,2,1,0:T(8,128)(2,1)S(1)}, bf16[32,2,16,128]{3,2,1,0:T(8,128)(2,1)S(1)}, u32[]{:S(2)}, u32[]{:S(2)}) %collective-permute-start.6) | collective-permute-done | bytes 262176 | tf_op jit(solution)/shard_map/ppermute | solution.py:191
  159.8 0.8 add_convert_fusion
  160.7 0.0 all-to-all-done.2.in_ref
  160.7 8.7 %all-to-all-start.3 = ((bf16[32,2,16,128]{3,2,1,0:T(8,128)(2,1)}), bf16[32,2,16,128]{3,2,1,0:T(8,128)(2,1)S(1)}, u32[]{:S(2)}, u32[]{:S(2)}) async-start(bf16[32,2,16,128]{3,2,1,0:T(8,128)(2,1)} %add_convert_fusion), calls=%async_computation.3 | async-start | bytes 524288 | tf_op jit(solution)/shard_map/all_to_all | solution.py:186
  169.4 0.8 shard_map.115
  170.3 18.9 %all-to-all-done.3.in_ref = bf16[32,2,16,128]{3,2,1,0:T(8,128)(2,1)S(1)} async-done(((bf16[32,2,16,128]{3,2,1,0:T(8,128)(2,1)}), bf16[32,2,16,128]{3,2,1,0:T(8,128)(2,1)S(1)}, u32[]{:S(2)}, u32[]{:S(2)}) %all-to-all-start.3) | async-done | bytes 262176 | tf_op jit(solution)/shard_map/all_to_all | solution.py:186
  189.2 0.7 shard_map.116
  (18 shorter events, 0.1 us)
Async XLA Ops:
  0.6 22.7 %copy-start.2 = (bf16[16,8192]{1,0:T(8,128)(2,1)S(1)}, bf16[16,8192]{1,0:T(8,128)(2,1)}, u32[]{:S(2)}) copy-start(bf16[16,8192]{1,0:T(8,128)(2,1)} %sup_ref.1) | copy-start | bytes 786436
  0.6 22.7 %copy-start.1 = (bf16[16,8192]{1,0:T(8,128)(2,1)S(1)}, bf16[16,8192]{1,0:T(8,128)(2,1)}, u32[]{:S(2)}) copy-start(bf16[16,8192]{1,0:T(8,128)(2,1)} %do_ref.1) | copy-start | bytes 786436
  0.7 22.7 %copy-start = (bf16[16,8192]{1,0:T(8,128)(2,1)S(1)}, bf16[16,8192]{1,0:T(8,128)(2,1)}, u32[]{:S(2)}) copy-start(bf16[16,8192]{1,0:T(8,128)(2,1)} %q_ref.1) | copy-start | bytes 786436
  0.7 0.8 copy-start.3
  1.5 0.8 copy-start.4
  3.0 38.8 %all-to-all-start = ((bf16[32,2,16,128]{3,2,1,0:T(8,128)(2,1)}), bf16[32,2,16,128]{3,2,1,0:T(8,128)(2,1)S(1)}, u32[]{:S(2)}, u32[]{:S(2)}) async-start(bf16[32,2,16,128]{3,2,1,0:T(8,128)(2,1)} %shard_map.113), calls=%async_computation | async-start | bytes 524288 | tf_op jit(solution)/shard_map/all_to_all | solution.py:186
  24.6 23.5 %copy-start.11 = (s32[8192]{0:T(1024)S(1)}, s32[8192]{0:T(1024)}, u32[]{:S(2)}) copy-start(s32[8192]{0:T(1024)} %param.16) | copy-start | bytes 98308
  24.6 36.5 %copy-start.12 = (s32[64,64]{1,0:T(8,128)S(1)}, s32[64,64]{1,0:T(8,128)}, u32[]{:S(2)}) copy-start(s32[64,64]{1,0:T(8,128)} %param.17) | copy-start | bytes 49156
  41.8 17.5 %all-to-all-start.1 = ((bf16[16,17,16,128]{3,2,1,0:T(8,128)(2,1)}), bf16[16,17,16,128]{3,2,1,0:T(8,128)(2,1)S(1)}, u32[]{:S(2)}, u32[]{:S(2)}) async-start(bf16[16,17,16,128]{3,2,1,0:T(8,128)(2,1)} %shard_map.112), calls=%async_computation.1 | async-start | bytes 2228224 | tf_op jit(solution)/shard_map/all_to_all | solution.py:186
  59.2 31.1 %collective-permute-start = (bf16[16,17,16,128]{3,2,1,0:T(8,128)(2,1)S(1)}, bf16[16,17,16,128]{3,2,1,0:T(8,128)(2,1)S(1)}, u32[]{:S(2)}, u32[]{:S(2)}) collective-permute-start(bf16[16,17,16,128]{3,2,1,0:T(8,128)(2,1)S(1)} %all-to-all-done.1.qa_ref), channel_id=1, source_target_pairs={{0,64},{64,0},{1,65},{65,1},{2,66},{66,2},{3,67},{67,3},{4,68},{68... | collective-permute-start | bytes 3342344 | tf_op jit(solution)/shard_map/ppermute | solution.py:257
  62.4 22.4 %collective-permute-start.3 = (bf16[32,2,16,128]{3,2,1,0:T(8,128)(2,1)S(1)}, bf16[32,2,16,128]{3,2,1,0:T(8,128)(2,1)S(1)}, u32[]{:S(2)}, u32[]{:S(2)}) collective-permute-start(bf16[32,2,16,128]{3,2,1,0:T(8,128)(2,1)S(1)} %all-to-all-done.kv0_ref), channel_id=1, source_target_pairs={{0,386},{1,387},{2,0},{3,1},{128,2},{129,3},{130,128},{131,129},{2... | collective-permute-start | bytes 786440 | tf_op jit(solution)/shard_map/ppermute | solution.py:191
  71.7 13.0 %collective-permute-start.2 = (bf16[32,2,16,128]{3,2,1,0:T(8,128)(2,1)S(1)}, bf16[32,2,16,128]{3,2,1,0:T(8,128)(2,1)S(1)}, u32[]{:S(2)}, u32[]{:S(2)}) collective-permute-start(bf16[32,2,16,128]{3,2,1,0:T(8,128)(2,1)S(1)} %all-to-all-done.kv0_ref), channel_id=1, source_target_pairs={{0,1},{1,2},{2,3},{3,128},{128,129},{129,130},{130,131},{131,256},... | collective-permute-start | bytes 786440 | tf_op jit(solution)/shard_map/ppermute | solution.py:191
  73.7 16.0 %collective-permute-start.1 = (bf16[32,2,16,128]{3,2,1,0:T(8,128)(2,1)S(1)}, bf16[32,2,16,128]{3,2,1,0:T(8,128)(2,1)S(1)}, u32[]{:S(2)}, u32[]{:S(2)}) collective-permute-start(bf16[32,2,16,128]{3,2,1,0:T(8,128)(2,1)S(1)} %all-to-all-done.kv0_ref), channel_id=1, source_target_pairs={{0,387},{1,0},{2,1},{3,2},{128,3},{129,128},{130,129},{131,130},{2... | collective-permute-start | bytes 786440 | tf_op jit(solution)/shard_map/ppermute | solution.py:191
  89.6 0.7 copy-start.7
  90.3 1.0 copy-start.8
  122.6 0.7 copy-start.5
  123.3 0.7 copy-start.9
  124.0 6.4 %copy-start.10 = (bf16[32,2,16,128]{3,2,1,0:T(8,128)(2,1)S(1)}, bf16[32,2,16,128]{3,2,1,0:T(8,128)(2,1)}, u32[]{:S(2)}) copy-start(bf16[32,2,16,128]{3,2,1,0:T(8,128)(2,1)} %copy-done.9) | copy-start | bytes 786436
  124.0 8.3 %copy-start.6 = (bf16[32,2,16,128]{3,2,1,0:T(8,128)(2,1)S(1)}, bf16[32,2,16,128]{3,2,1,0:T(8,128)(2,1)}, u32[]{:S(2)}) copy-start(bf16[32,2,16,128]{3,2,1,0:T(8,128)(2,1)} %copy-done.5) | copy-start | bytes 786436
  124.0 36.7 %all-to-all-start.2 = ((bf16[32,128,128]{2,1,0:T(8,128)(2,1)}), bf16[32,128,128]{2,1,0:T(8,128)(2,1)S(1)}, u32[]{:S(2)}, u32[]{:S(2)}) async-start(bf16[32,128,128]{2,1,0:T(8,128)(2,1)} %bitcast.5), calls=%async_computation.2 | async-start | bytes 2097152 | tf_op jit(solution)/shard_map/all_to_all | solution.py:186
  130.4 16.6 %collective-permute-start.4 = (bf16[32,2,16,128]{3,2,1,0:T(8,128)(2,1)S(1)}, bf16[32,2,16,128]{3,2,1,0:T(8,128)(2,1)S(1)}, u32[]{:S(2)}, u32[]{:S(2)}) collective-permute-start(bf16[32,2,16,128]{3,2,1,0:T(8,128)(2,1)S(1)} %copy-done.10), channel_id=1, source_target_pairs={{0,1},{1,2},{2,3},{3,128},{128,129},{129,130},{130,131},{131,256},... | collective-permute-start | bytes 786440 | tf_op jit(solution)/shard_map/ppermute | solution.py:191
  132.3 15.6 %collective-permute-start.5 = (bf16[32,2,16,128]{3,2,1,0:T(8,128)(2,1)S(1)}, bf16[32,2,16,128]{3,2,1,0:T(8,128)(2,1)S(1)}, u32[]{:S(2)}, u32[]{:S(2)}) collective-permute-start(bf16[32,2,16,128]{3,2,1,0:T(8,128)(2,1)S(1)} %copy-done.6), channel_id=1, source_target_pairs={{0,387},{1,0},{2,1},{3,2},{128,3},{129,128},{130,129},{131,130},{2... | collective-permute-start | bytes 786440 | tf_op jit(solution)/shard_map/ppermute | solution.py:191
  142.1 17.7 %collective-permute-start.6 = (bf16[32,2,16,128]{3,2,1,0:T(8,128)(2,1)S(1)}, bf16[32,2,16,128]{3,2,1,0:T(8,128)(2,1)S(1)}, u32[]{:S(2)}, u32[]{:S(2)}) collective-permute-start(bf16[32,2,16,128]{3,2,1,0:T(8,128)(2,1)S(1)} %get-tuple-element.18), channel_id=1, source_target_pairs={{0,2},{1,3},{2,128},{3,129},{128,130},{129,131},{130,256},{131,257... | collective-permute-start | bytes 786440 | tf_op jit(solution)/shard_map/ppermute | solution.py:191
  160.7 28.5 %all-to-all-start.3 = ((bf16[32,2,16,128]{3,2,1,0:T(8,128)(2,1)}), bf16[32,2,16,128]{3,2,1,0:T(8,128)(2,1)S(1)}, u32[]{:S(2)}, u32[]{:S(2)}) async-start(bf16[32,2,16,128]{3,2,1,0:T(8,128)(2,1)} %add_convert_fusion), calls=%async_computation.3 | async-start | bytes 524288 | tf_op jit(solution)/shard_map/all_to_all | solution.py:186

commit v2 on v1

v2 whole, which is shorter than its diff:
```python
import functools

import jax
import jax.numpy as jnp
from jax import lax
from jax.experimental import pallas as pl
from jax.experimental.pallas import tpu as pltpu
from jax.sharding import Mesh, PartitionSpec as P

QUERY_HEADS = 64
KEY_HEADS = 8
HEAD_WIDTH = 128
BLK = 128
GROUP = 8
ROWS = 16
BATCH = 8
UNROLL = 3
SLOTS = 2 * GROUP + 3
PIECE = 64
SCALE = HEAD_WIDTH ** (-0.5)
FAR = 1e30
STEPS = (0, 1, -1, 2)
TOKEN_AXES = ("x", "yh", "yl", "zlo", "zhi", "core")
PLANE = ("x", "yh", "yl")
QUARTER = 4
VMEM = pltpu.VMEM
F32 = jnp.float32
BF16 = jnp.bfloat16


def vmem_call(kernel, out_shape, ins, **kw):
    return pl.pallas_call(
        kernel,
        out_shape=out_shape,
        in_specs=ins,
        out_specs=jax.tree.map(lambda _: pl.BlockSpec(memory_space=VMEM), out_shape),
        compiler_params=pltpu.CompilerParams(vmem_limit_bytes=48 << 20),
        **kw,
    )


WHOLE = pl.BlockSpec(memory_space=VMEM)
SCALARS = pl.BlockSpec(memory_space=pltpu.SMEM)


def pack_kernel(q_ref, do_ref, sup_ref, thr_ref, sums_ref, k_ref, v_ref, out_ref):
    for head in range(KEY_HEADS):
        dests = [(head // 2) * 4 + yh * 2 + head % 2 for yh in range(2)]
        products = []
        for g in range(GROUP):
            n = head * GROUP + g
            cols = slice(n * HEAD_WIDTH, (n + 1) * HEAD_WIDTH)
            query, grad = q_ref[:, cols], do_ref[:, cols]
            for dest in dests:
                out_ref[dest, g] = query
                out_ref[dest, GROUP + g] = grad
            products.append(grad.astype(F32) * sup_ref[:, cols].astype(F32))
        row_dot = jnp.sum(jnp.concatenate(products, axis=0).T, axis=0, keepdims=True)
        mean = row_dot / sums_ref[head : head + 1, :]
        high = mean.astype(BF16).astype(F32)
        low = mean - high
        stats = jnp.concatenate(
            [thr_ref[head : head + 1, :], high, low, jnp.zeros((13, 128), F32)], axis=0
        ).astype(BF16)
        cols = slice(head * HEAD_WIDTH, (head + 1) * HEAD_WIDTH)
        for dest in dests:
            out_ref[dest, 2 * GROUP] = stats
            out_ref[dest, 2 * GROUP + 1] = k_ref[:, cols]
            out_ref[dest, 2 * GROUP + 2] = v_ref[:, cols]


def attention_kernel(
    list_ref,
    count_ref,
    place_ref,
    qa_ref,
    qb_ref,
    own_ref,
    up_ref,
    down_ref,
    far_a_ref,
    far_b_ref,
    dq_ref,
    own_out,
    up_out,
    down_out,
    far_a_out,
    far_b_out,
    k_s,
    v_s,
    bias_s,
    dk_s,
    dv_s,
    dqt_s,
    q_s,
    do_s,
    stat_s,
    work_s,
):
    core, zhi = place_ref[0], place_ref[1]
    ins = [own_ref, up_ref, down_ref, far_a_ref, far_b_ref]
    outs = [own_out, up_out, down_out, far_a_out, far_b_out]
    places = [(0, 8), (8, 8), (16, 8), (24, 4), (28, 4)]
    for ref, (first, many) in zip(ins, places):
        for b in range(many):
            k_s[first + b] = ref[b, :, 0].reshape(PIECE, HEAD_WIDTH)
            v_s[first + b] = ref[b, :, 1].reshape(PIECE, HEAD_WIDTH)
    dk_s[...] = jnp.zeros_like(dk_s)
    dv_s[...] = jnp.zeros_like(dv_s)
    dqt_s[...] = jnp.zeros_like(dqt_s)
    row = lax.broadcasted_iota(jnp.int32, (PIECE, 256), 0)
    lane = lax.broadcasted_iota(jnp.int32, (PIECE, 256), 1)
    part = row >> 4
    step = jnp.where(part == 0, 0, jnp.where(part == 1, 1, jnp.where(part == 2, 3, 2)))
    key_offset = ((zhi + step) & 3) * 32 + core * 16 + (row & 15)
    query_core = jnp.where(lane < 128, core, 1 - core)
    query_offset = zhi * 32 + query_core * 16 + (lane & 15)
    bias_s[0] = jnp.zeros((PIECE, 256), F32)
    bias_s[1] = jnp.where(key_offset <= query_offset, 0.0, FAR)
    bias_s[2] = jnp.full((PIECE, 256), FAR, F32)

    def prepare(j, total):
        pair = (qa_ref, qb_ref)
        tile = (GROUP * ROWS, HEAD_WIDTH)
        q_s[j] = jnp.concatenate([ref[j, :GROUP].reshape(tile) for ref in pair], axis=0)
        do_s[j] = jnp.concatenate(
            [ref[j, GROUP : 2 * GROUP].reshape(tile) for ref in pair], axis=0
        )
        stats = jnp.concatenate([ref[j, 2 * GROUP].astype(F32) for ref in pair], axis=1)
        stat_s[j, 0:1] = stats[0:1]
        stat_s[j, 1:2] = stats[1:2] + stats[2:3]

        def put(batch, at):
            work_s[at] = j * 32 + batch * BATCH
            return at + 1

        return lax.fori_loop(0, (count_ref[j] + BATCH - 1) // BATCH, put, total)

    total = lax.fori_loop(0, 16, prepare, jnp.int32(0))
    for extra in range(UNROLL - 1):
        work_s[total + extra] = 512

    def contract(a, b, a_dim, b_dim):
        return lax.dot_general(
            a, b, (((a_dim,), (b_dim,)), ((), ())), preferred_element_type=F32
        )

    def one_step(step, _):
        results = []
        for way in range(UNROLL):
            base = work_s[step * UNROLL + way]
            j = jnp.minimum(base >> 5, 15)
            entries = [list_ref[base + u] for u in range(BATCH)]
            ids = [entry & 31 for entry in entries]
            keys = jnp.concatenate([k_s[i] for i in ids], axis=0)
            values = jnp.concatenate([v_s[i] for i in ids], axis=0)
            bias = jnp.concatenate([bias_s[entry >> 5] for entry in entries], axis=0)
            query, grad = q_s[j], do_s[j]
            scores = contract(keys, query, 1, 1)
            dprob = contract(values, grad, 1, 1)
            gate = jnp.maximum(scores * (0.5 * SCALE) - stat_s[j, 0:1] - bias, 0.0)
            probs = (gate * gate).astype(BF16)
            dscore = (SCALE * gate * (dprob - stat_s[j, 1:2])).astype(BF16)
            dv = contract(probs, grad, 1, 0)
            dk = contract(dscore, query, 1, 0)
            results.append((j, ids, dk, dv, contract(keys, dscore, 0, 0)))
        for j, ids, dk, dv, dqt in results:
            dqt_s[j] += dqt
            for u, i in enumerate(ids):
                dk_s[i] += dk[u * PIECE : (u + 1) * PIECE]
                dv_s[i] += dv[u * PIECE : (u + 1) * PIECE]
        return 0

    lax.fori_loop(0, (total + UNROLL - 1) // UNROLL, one_step, 0)

    def finish(j, _):
        dq = dqt_s[j].T.astype(BF16)
        dq_ref[j, core] = dq[:128]
        dq_ref[j, 1 - core] = dq[128:]
        return 0

    lax.fori_loop(0, 16, finish, 0)
    for ref, (first, many) in zip(outs, places):
        for b in range(many):
            for kind, sums in enumerate((dk_s, dv_s)):
                ref[b, :, kind] = sums[first + b].astype(BF16).reshape(4, ROWS, HEAD_WIDTH)


def total_kernel(own_ref, up_ref, down_ref, far_a_ref, far_b_ref, o0_ref, o1_ref, o2_ref, o3_ref):
    for b in range(8):
        far = far_a_ref[b] if b < 4 else far_b_ref[b - 4]
        total = (own_ref[b].astype(F32) + up_ref[b].astype(F32)) + (
            down_ref[b].astype(F32) + far.astype(F32)
        )
        for part, ref in enumerate((o0_ref, o1_ref, o2_ref, o3_ref)):
            ref[b] = total[part].astype(ref.dtype)


def merge_kernel(place_ref, dq_ref, o0_ref, o1_ref, o2_ref, o3_ref, out_ref):
    yh, core = place_ref[2], place_ref[0]
    for chip in range(16):
        for c in range(2):
            out_ref[chip * 2 + c, :GROUP] = dq_ref[chip, c].reshape(GROUP, ROWS, HEAD_WIDTH)
            out_ref[chip * 2 + c, GROUP:] = jnp.zeros((2, ROWS, HEAD_WIDTH), BF16)
    for b in range(8):
        total = (o0_ref[b] + o1_ref[b].astype(F32)) + (
            o2_ref[b].astype(F32) + o3_ref[b].astype(F32)
        )
        x, yl = b // 2, b % 2
        out_ref[((x * 2 + yh) * 2 + yl) * 2 + core, GROUP:] = total.astype(BF16)


def unpack_kernel(place_ref, in_ref, dq_ref, dk_ref, dv_ref):
    mine_yh, mine_core = place_ref[2], place_ref[0]
    for head in range(KEY_HEADS):
        x, yl = head // 2, head % 2
        parts = [
            in_ref[((x * 2 + yh) * 2 + yl) * 2 + core, :GROUP].astype(F32)
            for yh in range(2)
            for core in range(2)
        ]
        total = ((parts[0] + parts[1]) + (parts[2] + parts[3])).astype(BF16)
        for g in range(GROUP):
            n = head * GROUP + g
            dq_ref[:, n * HEAD_WIDTH : (n + 1) * HEAD_WIDTH] = total[g]
        cols = slice(head * HEAD_WIDTH, (head + 1) * HEAD_WIDTH)
        source = ((x * 2 + mine_yh) * 2 + yl) * 2 + mine_core
        dk_ref[:, cols] = in_ref[source, GROUP]
        dv_ref[:, cols] = in_ref[source, GROUP + 1]


def exchange(value, axes):
    return lax.all_to_all(value, axes, split_axis=0, concat_axis=0, tiled=True)


def along_z(value, steps):
    pairs = [(z, (z + steps) % 16) for z in range(16)]
    return lax.ppermute(value, ("zhi", "zlo"), pairs)


def active_lists(token_pos, block_mask):
    yh, zlo = lax.axis_index("yh"), lax.axis_index("zlo")
    block_ids = token_pos.reshape(64, BLK)[:, 0] // BLK
    by_place = block_ids.reshape(16, 4)
    query_pos = lax.dynamic_index_in_dim(by_place, zlo, 1, keepdims=False)
    mine = lax.dynamic_index_in_dim(block_ids.reshape(4, 2, 2, 4), yh, 1, keepdims=False)
    key_pos = jnp.concatenate(
        [
            lax.dynamic_index_in_dim(mine, (zlo + step) % 4, 2, keepdims=False).reshape(8)
            for step in STEPS
        ]
    )
    span = jnp.arange(64, dtype=jnp.int32)
    pick_query = (query_pos[:, None] == span[None, :]).astype(BF16)
    pick_key = (key_pos[:, None] == span[None, :]).astype(BF16)
    seen = jnp.dot(
        jnp.dot(pick_query, (block_mask == 1).astype(BF16), preferred_element_type=F32).astype(BF16),
        pick_key.T,
        preferred_element_type=F32,
    )
    active = (seen > 0.5) & (key_pos[None, :] <= query_pos[:, None])
    same = key_pos[None, :] == query_pos[:, None]
    number = jnp.arange(32, dtype=jnp.int32)
    ones = active.astype(jnp.int32)
    before = jnp.sum(
        jnp.where(number[None, None, :] < number[None, :, None], ones[:, None, :], 0), axis=2
    )
    count = jnp.sum(ones, axis=1)
    code = number[None, :] + 32 * same.astype(jnp.int32)
    lists = jnp.sum(
        jnp.where(active[:, None, :] & (before[:, None, :] == number[None, :, None]), code[:, None, :], 0),
        axis=2,
    )
    lists = jnp.where(number[None, :] < count[:, None], lists, 64)
    return jnp.concatenate([lists.reshape(512), jnp.full((32,), 64, jnp.int32)]), count


def local(
    queries,
    key_head_rows,
    value_head_rows,
    output_gradient,
    support_values,
    thresholds,
    gate_row_sums,
    token_pos,
    block_mask,
):
    shape = jax.ShapeDtypeStruct

    def by_head(stat):
        return stat.astype(F32).T.reshape(KEY_HEADS, GROUP * ROWS)

    place = jnp.stack([lax.axis_index(name) for name in ("core", "zhi", "yh")]).astype(jnp.int32)
    message = (ROWS, HEAD_WIDTH)
    send = vmem_call(pack_kernel, shape((16, SLOTS, *message), BF16), [WHOLE] * 7)(
        queries,
        output_gradient,
        support_values,
        by_head(thresholds),
        by_head(gate_row_sums),
        key_head_rows,
        value_head_rows,
    )
    arrived = exchange(send, PLANE)
    pieces = lax.dynamic_index_in_dim(
        arrived.reshape(4, 2, 2, SLOTS, *message)[:, :, :, 2 * GROUP + 1 :],
        lax.axis_index("yh"),
        1,
        keepdims=False,
    ).reshape(8, 2, *message)
    own = jnp.stack([pieces] + [along_z(pieces, -step * QUARTER) for step in STEPS[1:]], axis=1)
    near = [
        along_z(own, -1),
        along_z(own, 1),
        along_z(own[:4], -2),
        along_z(own[4:], 2),
    ]
    arrived_other = lax.ppermute(arrived, "core", [(0, 1), (1, 0)])
    lists, count = active_lists(token_pos, block_mask)

    def part(many):
        return shape((many, 4, 2, *message), BF16)

    piece = (PIECE, HEAD_WIDTH)
    grad_query, grad_own, *grad_near = vmem_call(
        attention_kernel,
        [shape((16, 2, GROUP * ROWS, HEAD_WIDTH), BF16)] + [part(m) for m in (8, 8, 8, 4, 4)],
        [SCALARS] * 3 + [WHOLE] * 7,
        scratch_shapes=[
            VMEM((32, *piece), BF16),
            VMEM((32, *piece), BF16),
            VMEM((3, PIECE, 256), F32),
            VMEM((32, *piece), F32),
            VMEM((32, *piece), F32),
            VMEM((16, HEAD_WIDTH, 256), F32),
            VMEM((16, 256, HEAD_WIDTH), BF16),
            VMEM((16, 256, HEAD_WIDTH), BF16),
            VMEM((16, 8, 256), F32),
            pltpu.SMEM((80,), jnp.int32),
        ],
    )(lists, count, place, arrived, arrived_other, own, *near)

    back = [
        along_z(grad, step) for grad, step in zip(grad_near, (1, -1, 2, -2), strict=True)
    ]
    eight = (8, 2, *message)
    first, *others = vmem_call(
        total_kernel, [shape(eight, F32)] + [shape(eight, BF16)] * 3, [WHOLE] * 5
    )(grad_own, *back)
    others = [along_z(grad, step * QUARTER) for grad, step in zip(others, STEPS[1:], strict=True)]
    send_back = vmem_call(
        merge_kernel, shape((32, GROUP + 2, *message), BF16), [SCALARS] + [WHOLE] * 5
    )(place, grad_query, first, *others)
    returned = exchange(send_back, PLANE + ("core",))
    return vmem_call(
        unpack_kernel,
        [
            shape((ROWS, QUERY_HEADS * HEAD_WIDTH), BF16),
            shape((ROWS, KEY_HEADS * HEAD_WIDTH), BF16),
            shape((ROWS, KEY_HEADS * HEAD_WIDTH), BF16),
        ],
        [SCALARS, WHOLE],
    )(place, returned)


def solution(mesh):
    parts = Mesh(
        mesh.devices.reshape(4, 2, 4, 2, 2, 4), ("zhi", "core", "x", "yh", "yl", "zlo")
    )
    rows = P(TOKEN_AXES, None)
    return jax.shard_map(
        local,
        mesh=parts,
        in_specs=(rows,) * 7 + (P(), P()),
        out_specs=(rows,) * 3,
        check_vma=False,
    )
```

time: 191 us -> 182 us (0.953)
  the two profiles are of different devices: /device:TPU:16 before, /device:TPU:1 now
where the time goes in v2:
time: 182 us; the launch traced here: 181 us
  starting transfers between devices  84.2 us (46%)
  waiting for transfers between devices  36.1 us (20%)
  blocking collectives  29.7 us (16%)
  Pallas kernels  20.8 us (11%)
  local copies, waits for them, and re-layouts  6.58 us (4%)
  other arithmetic  2.75 us (2%)
    ppermute x14, starting transfers between devices, along_z(): return lax.ppermute(value, ('zhi', 'zlo'), pairs)  70.6 us
    all_to_all x1, blocking collectives, exchange(): return lax.all_to_all(value, axes, split_axis=0, concat_axis=0, tiled=True)  29.7 us
    ppermute x14, waiting for transfers between devices, along_z(): return lax.ppermute(value, ('zhi', 'zlo'), pairs)  21.9 us
    pallas_call x1, Pallas kernels, local(): vmem_call(attention_kernel, [shape((16, 2, GROUP * ROWS, HEAD_WIDTH), BF1...  17.3 us
    all_to_all x1, waiting for transfers between devices, exchange(): return lax.all_to_all(value, axes, split_axis=0, concat_axis=0, tiled=True)  14.2 us
    all_to_all x1, starting transfers between devices, exchange(): return lax.all_to_all(value, axes, split_axis=0, concat_axis=0, tiled=True)  7.72 us
    ppermute x1, starting transfers between devices, local(): arrived_other = lax.ppermute(arrived, 'core', [(0, 1), (1, 0)])  5.8 us
    unnamed x14, local copies, waits for them, and re-layouts  4.38 us
  transfers between devices with their start and end apart: 16, of which 8 were waited for; matrix products, arithmetic and copies ran while one was open for 2% of the time, Pallas kernels for 0%

profile of v2, /device:TPU:1, one launch (start us, length us, event | category | flops | bytes accessed | tf_op | source)
XLA Modules:
  0.0 181.4 jit_solution(4891108546187576630)
XLA Ops:
  0.6 0.7 convert_bitcast_fusion.1
  1.3 0.7 convert_bitcast_fusion
  2.0 0.1 copy.28
  2.1 0.1 reshape.126.sums_ref
  2.2 0.1 copy.27
  2.3 0.1 reshape.124.thr_ref
  2.3 1.0 copy-done
  3.3 0.9 copy-done.1
  4.2 0.9 copy-done.2
  5.2 0.8 copy-done.3
  6.0 0.8 copy-done.4
  6.7 1.3 shard_map.112
  8.0 7.7 %all-to-all-start = ((bf16[16,19,16,128]{3,2,1,0:T(8,128)(2,1)}), bf16[16,19,16,128]{3,2,1,0:T(8,128)(2,1)S(1)}, u32[]{:S(2)}, u32[]{:S(2)}) async-start(bf16[16,19,16,128]{3,2,1,0:T(8,128)(2,1)} %shard_map.112), calls=%async_computation | async-start | bytes 2490368 | tf_op jit(solution)/shard_map/all_to_all | solution.py:233
  15.8 0.1 slice_reduce_fusion
  15.9 0.1 squeeze.16
  16.0 0.1 squeeze.17
  16.2 0.4 dynamic-slice_reduce_fusion.3
  16.6 0.1 reshape.113
  16.7 0.1 reshape.116
  16.8 0.1 reshape.115
  16.9 0.1 reshape.114
  17.0 0.2 fusion.7
  17.2 0.1 pad_add_fusion.1
  17.3 0.0 copy-done.6
  17.3 0.3 fusion.17
  17.6 0.3 select_reduce_fusion.1
  17.9 14.2 %all-to-all-done.qa_ref = bf16[16,19,16,128]{3,2,1,0:T(8,128)(2,1)S(1)} async-done(((bf16[16,19,16,128]{3,2,1,0:T(8,128)(2,1)}), bf16[16,19,16,128]{3,2,1,0:T(8,128)(2,1)S(1)}, u32[]{:S(2)}, u32[]{:S(2)}) %all-to-all-start) | async-done | bytes 1245216 | tf_op jit(solution)/shard_map/all_to_all | solution.py:233
  32.1 5.8 %collective-permute-start = (bf16[16,19,16,128]{3,2,1,0:T(8,128)(2,1)S(1)}, bf16[16,19,16,128]{3,2,1,0:T(8,128)(2,1)S(1)}, u32[]{:S(2)}, u32[]{:S(2)}) collective-permute-start(bf16[16,19,16,128]{3,2,1,0:T(8,128)(2,1)S(1)} %all-to-all-done.qa_ref), channel_id=1, source_target_pairs={{0,64},{64,0},{1,65},{65,1},{2,66},{66,2},{3,67},{67,3},{4,68},{68... | collective-permute-start | bytes 3735560 | tf_op jit(solution)/shard_map/ppermute | solution.py:319
  37.9 0.1 select_add_fusion
  38.0 0.3 select_reduce_fusion
  38.4 16.2 %collective-permute-start.3 = (bf16[8,2,16,128]{3,2,1,0:T(8,128)(2,1)S(1)}, bf16[8,2,16,128]{3,2,1,0:T(8,128)(2,1)S(1)}, u32[]{:S(2)}, u32[]{:S(2)}) collective-permute-start(bf16[8,2,16,128]{3,2,1,0:T(8,128)(2,1)S(1)} %bitcast.22), channel_id=1, source_target_pairs={{0,256},{1,257},{2,258},{3,259},{128,384},{129,385},{130,386},{131... | collective-permute-start | bytes 196616 | tf_op jit(solution)/shard_map/ppermute | solution.py:238
  54.6 4.0 %collective-permute-start.2 = (bf16[8,2,16,128]{3,2,1,0:T(8,128)(2,1)S(1)}, bf16[8,2,16,128]{3,2,1,0:T(8,128)(2,1)S(1)}, u32[]{:S(2)}, u32[]{:S(2)}) collective-permute-start(bf16[8,2,16,128]{3,2,1,0:T(8,128)(2,1)S(1)} %bitcast.23), channel_id=1, source_target_pairs={{0,128},{1,129},{2,130},{3,131},{128,256},{129,257},{130,258},{131... | collective-permute-start | bytes 196616 | tf_op jit(solution)/shard_map/ppermute | solution.py:238
  58.6 5.2 %collective-permute-start.1 = (bf16[8,2,16,128]{3,2,1,0:T(8,128)(2,1)S(1)}, bf16[8,2,16,128]{3,2,1,0:T(8,128)(2,1)S(1)}, u32[]{:S(2)}, u32[]{:S(2)}) collective-permute-start(bf16[8,2,16,128]{3,2,1,0:T(8,128)(2,1)S(1)} %bitcast.24), channel_id=1, source_target_pairs={{0,384},{1,385},{2,386},{3,387},{128,0},{129,1},{130,2},{131,3},{2... | collective-permute-start | bytes 196616 | tf_op jit(solution)/shard_map/ppermute | solution.py:238
  63.8 0.1 convert_reduce_fusion.count_ref
  63.9 0.0 collective-permute-done.3
  63.9 0.1 collective-permute-done.2
  64.0 6.6 %collective-permute-done.1 = bf16[8,2,16,128]{3,2,1,0:T(8,128)(2,1)S(1)} collective-permute-done((bf16[8,2,16,128]{3,2,1,0:T(8,128)(2,1)S(1)}, bf16[8,2,16,128]{3,2,1,0:T(8,128)(2,1)S(1)}, u32[]{:S(2)}, u32[]{:S(2)}) %collective-permute-start.1) | collective-permute-done | bytes 65568 | tf_op jit(solution)/shard_map/ppermute | solution.py:238
  70.6 2.5 %collective-permute-start.5 = (bf16[8,4,2,16,128]{4,3,2,1,0:T(8,128)(2,1)S(1)}, bf16[8,4,2,16,128]{4,3,2,1,0:T(8,128)(2,1)S(1)}, u32[]{:S(2)}, u32[]{:S(2)}) collective-permute-start(bf16[8,4,2,16,128]{4,3,2,1,0:T(8,128)(2,1)S(1)} %pad_maximum_fusion.own_ref), channel_id=1, source_target_pairs={{0,1},{1,2},{2,3},{3,128},{128,129},{129,130},{130,131},{131,256},... | collective-permute-start | bytes 786440 | tf_op jit(solution)/shard_map/ppermute | solution.py:238
  73.1 4.0 %collective-permute-start.4 = (bf16[8,4,2,16,128]{4,3,2,1,0:T(8,128)(2,1)S(1)}, bf16[8,4,2,16,128]{4,3,2,1,0:T(8,128)(2,1)S(1)}, u32[]{:S(2)}, u32[]{:S(2)}) collective-permute-start(bf16[8,4,2,16,128]{4,3,2,1,0:T(8,128)(2,1)S(1)} %pad_maximum_fusion.own_ref), channel_id=1, source_target_pairs={{0,387},{1,0},{2,1},{3,2},{128,3},{129,128},{130,129},{131,130},{2... | collective-permute-start | bytes 786440 | tf_op jit(solution)/shard_map/ppermute | solution.py:238
  77.1 0.7 fusion.16
  77.9 2.3 %collective-permute-start.7 = (bf16[4,4,2,16,128]{4,3,2,1,0:T(8,128)(2,1)}, bf16[4,4,2,16,128]{4,3,2,1,0:T(8,128)(2,1)S(1)}, u32[]{:S(2)}, u32[]{:S(2)}) collective-permute-start(bf16[4,4,2,16,128]{4,3,2,1,0:T(8,128)(2,1)} %get-tuple-element.27), channel_id=1, source_target_pairs={{0,2},{1,3},{2,128},{3,129},{128,130},{129,131},{130,256},{131,257... | collective-permute-start | bytes 393224 | tf_op jit(solution)/shard_map/ppermute | solution.py:238
  80.2 5.1 %collective-permute-start.6 = (bf16[4,4,2,16,128]{4,3,2,1,0:T(8,128)(2,1)}, bf16[4,4,2,16,128]{4,3,2,1,0:T(8,128)(2,1)S(1)}, u32[]{:S(2)}, u32[]{:S(2)}) collective-permute-start(bf16[4,4,2,16,128]{4,3,2,1,0:T(8,128)(2,1)} %get-tuple-element.28), channel_id=1, source_target_pairs={{0,386},{1,387},{2,0},{3,1},{128,2},{129,3},{130,128},{131,129},{2... | collective-permute-start | bytes 393224 | tf_op jit(solution)/shard_map/ppermute | solution.py:238
  85.2 0.1 fusion.10
  85.3 0.1 select_n.97
  85.4 0.1 pad_add_fusion.place_ref
  85.5 3.3 %collective-permute-done.7.far_b_ref = bf16[4,4,2,16,128]{4,3,2,1,0:T(8,128)(2,1)S(1)} collective-permute-done((bf16[4,4,2,16,128]{4,3,2,1,0:T(8,128)(2,1)}, bf16[4,4,2,16,128]{4,3,2,1,0:T(8,128)(2,1)S(1)}, u32[]{:S(2)}, u32[]{:S(2)}) %collective-permute-start.7) | collective-permute-done | bytes 131104 | tf_op jit(solution)/shard_map/ppermute | solution.py:238
  88.8 1.2 collective-permute-done.6.far_a_ref
  90.0 0.0 collective-permute-done.5.down_ref
  90.0 17.3 %shard_map.113 = (bf16[16,2,128,128]{3,2,1,0:T(8,128)(2,1)S(1)}, bf16[8,4,2,16,128]{4,3,2,1,0:T(8,128)(2,1)S(1)}, bf16[8,4,2,16,128]{4,3,2,1,0:T(8,128)(2,1)S(1)...) custom-call(s32[544]{0:T(1024)S(1)} %concatenate.7.list_ref, ...), custom_call_target="tpu_custom_call" | custom-call | tf_op jit(solution)/shard_map/pallas_call | solution.py:326
  107.3 1.9 %collective-permute-start.8 = (bf16[8,4,2,16,128]{4,3,2,1,0:T(8,128)(2,1)S(1)}, bf16[8,4,2,16,128]{4,3,2,1,0:T(8,128)(2,1)S(1)}, u32[]{:S(2)}, u32[]{:S(2)}) collective-permute-start(bf16[8,4,2,16,128]{4,3,2,1,0:T(8,128)(2,1)S(1)} %get-tuple-element.15), channel_id=1, source_target_pairs={{0,1},{1,2},{2,3},{3,128},{128,129},{129,130},{130,131},{131,256},... | collective-permute-start | bytes 786440 | tf_op jit(solution)/shard_map/ppermute | solution.py:238
  109.3 6.0 %collective-permute-start.9 = (bf16[8,4,2,16,128]{4,3,2,1,0:T(8,128)(2,1)S(1)}, bf16[8,4,2,16,128]{4,3,2,1,0:T(8,128)(2,1)S(1)}, u32[]{:S(2)}, u32[]{:S(2)}) collective-permute-start(bf16[8,4,2,16,128]{4,3,2,1,0:T(8,128)(2,1)S(1)} %get-tuple-element.16), channel_id=1, source_target_pairs={{0,387},{1,0},{2,1},{3,2},{128,3},{129,128},{130,129},{131,130},{2... | collective-permute-start | bytes 786440 | tf_op jit(solution)/shard_map/ppermute | solution.py:238
  115.3 1.9 %collective-permute-start.10 = (bf16[4,4,2,16,128]{4,3,2,1,0:T(8,128)(2,1)S(1)}, bf16[4,4,2,16,128]{4,3,2,1,0:T(8,128)(2,1)S(1)}, u32[]{:S(2)}, u32[]{:S(2)}) collective-permute-start(bf16[4,4,2,16,128]{4,3,2,1,0:T(8,128)(2,1)S(1)} %get-tuple-element.17), channel_id=1, source_target_pairs={{0,2},{1,3},{2,128},{3,129},{128,130},{129,131},{130,256},{131,257... | collective-permute-start | bytes 393224 | tf_op jit(solution)/shard_map/ppermute | solution.py:238
  117.2 5.5 %collective-permute-start.11 = (bf16[4,4,2,16,128]{4,3,2,1,0:T(8,128)(2,1)S(1)}, bf16[4,4,2,16,128]{4,3,2,1,0:T(8,128)(2,1)S(1)}, u32[]{:S(2)}, u32[]{:S(2)}) collective-permute-start(bf16[4,4,2,16,128]{4,3,2,1,0:T(8,128)(2,1)S(1)} %get-tuple-element.18), channel_id=1, source_target_pairs={{0,386},{1,387},{2,0},{3,1},{128,2},{129,3},{130,128},{131,129},{2... | collective-permute-start | bytes 393224 | tf_op jit(solution)/shard_map/ppermute | solution.py:238
  122.7 3.2 %collective-permute-done.10.far_a_ref = bf16[4,4,2,16,128]{4,3,2,1,0:T(8,128)(2,1)S(1)} collective-permute-done((bf16[4,4,2,16,128]{4,3,2,1,0:T(8,128)(2,1)S(1)}, bf16[4,4,2,16,128]{4,3,2,1,0:T(8,128)(2,1)S(1)}, u32[]{:S(2)}, u32[]{:S(2)}) %collective-permute-start.10) | collective-permute-done | bytes 131104 | tf_op jit(solution)/shard_map/ppermute | solution.py:238
  125.9 0.6 collective-permute-done.11.far_b_ref
  126.5 0.1 shard_map.114
  126.6 3.2 %collective-permute-start.12 = (bf16[8,2,16,128]{3,2,1,0:T(8,128)(2,1)S(1)}, bf16[8,2,16,128]{3,2,1,0:T(8,128)(2,1)S(1)}, u32[]{:S(2)}, u32[]{:S(2)}) collective-permute-start(bf16[8,2,16,128]{3,2,1,0:T(8,128)(2,1)S(1)} %get-tuple-element.20), channel_id=1, source_target_pairs={{0,128},{1,129},{2,130},{3,131},{128,256},{129,257},{130,258},{131... | collective-permute-start | bytes 196616 | tf_op jit(solution)/shard_map/ppermute | solution.py:238
  129.9 6.0 %collective-permute-start.13 = (bf16[8,2,16,128]{3,2,1,0:T(8,128)(2,1)S(1)}, bf16[8,2,16,128]{3,2,1,0:T(8,128)(2,1)S(1)}, u32[]{:S(2)}, u32[]{:S(2)}) collective-permute-start(bf16[8,2,16,128]{3,2,1,0:T(8,128)(2,1)S(1)} %get-tuple-element.21), channel_id=1, source_target_pairs={{0,384},{1,385},{2,386},{3,387},{128,0},{129,1},{130,2},{131,3},{2... | collective-permute-start | bytes 196616 | tf_op jit(solution)/shard_map/ppermute | solution.py:238
  135.8 6.9 %collective-permute-start.14 = (bf16[8,2,16,128]{3,2,1,0:T(8,128)(2,1)S(1)}, bf16[8,2,16,128]{3,2,1,0:T(8,128)(2,1)S(1)}, u32[]{:S(2)}, u32[]{:S(2)}) collective-permute-start(bf16[8,2,16,128]{3,2,1,0:T(8,128)(2,1)S(1)} %get-tuple-element.22), channel_id=1, source_target_pairs={{0,256},{1,257},{2,258},{3,259},{128,384},{129,385},{130,386},{131... | collective-permute-start | bytes 196616 | tf_op jit(solution)/shard_map/ppermute | solution.py:238
  142.8 0.0 collective-permute-done.12.o1_ref
  142.8 6.8 %collective-permute-done.14.o3_ref = bf16[8,2,16,128]{3,2,1,0:T(8,128)(2,1)S(1)} collective-permute-done((bf16[8,2,16,128]{3,2,1,0:T(8,128)(2,1)S(1)}, bf16[8,2,16,128]{3,2,1,0:T(8,128)(2,1)S(1)}, u32[]{:S(2)}, u32[]{:S(2)}) %collective-permute-start.14) | collective-permute-done | bytes 65568 | tf_op jit(solution)/shard_map/ppermute | solution.py:238
  149.6 0.7 shard_map.115
  150.2 29.7 %all_to_all.10.in_ref = bf16[32,10,16,128]{3,2,1,0:T(8,128)(2,1)S(1)} all-to-all(bf16[32,10,16,128]{3,2,1,0:T(8,128)(2,1)S(1)} %shard_map.115), channel_id=1, replica_groups=mesh['zhi'=4,'core'=2,'x'=4,'yh'=2,'yl'=2,'zlo'=4] {'x','yh','yl','core'}, dimensions={0} | all-to-all | bytes 2621440 | tf_op jit(solution)/shard_map/all_to_all | solution.py:233
  180.0 1.4 shard_map.116
  (21 shorter events, 0.1 us)
Async XLA Ops:
  2.3 1.0 copy-start
  3.3 0.9 copy-start.1
  4.2 0.9 copy-start.2
  5.2 0.8 copy-start.3
  6.0 0.8 copy-start.4
  8.0 7.8 %copy-start.5 = (s32[8192]{0:T(1024)S(1)}, s32[8192]{0:T(1024)}, u32[]{:S(2)}) copy-start(s32[8192]{0:T(1024)} %param.16) | copy-start | bytes 98308
  8.0 9.2 %copy-start.6 = (s32[64,64]{1,0:T(8,128)S(1)}, s32[64,64]{1,0:T(8,128)}, u32[]{:S(2)}) copy-start(s32[64,64]{1,0:T(8,128)} %param.17) | copy-start | bytes 49156
  8.0 24.1 %all-to-all-start = ((bf16[16,19,16,128]{3,2,1,0:T(8,128)(2,1)}), bf16[16,19,16,128]{3,2,1,0:T(8,128)(2,1)S(1)}, u32[]{:S(2)}, u32[]{:S(2)}) async-start(bf16[16,19,16,128]{3,2,1,0:T(8,128)(2,1)} %shard_map.112), calls=%async_computation | async-start | bytes 2490368 | tf_op jit(solution)/shard_map/all_to_all | solution.py:233
  32.1 57.9 %collective-permute-start = (bf16[16,19,16,128]{3,2,1,0:T(8,128)(2,1)S(1)}, bf16[16,19,16,128]{3,2,1,0:T(8,128)(2,1)S(1)}, u32[]{:S(2)}, u32[]{:S(2)}) collective-permute-start(bf16[16,19,16,128]{3,2,1,0:T(8,128)(2,1)S(1)} %all-to-all-done.qa_ref), channel_id=1, source_target_pairs={{0,64},{64,0},{1,65},{65,1},{2,66},{66,2},{3,67},{67,3},{4,68},{68... | collective-permute-start | bytes 3735560 | tf_op jit(solution)/shard_map/ppermute | solution.py:319
  38.4 25.5 %collective-permute-start.3 = (bf16[8,2,16,128]{3,2,1,0:T(8,128)(2,1)S(1)}, bf16[8,2,16,128]{3,2,1,0:T(8,128)(2,1)S(1)}, u32[]{:S(2)}, u32[]{:S(2)}) collective-permute-start(bf16[8,2,16,128]{3,2,1,0:T(8,128)(2,1)S(1)} %bitcast.22), channel_id=1, source_target_pairs={{0,256},{1,257},{2,258},{3,259},{128,384},{129,385},{130,386},{131... | collective-permute-start | bytes 196616 | tf_op jit(solution)/shard_map/ppermute | solution.py:238
  54.6 9.5 %collective-permute-start.2 = (bf16[8,2,16,128]{3,2,1,0:T(8,128)(2,1)S(1)}, bf16[8,2,16,128]{3,2,1,0:T(8,128)(2,1)S(1)}, u32[]{:S(2)}, u32[]{:S(2)}) collective-permute-start(bf16[8,2,16,128]{3,2,1,0:T(8,128)(2,1)S(1)} %bitcast.23), channel_id=1, source_target_pairs={{0,128},{1,129},{2,130},{3,131},{128,256},{129,257},{130,258},{131... | collective-permute-start | bytes 196616 | tf_op jit(solution)/shard_map/ppermute | solution.py:238
  58.6 12.0 %collective-permute-start.1 = (bf16[8,2,16,128]{3,2,1,0:T(8,128)(2,1)S(1)}, bf16[8,2,16,128]{3,2,1,0:T(8,128)(2,1)S(1)}, u32[]{:S(2)}, u32[]{:S(2)}) collective-permute-start(bf16[8,2,16,128]{3,2,1,0:T(8,128)(2,1)S(1)} %bitcast.24), channel_id=1, source_target_pairs={{0,384},{1,385},{2,386},{3,387},{128,0},{129,1},{130,2},{131,3},{2... | collective-permute-start | bytes 196616 | tf_op jit(solution)/shard_map/ppermute | solution.py:238
  70.6 19.4 %collective-permute-start.5 = (bf16[8,4,2,16,128]{4,3,2,1,0:T(8,128)(2,1)S(1)}, bf16[8,4,2,16,128]{4,3,2,1,0:T(8,128)(2,1)S(1)}, u32[]{:S(2)}, u32[]{:S(2)}) collective-permute-start(bf16[8,4,2,16,128]{4,3,2,1,0:T(8,128)(2,1)S(1)} %pad_maximum_fusion.own_ref), channel_id=1, source_target_pairs={{0,1},{1,2},{2,3},{3,128},{128,129},{129,130},{130,131},{131,256},... | collective-permute-start | bytes 786440 | tf_op jit(solution)/shard_map/ppermute | solution.py:238
  73.1 16.9 %collective-permute-start.4 = (bf16[8,4,2,16,128]{4,3,2,1,0:T(8,128)(2,1)S(1)}, bf16[8,4,2,16,128]{4,3,2,1,0:T(8,128)(2,1)S(1)}, u32[]{:S(2)}, u32[]{:S(2)}) collective-permute-start(bf16[8,4,2,16,128]{4,3,2,1,0:T(8,128)(2,1)S(1)} %pad_maximum_fusion.own_ref), channel_id=1, source_target_pairs={{0,387},{1,0},{2,1},{3,2},{128,3},{129,128},{130,129},{131,130},{2... | collective-permute-start | bytes 786440 | tf_op jit(solution)/shard_map/ppermute | solution.py:238
  77.9 11.0 %collective-permute-start.7 = (bf16[4,4,2,16,128]{4,3,2,1,0:T(8,128)(2,1)}, bf16[4,4,2,16,128]{4,3,2,1,0:T(8,128)(2,1)S(1)}, u32[]{:S(2)}, u32[]{:S(2)}) collective-permute-start(bf16[4,4,2,16,128]{4,3,2,1,0:T(8,128)(2,1)} %get-tuple-element.27), channel_id=1, source_target_pairs={{0,2},{1,3},{2,128},{3,129},{128,130},{129,131},{130,256},{131,257... | collective-permute-start | bytes 393224 | tf_op jit(solution)/shard_map/ppermute | solution.py:238
  80.2 9.9 %collective-permute-start.6 = (bf16[4,4,2,16,128]{4,3,2,1,0:T(8,128)(2,1)}, bf16[4,4,2,16,128]{4,3,2,1,0:T(8,128)(2,1)S(1)}, u32[]{:S(2)}, u32[]{:S(2)}) collective-permute-start(bf16[4,4,2,16,128]{4,3,2,1,0:T(8,128)(2,1)} %get-tuple-element.28), channel_id=1, source_target_pairs={{0,386},{1,387},{2,0},{3,1},{128,2},{129,3},{130,128},{131,129},{2... | collective-permute-start | bytes 393224 | tf_op jit(solution)/shard_map/ppermute | solution.py:238
  107.3 19.2 %collective-permute-start.8 = (bf16[8,4,2,16,128]{4,3,2,1,0:T(8,128)(2,1)S(1)}, bf16[8,4,2,16,128]{4,3,2,1,0:T(8,128)(2,1)S(1)}, u32[]{:S(2)}, u32[]{:S(2)}) collective-permute-start(bf16[8,4,2,16,128]{4,3,2,1,0:T(8,128)(2,1)S(1)} %get-tuple-element.15), channel_id=1, source_target_pairs={{0,1},{1,2},{2,3},{3,128},{128,129},{129,130},{130,131},{131,256},... | collective-permute-start | bytes 786440 | tf_op jit(solution)/shard_map/ppermute | solution.py:238
  109.3 17.3 %collective-permute-start.9 = (bf16[8,4,2,16,128]{4,3,2,1,0:T(8,128)(2,1)S(1)}, bf16[8,4,2,16,128]{4,3,2,1,0:T(8,128)(2,1)S(1)}, u32[]{:S(2)}, u32[]{:S(2)}) collective-permute-start(bf16[8,4,2,16,128]{4,3,2,1,0:T(8,128)(2,1)S(1)} %get-tuple-element.16), channel_id=1, source_target_pairs={{0,387},{1,0},{2,1},{3,2},{128,3},{129,128},{130,129},{131,130},{2... | collective-permute-start | bytes 786440 | tf_op jit(solution)/shard_map/ppermute | solution.py:238
  115.3 10.6 %collective-permute-start.10 = (bf16[4,4,2,16,128]{4,3,2,1,0:T(8,128)(2,1)S(1)}, bf16[4,4,2,16,128]{4,3,2,1,0:T(8,128)(2,1)S(1)}, u32[]{:S(2)}, u32[]{:S(2)}) collective-permute-start(bf16[4,4,2,16,128]{4,3,2,1,0:T(8,128)(2,1)S(1)} %get-tuple-element.17), channel_id=1, source_target_pairs={{0,2},{1,3},{2,128},{3,129},{128,130},{129,131},{130,256},{131,257... | collective-permute-start | bytes 393224 | tf_op jit(solution)/shard_map/ppermute | solution.py:238
  117.2 9.3 %collective-permute-start.11 = (bf16[4,4,2,16,128]{4,3,2,1,0:T(8,128)(2,1)S(1)}, bf16[4,4,2,16,128]{4,3,2,1,0:T(8,128)(2,1)S(1)}, u32[]{:S(2)}, u32[]{:S(2)}) collective-permute-start(bf16[4,4,2,16,128]{4,3,2,1,0:T(8,128)(2,1)S(1)} %get-tuple-element.18), channel_id=1, source_target_pairs={{0,386},{1,387},{2,0},{3,1},{128,2},{129,3},{130,128},{131,129},{2... | collective-permute-start | bytes 393224 | tf_op jit(solution)/shard_map/ppermute | solution.py:238
  126.6 16.1 %collective-permute-start.12 = (bf16[8,2,16,128]{3,2,1,0:T(8,128)(2,1)S(1)}, bf16[8,2,16,128]{3,2,1,0:T(8,128)(2,1)S(1)}, u32[]{:S(2)}, u32[]{:S(2)}) collective-permute-start(bf16[8,2,16,128]{3,2,1,0:T(8,128)(2,1)S(1)} %get-tuple-element.20), channel_id=1, source_target_pairs={{0,128},{1,129},{2,130},{3,131},{128,256},{129,257},{130,258},{131... | collective-permute-start | bytes 196616 | tf_op jit(solution)/shard_map/ppermute | solution.py:238
  129.9 12.9 %collective-permute-start.13 = (bf16[8,2,16,128]{3,2,1,0:T(8,128)(2,1)S(1)}, bf16[8,2,16,128]{3,2,1,0:T(8,128)(2,1)S(1)}, u32[]{:S(2)}, u32[]{:S(2)}) collective-permute-start(bf16[8,2,16,128]{3,2,1,0:T(8,128)(2,1)S(1)} %get-tuple-element.21), channel_id=1, source_target_pairs={{0,384},{1,385},{2,386},{3,387},{128,0},{129,1},{130,2},{131,3},{2... | collective-permute-start | bytes 196616 | tf_op jit(solution)/shard_map/ppermute | solution.py:238
  135.8 13.7 %collective-permute-start.14 = (bf16[8,2,16,128]{3,2,1,0:T(8,128)(2,1)S(1)}, bf16[8,2,16,128]{3,2,1,0:T(8,128)(2,1)S(1)}, u32[]{:S(2)}, u32[]{:S(2)}) collective-permute-start(bf16[8,2,16,128]{3,2,1,0:T(8,128)(2,1)S(1)} %get-tuple-element.22), channel_id=1, source_target_pairs={{0,256},{1,257},{2,258},{3,259},{128,384},{129,385},{130,386},{131... | collective-permute-start | bytes 196616 | tf_op jit(solution)/shard_map/ppermute | solution.py:238

commit v3 on v2

--- a/solution.py
+++ b/solution.py
@@ -15,14 +15,14 @@
 ROWS = 16
 BATCH = 8
 UNROLL = 3
-SLOTS = 2 * GROUP + 3
+SLOTS = 2 * GROUP + 1
 PIECE = 64
 SCALE = HEAD_WIDTH ** (-0.5)
 FAR = 1e30
 STEPS = (0, 1, -1, 2)
 TOKEN_AXES = ("x", "yh", "yl", "zlo", "zhi", "core")
 PLANE = ("x", "yh", "yl")
-QUARTER = 4
+KEY_AXES = ("x", "yl", "zhi")
 VMEM = pltpu.VMEM
 F32 = jnp.float32
 BF16 = jnp.bfloat16
@@ -43,7 +43,16 @@
 SCALARS = pl.BlockSpec(memory_space=pltpu.SMEM)
 
 
-def pack_kernel(q_ref, do_ref, sup_ref, thr_ref, sums_ref, k_ref, v_ref, out_ref):
+def pack_keys_kernel(k_ref, v_ref, out_ref):
+    for head in range(KEY_HEADS):
+        cols = slice(head * HEAD_WIDTH, (head + 1) * HEAD_WIDTH)
+        key, value = k_ref[:, cols], v_ref[:, cols]
+        for copy in range(4):
+            out_ref[head * 4 + copy, 0] = key
+            out_ref[head * 4 + copy, 1] = value
+
+
+def pack_queries_kernel(q_ref, do_ref, sup_ref, thr_ref, sums_ref, out_ref):
     for head in range(KEY_HEADS):
         dests = [(head // 2) * 4 + yh * 2 + head % 2 for yh in range(2)]
         products = []
@@ -62,11 +71,8 @@
         stats = jnp.concatenate(
             [thr_ref[head : head + 1, :], high, low, jnp.zeros((13, 128), F32)], axis=0
         ).astype(BF16)
-        cols = slice(head * HEAD_WIDTH, (head + 1) * HEAD_WIDTH)
         for dest in dests:
             out_ref[dest, 2 * GROUP] = stats
-            out_ref[dest, 2 * GROUP + 1] = k_ref[:, cols]
-            out_ref[dest, 2 * GROUP + 2] = v_ref[:, cols]
 
 
 def attention_kernel(
@@ -110,9 +116,7 @@
     dqt_s[...] = jnp.zeros_like(dqt_s)
     row = lax.broadcasted_iota(jnp.int32, (PIECE, 256), 0)
     lane = lax.broadcasted_iota(jnp.int32, (PIECE, 256), 1)
-    part = row >> 4
-    step = jnp.where(part == 0, 0, jnp.where(part == 1, 1, jnp.where(part == 2, 3, 2)))
-    key_offset = ((zhi + step) & 3) * 32 + core * 16 + (row & 15)
+    key_offset = (row >> 4) * 32 + core * 16 + (row & 15)
     query_core = jnp.where(lane < 128, core, 1 - core)
     query_offset = zhi * 32 + query_core * 16 + (lane & 15)
     bias_s[0] = jnp.zeros((PIECE, 256), F32)
@@ -186,47 +190,34 @@
                 ref[b, :, kind] = sums[first + b].astype(BF16).reshape(4, ROWS, HEAD_WIDTH)
 
 
-def total_kernel(own_ref, up_ref, down_ref, far_a_ref, far_b_ref, o0_ref, o1_ref, o2_ref, o3_ref):
+def total_kernel(own_ref, up_ref, down_ref, far_a_ref, far_b_ref, out_ref):
     for b in range(8):
         far = far_a_ref[b] if b < 4 else far_b_ref[b - 4]
         total = (own_ref[b].astype(F32) + up_ref[b].astype(F32)) + (
             down_ref[b].astype(F32) + far.astype(F32)
         )
-        for part, ref in enumerate((o0_ref, o1_ref, o2_ref, o3_ref)):
-            ref[b] = total[part].astype(ref.dtype)
-
-
-def merge_kernel(place_ref, dq_ref, o0_ref, o1_ref, o2_ref, o3_ref, out_ref):
-    yh, core = place_ref[2], place_ref[0]
-    for chip in range(16):
-        for c in range(2):
-            out_ref[chip * 2 + c, :GROUP] = dq_ref[chip, c].reshape(GROUP, ROWS, HEAD_WIDTH)
-            out_ref[chip * 2 + c, GROUP:] = jnp.zeros((2, ROWS, HEAD_WIDTH), BF16)
-    for b in range(8):
-        total = (o0_ref[b] + o1_ref[b].astype(F32)) + (
-            o2_ref[b].astype(F32) + o3_ref[b].astype(F32)
-        )
-        x, yl = b // 2, b % 2
-        out_ref[((x * 2 + yh) * 2 + yl) * 2 + core, GROUP:] = total.astype(BF16)
-
-
-def unpack_kernel(place_ref, in_ref, dq_ref, dk_ref, dv_ref):
-    mine_yh, mine_core = place_ref[2], place_ref[0]
+        out_ref[b] = total.astype(BF16)
+
+
+def sum_queries_kernel(in_ref, out_ref):
     for head in range(KEY_HEADS):
-        x, yl = head // 2, head % 2
         parts = [
-            in_ref[((x * 2 + yh) * 2 + yl) * 2 + core, :GROUP].astype(F32)
+            in_ref[(((head // 2) * 2 + yh) * 2 + head % 2) * 2 + core].astype(F32)
             for yh in range(2)
             for core in range(2)
         ]
         total = ((parts[0] + parts[1]) + (parts[2] + parts[3])).astype(BF16)
         for g in range(GROUP):
             n = head * GROUP + g
-            dq_ref[:, n * HEAD_WIDTH : (n + 1) * HEAD_WIDTH] = total[g]
+            out_ref[:, n * HEAD_WIDTH : (n + 1) * HEAD_WIDTH] = total[g * ROWS : (g + 1) * ROWS]
+
+
+def sum_keys_kernel(in_ref, dk_ref, dv_ref):
+    for head in range(KEY_HEADS):
         cols = slice(head * HEAD_WIDTH, (head + 1) * HEAD_WIDTH)
-        source = ((x * 2 + mine_yh) * 2 + yl) * 2 + mine_core
-        dk_ref[:, cols] = in_ref[source, GROUP]
-        dv_ref[:, cols] = in_ref[source, GROUP + 1]
+        for kind, ref in enumerate((dk_ref, dv_ref)):
+            parts = [in_ref[head * 4 + zhi, kind].astype(F32) for zhi in range(4)]
+            ref[:, cols] = ((parts[0] + parts[1]) + (parts[2] + parts[3])).astype(BF16)
 
 
 def exchange(value, axes):
@@ -291,31 +282,28 @@
     def by_head(stat):
         return stat.astype(F32).T.reshape(KEY_HEADS, GROUP * ROWS)
 
-    place = jnp.stack([lax.axis_index(name) for name in ("core", "zhi", "yh")]).astype(jnp.int32)
+    place = jnp.stack([lax.axis_index(name) for name in ("core", "zhi")]).astype(jnp.int32)
     message = (ROWS, HEAD_WIDTH)
-    send = vmem_call(pack_kernel, shape((16, SLOTS, *message), BF16), [WHOLE] * 7)(
+    send_keys = vmem_call(pack_keys_kernel, shape((32, 2, *message), BF16), [WHOLE] * 2)(
+        key_head_rows, value_head_rows
+    )
+    own = exchange(send_keys, KEY_AXES).reshape(8, 4, 2, *message)
+    send = vmem_call(pack_queries_kernel, shape((16, SLOTS, *message), BF16), [WHOLE] * 5)(
         queries,
         output_gradient,
         support_values,
         by_head(thresholds),
         by_head(gate_row_sums),
-        key_head_rows,
-        value_head_rows,
-    )
-    arrived = exchange(send, PLANE)
-    pieces = lax.dynamic_index_in_dim(
-        arrived.reshape(4, 2, 2, SLOTS, *message)[:, :, :, 2 * GROUP + 1 :],
-        lax.axis_index("yh"),
-        1,
-        keepdims=False,
-    ).reshape(8, 2, *message)
-    own = jnp.stack([pieces] + [along_z(pieces, -step * QUARTER) for step in STEPS[1:]], axis=1)
+    )
+    send, own = lax.optimization_barrier((send, own))
     near = [
         along_z(own, -1),
         along_z(own, 1),
         along_z(own[:4], -2),
         along_z(own[4:], 2),
     ]
+    arrived = exchange(send, PLANE)
+    arrived, *near = lax.optimization_barrier((arrived, *near))
     arrived_other = lax.ppermute(arrived, "core", [(0, 1), (1, 0)])
     lists, count = active_lists(token_pos, block_mask)
 
@@ -344,24 +332,17 @@
     back = [
         along_z(grad, step) for grad, step in zip(grad_near, (1, -1, 2, -2), strict=True)
     ]
-    eight = (8, 2, *message)
-    first, *others = vmem_call(
-        total_kernel, [shape(eight, F32)] + [shape(eight, BF16)] * 3, [WHOLE] * 5
-    )(grad_own, *back)
-    others = [along_z(grad, step * QUARTER) for grad, step in zip(others, STEPS[1:], strict=True)]
-    send_back = vmem_call(
-        merge_kernel, shape((32, GROUP + 2, *message), BF16), [SCALARS] + [WHOLE] * 5
-    )(place, grad_query, first, *others)
-    returned = exchange(send_back, PLANE + ("core",))
-    return vmem_call(
-        unpack_kernel,
-        [
-            shape((ROWS, QUERY_HEADS * HEAD_WIDTH), BF16),
-            shape((ROWS, KEY_HEADS * HEAD_WIDTH), BF16),
-            shape((ROWS, KEY_HEADS * HEAD_WIDTH), BF16),
-        ],
-        [SCALARS, WHOLE],
-    )(place, returned)
+    back_query = exchange(
+        grad_query.reshape(32, GROUP * ROWS, HEAD_WIDTH), PLANE + ("core",)
+    )
+    query_out = vmem_call(
+        sum_queries_kernel, shape((ROWS, QUERY_HEADS * HEAD_WIDTH), BF16), [WHOLE]
+    )(back_query)
+    total = vmem_call(total_kernel, part(8), [WHOLE] * 5)(grad_own, *back)
+    back_keys = exchange(total.reshape(32, 2, *message), KEY_AXES)
+    key_shape = shape((ROWS, KEY_HEADS * HEAD_WIDTH), BF16)
+    key_out, value_out = vmem_call(sum_keys_kernel, [key_shape, key_shape], [WHOLE])(back_keys)
+    return query_out, key_out, value_out
 
 
 def solution(mesh):

time: 182 us -> 156 us (0.86)
  the two profiles are of different devices: /device:TPU:1 before, /device:TPU:64 now
where the time goes in v3:
time: 156 us; the launch traced here: 155 us
  starting transfers between devices  70.8 us (45%)
  waiting for transfers between devices  52 us (33%)
  Pallas kernels  22.5 us (14%)
  local copies, waits for them, and re-layouts  6.56 us (4%)
  other arithmetic  2.04 us (1%)
    all_to_all x4, starting transfers between devices, exchange(): return lax.all_to_all(value, axes, split_axis=0, concat_axis=0, tiled=True)  40.3 us
    all_to_all x4, waiting for transfers between devices, exchange(): return lax.all_to_all(value, axes, split_axis=0, concat_axis=0, tiled=True)  40.1 us
    ppermute x8, starting transfers between devices, along_z(): return lax.ppermute(value, ('zhi', 'zlo'), pairs)  28.6 us
    pallas_call x1, Pallas kernels, local(): vmem_call(attention_kernel, [shape((16, 2, GROUP * ROWS, HEAD_WIDTH), BF1...  18.2 us
    ppermute x8, waiting for transfers between devices, along_z(): return lax.ppermute(value, ('zhi', 'zlo'), pairs)  10.6 us
    unnamed x30, local copies, waits for them, and re-layouts  4.31 us
  transfers between devices with their start and end apart: 13, of which 7 were waited for; matrix products, arithmetic and copies ran while one was open for 3% of the time, Pallas kernels for 2%

profile of v3, /device:TPU:64, one launch (start us, length us, event | category | flops | bytes accessed | tf_op | source)
XLA Modules:
  0.0 155.2 jit_solution(193160441764920420)
XLA Ops:
  0.6 0.0 copy-start.2
  0.7 0.8 copy-done.3
  1.5 0.8 copy-done.4
  2.2 0.7 shard_map.113
  3.0 17.2 %all-to-all-start = ((bf16[32,2,16,128]{3,2,1,0:T(8,128)(2,1)}), bf16[32,2,16,128]{3,2,1,0:T(8,128)(2,1)S(1)}, u32[]{:S(2)}, u32[]{:S(2)}) async-start(bf16[32,2,16,128]{3,2,1,0:T(8,128)(2,1)} %shard_map.113), calls=%async_computation | async-start | bytes 524288 | tf_op jit(solution)/shard_map/all_to_all | solution.py:224
  20.2 0.9 slice_reduce_fusion
  21.1 0.1 squeeze.14
  21.2 0.1 squeeze.15
  21.3 0.7 convert_bitcast_fusion
  22.0 0.1 copy.19
  22.1 0.1 reshape.128.sums_ref
  22.2 0.1 copy.18
  22.3 0.1 reshape.126.thr_ref
  22.4 1.3 shard_map.112
  23.6 20.6 %all-to-all-done = bf16[32,2,16,128]{3,2,1,0:T(8,128)(2,1)S(1)} async-done(((bf16[32,2,16,128]{3,2,1,0:T(8,128)(2,1)}), bf16[32,2,16,128]{3,2,1,0:T(8,128)(2,1)S(1)}, u32[]{:S(2)}, u32[]{:S(2)}) %all-to-all-start) | async-done | bytes 262176 | tf_op jit(solution)/shard_map/all_to_all | solution.py:224
  44.2 5.4 %all-to-all-start.1 = ((bf16[16,17,16,128]{3,2,1,0:T(8,128)(2,1)}), bf16[16,17,16,128]{3,2,1,0:T(8,128)(2,1)S(1)}, u32[]{:S(2)}, u32[]{:S(2)}) async-start(bf16[16,17,16,128]{3,2,1,0:T(8,128)(2,1)} %shard_map.112), calls=%async_computation.1 | async-start | bytes 2228224 | tf_op jit(solution)/shard_map/all_to_all | solution.py:224
  49.7 0.4 dynamic-slice_reduce_fusion.3
  50.1 0.1 reshape.114
  50.2 0.1 reshape.117
  50.3 0.1 reshape.116
  50.4 0.1 reshape.115
  50.5 1.9 %collective-permute-start.1 = (bf16[8,4,2,16,128]{4,3,2,1,0:T(8,128)(2,1)S(1)}, bf16[8,4,2,16,128]{4,3,2,1,0:T(8,128)(2,1)S(1)}, u32[]{:S(2)}, u32[]{:S(2)}) collective-permute-start(bf16[8,4,2,16,128]{4,3,2,1,0:T(8,128)(2,1)S(1)} %bitcast.10), channel_id=1, source_target_pairs={{0,1},{1,2},{2,3},{3,128},{128,129},{129,130},{130,131},{131,256},... | collective-permute-start | bytes 786440 | tf_op jit(solution)/shard_map/ppermute | solution.py:229
  52.4 3.9 %collective-permute-start = (bf16[8,4,2,16,128]{4,3,2,1,0:T(8,128)(2,1)S(1)}, bf16[8,4,2,16,128]{4,3,2,1,0:T(8,128)(2,1)S(1)}, u32[]{:S(2)}, u32[]{:S(2)}) collective-permute-start(bf16[8,4,2,16,128]{4,3,2,1,0:T(8,128)(2,1)S(1)} %bitcast.11), channel_id=1, source_target_pairs={{0,387},{1,0},{2,1},{3,2},{128,3},{129,128},{130,129},{131,130},{2... | collective-permute-start | bytes 786440 | tf_op jit(solution)/shard_map/ppermute | solution.py:229
  56.3 1.9 %collective-permute-start.3 = (bf16[4,4,2,16,128]{4,3,2,1,0:T(8,128)(2,1)S(1)}, bf16[4,4,2,16,128]{4,3,2,1,0:T(8,128)(2,1)S(1)}, u32[]{:S(2)}, u32[]{:S(2)}) collective-permute-start(bf16[4,4,2,16,128]{4,3,2,1,0:T(8,128)(2,1)S(1)} %get-tuple-element.37), channel_id=1, source_target_pairs={{0,2},{1,3},{2,128},{3,129},{128,130},{129,131},{130,256},{131,257... | collective-permute-start | bytes 393224 | tf_op jit(solution)/shard_map/ppermute | solution.py:229
  58.3 4.8 %collective-permute-start.2 = (bf16[4,4,2,16,128]{4,3,2,1,0:T(8,128)(2,1)S(1)}, bf16[4,4,2,16,128]{4,3,2,1,0:T(8,128)(2,1)S(1)}, u32[]{:S(2)}, u32[]{:S(2)}) collective-permute-start(bf16[4,4,2,16,128]{4,3,2,1,0:T(8,128)(2,1)S(1)} %get-tuple-element.38), channel_id=1, source_target_pairs={{0,386},{1,387},{2,0},{3,1},{128,2},{129,3},{130,128},{131,129},{2... | collective-permute-start | bytes 393224 | tf_op jit(solution)/shard_map/ppermute | solution.py:229
  63.1 0.1 pad_add_fusion
  63.2 0.2 fusion.7
  63.4 1.7 %collective-permute-done.3.far_b_ref = bf16[4,4,2,16,128]{4,3,2,1,0:T(8,128)(2,1)S(1)} collective-permute-done((bf16[4,4,2,16,128]{4,3,2,1,0:T(8,128)(2,1)S(1)}, bf16[4,4,2,16,128]{4,3,2,1,0:T(8,128)(2,1)S(1)}, u32[]{:S(2)}, u32[]{:S(2)}) %collective-permute-start.3) | collective-permute-done | bytes 131104 | tf_op jit(solution)/shard_map/ppermute | solution.py:229
  65.1 2.5 %collective-permute-done.2.far_a_ref = bf16[4,4,2,16,128]{4,3,2,1,0:T(8,128)(2,1)S(1)} collective-permute-done((bf16[4,4,2,16,128]{4,3,2,1,0:T(8,128)(2,1)S(1)}, bf16[4,4,2,16,128]{4,3,2,1,0:T(8,128)(2,1)S(1)}, u32[]{:S(2)}, u32[]{:S(2)}) %collective-permute-start.2) | collective-permute-done | bytes 131104 | tf_op jit(solution)/shard_map/ppermute | solution.py:229
  67.5 0.0 collective-permute-done.1.down_ref
  67.5 0.0 collective-permute-done.up_ref
  67.5 0.0 all-to-all-done.1.qa_ref
  67.5 1.9 %collective-permute-start.4 = (bf16[16,17,16,128]{3,2,1,0:T(8,128)(2,1)S(1)}, bf16[16,17,16,128]{3,2,1,0:T(8,128)(2,1)S(1)}, u32[]{:S(2)}, u32[]{:S(2)}) collective-permute-start(bf16[16,17,16,128]{3,2,1,0:T(8,128)(2,1)S(1)} %all-to-all-done.1.qa_ref), channel_id=1, source_target_pairs={{0,64},{64,0},{1,65},{65,1},{2,66},{66,2},{3,67},{67,3},{4,68},{68... | collective-permute-start | bytes 3342344 | tf_op jit(solution)/shard_map/ppermute | solution.py:307
  69.5 0.3 fusion.17
  69.8 0.1 convert_reduce_fusion.count_ref
  69.9 0.4 select_reduce_fusion.1
  70.3 0.1 select_add_fusion
  70.3 0.4 select_reduce_fusion
  70.7 0.1 fusion.10
  70.8 0.1 select_n.95
  70.8 0.1 pad_add_fusion.1.place_ref
  70.9 1.3 collective-permute-done.4.qb_ref
  72.2 18.2 %shard_map.114 = (bf16[16,2,128,128]{3,2,1,0:T(8,128)(2,1)}, bf16[8,4,2,16,128]{4,3,2,1,0:T(8,128)(2,1)S(1)}, bf16[8,4,2,16,128]{4,3,2,1,0:T(8,128)(2,1)S(1)}, b...) custom-call(s32[544]{0:T(1024)S(1)} %concatenate.7.list_ref, ...), custom_call_target="tpu_custom_call" | custom-call | tf_op jit(solution)/shard_map/pallas_call | solution.py:314
  90.4 0.7 copy-done.5
  91.1 0.7 copy-done.7
  91.8 0.6 copy-done.9
  92.4 0.7 copy-done.11
  93.1 6.0 %all-to-all-start.2 = ((bf16[32,128,128]{2,1,0:T(8,128)(2,1)}), bf16[32,128,128]{2,1,0:T(8,128)(2,1)S(1)}, u32[]{:S(2)}, u32[]{:S(2)}) async-start(bf16[32,128,128]{2,1,0:T(8,128)(2,1)} %bitcast.6), calls=%async_computation.2 | async-start | bytes 2097152 | tf_op jit(solution)/shard_map/all_to_all | solution.py:224
  99.0 5.3 %collective-permute-start.5 = (bf16[8,4,2,16,128]{4,3,2,1,0:T(8,128)(2,1)S(1)}, bf16[8,4,2,16,128]{4,3,2,1,0:T(8,128)(2,1)S(1)}, u32[]{:S(2)}, u32[]{:S(2)}) collective-permute-start(bf16[8,4,2,16,128]{4,3,2,1,0:T(8,128)(2,1)S(1)} %copy-done.8), channel_id=1, source_target_pairs={{0,1},{1,2},{2,3},{3,128},{128,129},{129,130},{130,131},{131,256},... | collective-permute-start | bytes 786440 | tf_op jit(solution)/shard_map/ppermute | solution.py:229
  104.4 0.0 copy-done.6
  104.4 1.9 %collective-permute-start.6 = (bf16[8,4,2,16,128]{4,3,2,1,0:T(8,128)(2,1)S(1)}, bf16[8,4,2,16,128]{4,3,2,1,0:T(8,128)(2,1)S(1)}, u32[]{:S(2)}, u32[]{:S(2)}) collective-permute-start(bf16[8,4,2,16,128]{4,3,2,1,0:T(8,128)(2,1)S(1)} %copy-done.6), channel_id=1, source_target_pairs={{0,387},{1,0},{2,1},{3,2},{128,3},{129,128},{130,129},{131,130},{2... | collective-permute-start | bytes 786440 | tf_op jit(solution)/shard_map/ppermute | solution.py:229
  106.3 0.0 copy-done.12
  106.3 5.0 %collective-permute-start.7 = (bf16[4,4,2,16,128]{4,3,2,1,0:T(8,128)(2,1)S(1)}, bf16[4,4,2,16,128]{4,3,2,1,0:T(8,128)(2,1)S(1)}, u32[]{:S(2)}, u32[]{:S(2)}) collective-permute-start(bf16[4,4,2,16,128]{4,3,2,1,0:T(8,128)(2,1)S(1)} %copy-done.12), channel_id=1, source_target_pairs={{0,2},{1,3},{2,128},{3,129},{128,130},{129,131},{130,256},{131,257... | collective-permute-start | bytes 393224 | tf_op jit(solution)/shard_map/ppermute | solution.py:229
  111.3 3.8 %collective-permute-start.8 = (bf16[4,4,2,16,128]{4,3,2,1,0:T(8,128)(2,1)S(1)}, bf16[4,4,2,16,128]{4,3,2,1,0:T(8,128)(2,1)S(1)}, u32[]{:S(2)}, u32[]{:S(2)}) collective-permute-start(bf16[4,4,2,16,128]{4,3,2,1,0:T(8,128)(2,1)S(1)} %copy-done.10), channel_id=1, source_target_pairs={{0,386},{1,387},{2,0},{3,1},{128,2},{129,3},{130,128},{131,129},{2... | collective-permute-start | bytes 393224 | tf_op jit(solution)/shard_map/ppermute | solution.py:229
  115.1 4.2 %collective-permute-done.7.far_a_ref = bf16[4,4,2,16,128]{4,3,2,1,0:T(8,128)(2,1)S(1)} collective-permute-done((bf16[4,4,2,16,128]{4,3,2,1,0:T(8,128)(2,1)S(1)}, bf16[4,4,2,16,128]{4,3,2,1,0:T(8,128)(2,1)S(1)}, u32[]{:S(2)}, u32[]{:S(2)}) %collective-permute-start.7) | collective-permute-done | bytes 131104 | tf_op jit(solution)/shard_map/ppermute | solution.py:229
  119.4 2.2 %collective-permute-done.8.far_b_ref = bf16[4,4,2,16,128]{4,3,2,1,0:T(8,128)(2,1)S(1)} collective-permute-done((bf16[4,4,2,16,128]{4,3,2,1,0:T(8,128)(2,1)S(1)}, bf16[4,4,2,16,128]{4,3,2,1,0:T(8,128)(2,1)S(1)}, u32[]{:S(2)}, u32[]{:S(2)}) %collective-permute-start.8) | collective-permute-done | bytes 131104 | tf_op jit(solution)/shard_map/ppermute | solution.py:229
  121.6 0.0 collective-permute-done.5.up_ref
  121.6 0.0 collective-permute-done.6.down_ref
  121.6 0.8 shard_map.116
  122.4 0.0 all-to-all-done.2.in_ref
  122.4 11.8 %all-to-all-start.3 = ((bf16[32,2,16,128]{3,2,1,0:T(8,128)(2,1)}), bf16[32,2,16,128]{3,2,1,0:T(8,128)(2,1)S(1)}, u32[]{:S(2)}, u32[]{:S(2)}) async-start(bf16[32,2,16,128]{3,2,1,0:T(8,128)(2,1)} %bitcast.7), calls=%async_computation.3 | async-start | bytes 524288 | tf_op jit(solution)/shard_map/all_to_all | solution.py:224
  134.2 0.8 shard_map.115
  135.0 19.6 %all-to-all-done.3.in_ref = bf16[32,2,16,128]{3,2,1,0:T(8,128)(2,1)S(1)} async-done(((bf16[32,2,16,128]{3,2,1,0:T(8,128)(2,1)}), bf16[32,2,16,128]{3,2,1,0:T(8,128)(2,1)S(1)}, u32[]{:S(2)}, u32[]{:S(2)}) %all-to-all-start.3) | async-done | bytes 262176 | tf_op jit(solution)/shard_map/all_to_all | solution.py:224
  154.6 0.7 shard_map.117
  (28 shorter events, 0.1 us)
Async XLA Ops:
  0.6 21.7 %copy-start.2 = (bf16[16,8192]{1,0:T(8,128)(2,1)S(1)}, bf16[16,8192]{1,0:T(8,128)(2,1)}, u32[]{:S(2)}) copy-start(bf16[16,8192]{1,0:T(8,128)(2,1)} %sup_ref.1) | copy-start | bytes 786436
  0.6 21.7 %copy-start.1 = (bf16[16,8192]{1,0:T(8,128)(2,1)S(1)}, bf16[16,8192]{1,0:T(8,128)(2,1)}, u32[]{:S(2)}) copy-start(bf16[16,8192]{1,0:T(8,128)(2,1)} %do_ref.1) | copy-start | bytes 786436
  0.7 21.7 %copy-start = (bf16[16,8192]{1,0:T(8,128)(2,1)S(1)}, bf16[16,8192]{1,0:T(8,128)(2,1)}, u32[]{:S(2)}) copy-start(bf16[16,8192]{1,0:T(8,128)(2,1)} %q_ref.1) | copy-start | bytes 786436
  0.7 0.8 copy-start.3
  1.5 0.8 copy-start.4
  2.2 19.9 %copy-start.13 = (bf16[16,64]{1,0:T(8,128)(2,1)S(1)}, bf16[16,64]{1,0:T(8,128)(2,1)}, u32[]{:S(2)}) copy-start(bf16[16,64]{1,0:T(8,128)(2,1)} %param.14) | copy-start | bytes 6148
  3.0 41.2 %all-to-all-start = ((bf16[32,2,16,128]{3,2,1,0:T(8,128)(2,1)}), bf16[32,2,16,128]{3,2,1,0:T(8,128)(2,1)S(1)}, u32[]{:S(2)}, u32[]{:S(2)}) async-start(bf16[32,2,16,128]{3,2,1,0:T(8,128)(2,1)} %shard_map.113), calls=%async_computation | async-start | bytes 524288 | tf_op jit(solution)/shard_map/all_to_all | solution.py:224
  44.2 25.3 %copy-start.14 = (s32[64,64]{1,0:T(8,128)S(1)}, s32[64,64]{1,0:T(8,128)}, u32[]{:S(2)}) copy-start(s32[64,64]{1,0:T(8,128)} %param.17) | copy-start | bytes 49156
  44.2 23.3 %all-to-all-start.1 = ((bf16[16,17,16,128]{3,2,1,0:T(8,128)(2,1)}), bf16[16,17,16,128]{3,2,1,0:T(8,128)(2,1)S(1)}, u32[]{:S(2)}, u32[]{:S(2)}) async-start(bf16[16,17,16,128]{3,2,1,0:T(8,128)(2,1)} %shard_map.112), calls=%async_computation.1 | async-start | bytes 2228224 | tf_op jit(solution)/shard_map/all_to_all | solution.py:224
  50.5 17.1 %collective-permute-start.1 = (bf16[8,4,2,16,128]{4,3,2,1,0:T(8,128)(2,1)S(1)}, bf16[8,4,2,16,128]{4,3,2,1,0:T(8,128)(2,1)S(1)}, u32[]{:S(2)}, u32[]{:S(2)}) collective-permute-start(bf16[8,4,2,16,128]{4,3,2,1,0:T(8,128)(2,1)S(1)} %bitcast.10), channel_id=1, source_target_pairs={{0,1},{1,2},{2,3},{3,128},{128,129},{129,130},{130,131},{131,256},... | collective-permute-start | bytes 786440 | tf_op jit(solution)/shard_map/ppermute | solution.py:229
  52.4 15.2 %collective-permute-start = (bf16[8,4,2,16,128]{4,3,2,1,0:T(8,128)(2,1)S(1)}, bf16[8,4,2,16,128]{4,3,2,1,0:T(8,128)(2,1)S(1)}, u32[]{:S(2)}, u32[]{:S(2)}) collective-permute-start(bf16[8,4,2,16,128]{4,3,2,1,0:T(8,128)(2,1)S(1)} %bitcast.11), channel_id=1, source_target_pairs={{0,387},{1,0},{2,1},{3,2},{128,3},{129,128},{130,129},{131,130},{2... | collective-permute-start | bytes 786440 | tf_op jit(solution)/shard_map/ppermute | solution.py:229
  56.3 8.7 %collective-permute-start.3 = (bf16[4,4,2,16,128]{4,3,2,1,0:T(8,128)(2,1)S(1)}, bf16[4,4,2,16,128]{4,3,2,1,0:T(8,128)(2,1)S(1)}, u32[]{:S(2)}, u32[]{:S(2)}) collective-permute-start(bf16[4,4,2,16,128]{4,3,2,1,0:T(8,128)(2,1)S(1)} %get-tuple-element.37), channel_id=1, source_target_pairs={{0,2},{1,3},{2,128},{3,129},{128,130},{129,131},{130,256},{131,257... | collective-permute-start | bytes 393224 | tf_op jit(solution)/shard_map/ppermute | solution.py:229
  58.3 9.3 %collective-permute-start.2 = (bf16[4,4,2,16,128]{4,3,2,1,0:T(8,128)(2,1)S(1)}, bf16[4,4,2,16,128]{4,3,2,1,0:T(8,128)(2,1)S(1)}, u32[]{:S(2)}, u32[]{:S(2)}) collective-permute-start(bf16[4,4,2,16,128]{4,3,2,1,0:T(8,128)(2,1)S(1)} %get-tuple-element.38), channel_id=1, source_target_pairs={{0,386},{1,387},{2,0},{3,1},{128,2},{129,3},{130,128},{131,129},{2... | collective-permute-start | bytes 393224 | tf_op jit(solution)/shard_map/ppermute | solution.py:229
  67.5 4.6 %collective-permute-start.4 = (bf16[16,17,16,128]{3,2,1,0:T(8,128)(2,1)S(1)}, bf16[16,17,16,128]{3,2,1,0:T(8,128)(2,1)S(1)}, u32[]{:S(2)}, u32[]{:S(2)}) collective-permute-start(bf16[16,17,16,128]{3,2,1,0:T(8,128)(2,1)S(1)} %all-to-all-done.1.qa_ref), channel_id=1, source_target_pairs={{0,64},{64,0},{1,65},{65,1},{2,66},{66,2},{3,67},{67,3},{4,68},{68... | collective-permute-start | bytes 3342344 | tf_op jit(solution)/shard_map/ppermute | solution.py:307
  90.4 0.7 copy-start.5
  91.1 0.7 copy-start.7
  91.8 0.6 copy-start.9
  92.4 0.7 copy-start.11
  93.1 6.0 %copy-start.8 = (bf16[8,4,2,16,128]{4,3,2,1,0:T(8,128)(2,1)S(1)}, bf16[8,4,2,16,128]{4,3,2,1,0:T(8,128)(2,1)}, u32[]{:S(2)}) copy-start(bf16[8,4,2,16,128]{4,3,2,1,0:T(8,128)(2,1)} %copy-done.7) | copy-start | bytes 786436
  93.1 11.3 %copy-start.6 = (bf16[8,4,2,16,128]{4,3,2,1,0:T(8,128)(2,1)S(1)}, bf16[8,4,2,16,128]{4,3,2,1,0:T(8,128)(2,1)}, u32[]{:S(2)}) copy-start(bf16[8,4,2,16,128]{4,3,2,1,0:T(8,128)(2,1)} %copy-done.5) | copy-start | bytes 786436
  93.1 13.3 %copy-start.12 = (bf16[4,4,2,16,128]{4,3,2,1,0:T(8,128)(2,1)S(1)}, bf16[4,4,2,16,128]{4,3,2,1,0:T(8,128)(2,1)}, u32[]{:S(2)}) copy-start(bf16[4,4,2,16,128]{4,3,2,1,0:T(8,128)(2,1)} %copy-done.11) | copy-start | bytes 393220
  93.1 18.3 %copy-start.10 = (bf16[4,4,2,16,128]{4,3,2,1,0:T(8,128)(2,1)S(1)}, bf16[4,4,2,16,128]{4,3,2,1,0:T(8,128)(2,1)}, u32[]{:S(2)}) copy-start(bf16[4,4,2,16,128]{4,3,2,1,0:T(8,128)(2,1)} %copy-done.9) | copy-start | bytes 393220
  93.1 29.4 %all-to-all-start.2 = ((bf16[32,128,128]{2,1,0:T(8,128)(2,1)}), bf16[32,128,128]{2,1,0:T(8,128)(2,1)S(1)}, u32[]{:S(2)}, u32[]{:S(2)}) async-start(bf16[32,128,128]{2,1,0:T(8,128)(2,1)} %bitcast.6), calls=%async_computation.2 | async-start | bytes 2097152 | tf_op jit(solution)/shard_map/all_to_all | solution.py:224
  99.0 22.5 %collective-permute-start.5 = (bf16[8,4,2,16,128]{4,3,2,1,0:T(8,128)(2,1)S(1)}, bf16[8,4,2,16,128]{4,3,2,1,0:T(8,128)(2,1)S(1)}, u32[]{:S(2)}, u32[]{:S(2)}) collective-permute-start(bf16[8,4,2,16,128]{4,3,2,1,0:T(8,128)(2,1)S(1)} %copy-done.8), channel_id=1, source_target_pairs={{0,1},{1,2},{2,3},{3,128},{128,129},{129,130},{130,131},{131,256},... | collective-permute-start | bytes 786440 | tf_op jit(solution)/shard_map/ppermute | solution.py:229
  104.4 17.2 %collective-permute-start.6 = (bf16[8,4,2,16,128]{4,3,2,1,0:T(8,128)(2,1)S(1)}, bf16[8,4,2,16,128]{4,3,2,1,0:T(8,128)(2,1)S(1)}, u32[]{:S(2)}, u32[]{:S(2)}) collective-permute-start(bf16[8,4,2,16,128]{4,3,2,1,0:T(8,128)(2,1)S(1)} %copy-done.6), channel_id=1, source_target_pairs={{0,387},{1,0},{2,1},{3,2},{128,3},{129,128},{130,129},{131,130},{2... | collective-permute-start | bytes 786440 | tf_op jit(solution)/shard_map/ppermute | solution.py:229
  106.3 13.1 %collective-permute-start.7 = (bf16[4,4,2,16,128]{4,3,2,1,0:T(8,128)(2,1)S(1)}, bf16[4,4,2,16,128]{4,3,2,1,0:T(8,128)(2,1)S(1)}, u32[]{:S(2)}, u32[]{:S(2)}) collective-permute-start(bf16[4,4,2,16,128]{4,3,2,1,0:T(8,128)(2,1)S(1)} %copy-done.12), channel_id=1, source_target_pairs={{0,2},{1,3},{2,128},{3,129},{128,130},{129,131},{130,256},{131,257... | collective-permute-start | bytes 393224 | tf_op jit(solution)/shard_map/ppermute | solution.py:229
  111.3 10.2 %collective-permute-start.8 = (bf16[4,4,2,16,128]{4,3,2,1,0:T(8,128)(2,1)S(1)}, bf16[4,4,2,16,128]{4,3,2,1,0:T(8,128)(2,1)S(1)}, u32[]{:S(2)}, u32[]{:S(2)}) collective-permute-start(bf16[4,4,2,16,128]{4,3,2,1,0:T(8,128)(2,1)S(1)} %copy-done.10), channel_id=1, source_target_pairs={{0,386},{1,387},{2,0},{3,1},{128,2},{129,3},{130,128},{131,129},{2... | collective-permute-start | bytes 393224 | tf_op jit(solution)/shard_map/ppermute | solution.py:229
  122.4 32.2 %all-to-all-start.3 = ((bf16[32,2,16,128]{3,2,1,0:T(8,128)(2,1)}), bf16[32,2,16,128]{3,2,1,0:T(8,128)(2,1)S(1)}, u32[]{:S(2)}, u32[]{:S(2)}) async-start(bf16[32,2,16,128]{3,2,1,0:T(8,128)(2,1)} %bitcast.7), calls=%async_computation.3 | async-start | bytes 524288 | tf_op jit(solution)/shard_map/all_to_all | solution.py:224

commit v4 on v3

v4 whole, which is shorter than its diff:
```python
import functools

import jax
import jax.numpy as jnp
from jax import lax
from jax.experimental import pallas as pl
from jax.experimental.pallas import tpu as pltpu
from jax.sharding import Mesh, PartitionSpec as P

QUERY_HEADS = 64
KEY_HEADS = 8
HEAD_WIDTH = 128
BLK = 128
GROUP = 8
ROWS = 16
OWN, REST = 8, 24
BATCH = {OWN: 4, REST: 8}
UNROLL = {OWN: 4, REST: 3}
SLOTS = 2 * GROUP + 1
PIECE = 64
SCALE = HEAD_WIDTH ** (-0.5)
FAR = 1e30
STEPS = (0, 1, -1, 2)
QUARTER = 4
TOKEN_AXES = ("x", "yh", "yl", "zlo", "zhi", "core")
PLANE = ("x", "yh", "yl")
HEAD_AXES = ("x", "yl")
KEY_AXES = ("x", "yl", "zhi")
VMEM = pltpu.VMEM
F32 = jnp.float32
BF16 = jnp.bfloat16


def vmem_call(kernel, out_shape, ins, **kw):
    return pl.pallas_call(
        kernel,
        out_shape=out_shape,
        in_specs=ins,
        out_specs=jax.tree.map(lambda _: pl.BlockSpec(memory_space=VMEM), out_shape),
        compiler_params=pltpu.CompilerParams(vmem_limit_bytes=20 << 20),
        **kw,
    )


WHOLE = pl.BlockSpec(memory_space=VMEM)
SCALARS = pl.BlockSpec(memory_space=pltpu.SMEM)


def pack_keys_kernel(k_ref, v_ref, out_ref):
    for head in range(KEY_HEADS):
        cols = slice(head * HEAD_WIDTH, (head + 1) * HEAD_WIDTH)
        out_ref[head, 0] = k_ref[:, cols]
        out_ref[head, 1] = v_ref[:, cols]


def pack_queries_kernel(q_ref, do_ref, sup_ref, thr_ref, sums_ref, out_ref):
    for head in range(KEY_HEADS):
        dests = [(head // 2) * 4 + yh * 2 + head % 2 for yh in range(2)]
        products = []
        for g in range(GROUP):
            n = head * GROUP + g
            cols = slice(n * HEAD_WIDTH, (n + 1) * HEAD_WIDTH)
            query, grad = q_ref[:, cols], do_ref[:, cols]
            for dest in dests:
                out_ref[dest, g] = query
                out_ref[dest, GROUP + g] = grad
            products.append(grad.astype(F32) * sup_ref[:, cols].astype(F32))
        row_dot = jnp.sum(jnp.concatenate(products, axis=0).T, axis=0, keepdims=True)
        mean = row_dot / sums_ref[head : head + 1, :]
        high = mean.astype(BF16).astype(F32)
        low = mean - high
        stats = jnp.concatenate(
            [thr_ref[head : head + 1, :], high, low, jnp.zeros((13, 128), F32)], axis=0
        ).astype(BF16)
        for dest in dests:
            out_ref[dest, 2 * GROUP] = stats


def contract(a, b, a_dim, b_dim):
    return lax.dot_general(a, b, (((a_dim,), (b_dim,)), ((), ())), preferred_element_type=F32)


def load_keys(refs, k_s, v_s):
    at = 0
    for ref in refs:
        for b in range(ref.shape[0]):
            k_s[at] = ref[b, :, 0].reshape(PIECE, HEAD_WIDTH)
            v_s[at] = ref[b, :, 1].reshape(PIECE, HEAD_WIDTH)
            at += 1


def store_keys(refs, dk_s, dv_s):
    at = 0
    for ref in refs:
        for b in range(ref.shape[0]):
            for kind, sums in enumerate((dk_s, dv_s)):
                ref[b, :, kind] = sums[at].astype(BF16).reshape(4, ROWS, HEAD_WIDTH)
            at += 1


def add_tiles(
    pieces, list_ref, count_ref, k_s, v_s, dk_s, dv_s, dqt_s, q_s, do_s, stat_s, work_s, bias_s
):
    batch, unroll = BATCH[pieces], UNROLL[pieces]

    def plan(j, total):
        def put(step, at):
            work_s[at] = j * pieces + step * batch
            return at + 1

        return lax.fori_loop(0, (count_ref[j] + batch - 1) // batch, put, total)

    total = lax.fori_loop(0, 16, plan, jnp.int32(0))
    for extra in range(unroll - 1):
        work_s[total + extra] = 16 * pieces

    def one_step(step, _):
        results = []
        for way in range(unroll):
            base = work_s[step * unroll + way]
            j = jnp.minimum(base // pieces, 15)
            entries = [list_ref[base + u] for u in range(batch)]
            ids = [entry & 31 for entry in entries]
            keys = jnp.concatenate([k_s[i] for i in ids], axis=0)
            values = jnp.concatenate([v_s[i] for i in ids], axis=0)
            query, grad = q_s[j], do_s[j]
            thresh = stat_s[j, 0:1]
            scores = contract(keys, query, 1, 1) * (0.5 * SCALE)
            if bias_s is None:
                above = jnp.concatenate(
                    [
                        scores[u * PIECE : (u + 1) * PIECE]
                        - (thresh + jnp.where(entry >= 64, FAR, 0.0))
                        for u, entry in enumerate(entries)
                    ],
                    axis=0,
                )
            else:
                bias = jnp.concatenate([bias_s[entry >> 5] for entry in entries], axis=0)
                above = scores - thresh - bias
            gate = jnp.maximum(above, 0.0)
            dprob = contract(values, grad, 1, 1)
            probs = (gate * gate).astype(BF16)
            dscore = (SCALE * gate * (dprob - stat_s[j, 1:2])).astype(BF16)
            dv = contract(probs, grad, 1, 0)
            dk = contract(dscore, query, 1, 0)
            results.append((j, ids, dk, dv, contract(keys, dscore, 0, 0)))
        for j, ids, dk, dv, dqt in results:
            dqt_s[j] += dqt
            for u, i in enumerate(ids):
                dk_s[i] += dk[u * PIECE : (u + 1) * PIECE]
                dv_s[i] += dv[u * PIECE : (u + 1) * PIECE]
        return 0

    lax.fori_loop(0, (total + unroll - 1) // unroll, one_step, 0)


def own_kernel(
    list_ref,
    count_ref,
    place_ref,
    qa_ref,
    qb_ref,
    own_ref,
    own_out,
    dqt_s,
    q_s,
    do_s,
    stat_s,
    k_s,
    v_s,
    bias_s,
    dk_s,
    dv_s,
    work_s,
):
    core, zhi = place_ref[0], place_ref[1]
    load_keys([own_ref], k_s, v_s)
    dk_s[...] = jnp.zeros_like(dk_s)
    dv_s[...] = jnp.zeros_like(dv_s)
    dqt_s[...] = jnp.zeros_like(dqt_s)
    row = lax.broadcasted_iota(jnp.int32, (PIECE, 256), 0)
    lane = lax.broadcasted_iota(jnp.int32, (PIECE, 256), 1)
    part = row >> 4
    step = jnp.where(part == 0, 0, jnp.where(part == 1, 1, jnp.where(part == 2, 3, 2)))
    key_offset = ((zhi + step) & 3) * 32 + core * 16 + (row & 15)
    query_core = jnp.where(lane < 128, core, 1 - core)
    query_offset = zhi * 32 + query_core * 16 + (lane & 15)
    bias_s[0] = jnp.zeros((PIECE, 256), F32)
    bias_s[1] = jnp.where(key_offset <= query_offset, 0.0, FAR)
    bias_s[2] = jnp.full((PIECE, 256), FAR, F32)

    def prepare(j, _):
        pair = (qa_ref, qb_ref)
        tile = (GROUP * ROWS, HEAD_WIDTH)
        q_s[j] = jnp.concatenate([ref[j, :GROUP].reshape(tile) for ref in pair], axis=0)
        do_s[j] = jnp.concatenate(
            [ref[j, GROUP : 2 * GROUP].reshape(tile) for ref in pair], axis=0
        )
        stats = jnp.concatenate([ref[j, 2 * GROUP].astype(F32) for ref in pair], axis=1)
        stat_s[j, 0:1] = stats[0:1]
        stat_s[j, 1:2] = stats[1:2] + stats[2:3]
        return 0

    lax.fori_loop(0, 16, prepare, 0)
    add_tiles(
        OWN, list_ref, count_ref, k_s, v_s, dk_s, dv_s, dqt_s, q_s, do_s, stat_s, work_s, bias_s
    )
    store_keys([own_out], dk_s, dv_s)


def rest_kernel(
    list_ref,
    count_ref,
    place_ref,
    dqt_in,
    q_s,
    do_s,
    stat_s,
    up_ref,
    down_ref,
    far_a_ref,
    far_b_ref,
    dq_ref,
    up_out,
    down_out,
    far_a_out,
    far_b_out,
    k_s,
    v_s,
    dk_s,
    dv_s,
    dqt_s,
    work_s,
):
    core = place_ref[0]
    load_keys([up_ref, down_ref, far_a_ref, far_b_ref], k_s, v_s)
    dk_s[...] = jnp.zeros_like(dk_s)
    dv_s[...] = jnp.zeros_like(dv_s)
    dqt_s[...] = dqt_in[...]
    add_tiles(
        REST, list_ref, count_ref, k_s, v_s, dk_s, dv_s, dqt_s, q_s, do_s, stat_s, work_s, None
    )

    def finish(j, _):
        dq = dqt_s[j].T.astype(BF16)
        dq_ref[j, core] = dq[:128]
        dq_ref[j, 1 - core] = dq[128:]
        return 0

    lax.fori_loop(0, 16, finish, 0)
    store_keys([up_out, down_out, far_a_out, far_b_out], dk_s, dv_s)


def total_kernel(place_ref, own_ref, up_ref, down_ref, far_a_ref, far_b_ref, out_ref):
    for b in range(8):
        far = far_a_ref[b] if b < 4 else far_b_ref[b - 4]
        total = (own_ref[b].astype(F32) + up_ref[b].astype(F32)) + (
            down_ref[b].astype(F32) + far.astype(F32)
        )
        for part, step in enumerate(STEPS):
            out_ref[b, (place_ref[1] + step) & 3] = total[part].astype(BF16)


def sum_queries_kernel(in_ref, out_ref):
    for head in range(KEY_HEADS):
        parts = [
            in_ref[(((head // 2) * 2 + yh) * 2 + head % 2) * 2 + core].astype(F32)
            for yh in range(2)
            for core in range(2)
        ]
        total = ((parts[0] + parts[1]) + (parts[2] + parts[3])).astype(BF16)
        for g in range(GROUP):
            n = head * GROUP + g
            out_ref[:, n * HEAD_WIDTH : (n + 1) * HEAD_WIDTH] = total[g * ROWS : (g + 1) * ROWS]


def sum_keys_kernel(in_ref, dk_ref, dv_ref):
    for head in range(KEY_HEADS):
        cols = slice(head * HEAD_WIDTH, (head + 1) * HEAD_WIDTH)
        for kind, ref in enumerate((dk_ref, dv_ref)):
            parts = [in_ref[head * 4 + zhi, kind].astype(F32) for zhi in range(4)]
            ref[:, cols] = ((parts[0] + parts[1]) + (parts[2] + parts[3])).astype(BF16)


def exchange(value, axes):
    return lax.all_to_all(value, axes, split_axis=0, concat_axis=0, tiled=True)


def along_z(value, steps):
    pairs = [(z, (z + steps) % 16) for z in range(16)]
    return lax.ppermute(value, ("zhi", "zlo"), pairs)


def active_lists(token_pos, block_mask):
    yh, zlo = lax.axis_index("yh"), lax.axis_index("zlo")
    block_ids = token_pos.reshape(64, BLK)[:, 0] // BLK
    by_place = block_ids.reshape(16, 4)
    query_pos = lax.dynamic_index_in_dim(by_place, zlo, 1, keepdims=False)
    mine = lax.dynamic_index_in_dim(block_ids.reshape(4, 2, 2, 4), yh, 1, keepdims=False)
    key_pos = jnp.concatenate(
        [
            lax.dynamic_index_in_dim(mine, (zlo + step) % 4, 2, keepdims=False).reshape(8)
            for step in STEPS
        ]
    )
    span = jnp.arange(64, dtype=jnp.int32)
    pick_query = (query_pos[:, None] == span[None, :]).astype(BF16)
    pick_key = (key_pos[:, None] == span[None, :]).astype(BF16)
    seen = jnp.dot(
        jnp.dot(pick_query, (block_mask == 1).astype(BF16), preferred_element_type=F32).astype(BF16),
        pick_key.T,
        preferred_element_type=F32,
    )
    active = (seen > 0.5) & (key_pos[None, :] <= query_pos[:, None])
    same = key_pos[None, :] == query_pos[:, None]

    def packed(first, many):
        seen = active[:, first : first + many]
        number = jnp.arange(many, dtype=jnp.int32)
        ones = seen.astype(jnp.int32)
        before = jnp.sum(
            jnp.where(number[None, None, :] < number[None, :, None], ones[:, None, :], 0), axis=2
        )
        count = jnp.sum(ones, axis=1)
        code = number[None, :] + 32 * same[:, first : first + many].astype(jnp.int32)
        place = seen[:, None, :] & (before[:, None, :] == number[None, :, None])
        lists = jnp.sum(jnp.where(place, code[:, None, :], 0), axis=2)
        lists = jnp.where(number[None, :] < count[:, None], lists, 64)
        lists = jnp.concatenate([lists.reshape(16 * many), jnp.full((32,), 64, jnp.int32)])
        return lists, count

    return packed(0, OWN), packed(OWN, REST)


def local(
    queries,
    key_head_rows,
    value_head_rows,
    output_gradient,
    support_values,
    thresholds,
    gate_row_sums,
    token_pos,
    block_mask,
):
    shape = jax.ShapeDtypeStruct

    def by_head(stat):
        return stat.astype(F32).T.reshape(KEY_HEADS, GROUP * ROWS)

    place = jnp.stack([lax.axis_index(name) for name in ("core", "zhi")]).astype(jnp.int32)
    message = (ROWS, HEAD_WIDTH)
    send_keys = vmem_call(pack_keys_kernel, shape((KEY_HEADS, 2, *message), BF16), [WHOLE] * 2)(
        key_head_rows, value_head_rows
    )
    pieces = exchange(send_keys, HEAD_AXES)
    send = vmem_call(pack_queries_kernel, shape((16, SLOTS, *message), BF16), [WHOLE] * 5)(
        queries,
        output_gradient,
        support_values,
        by_head(thresholds),
        by_head(gate_row_sums),
    )
    send, pieces = lax.optimization_barrier((send, pieces))
    others = [along_z(pieces, -step * QUARTER) for step in STEPS[1:]]
    arrived = exchange(send, PLANE)
    arrived, *others = lax.optimization_barrier((arrived, *others))
    own = jnp.stack([pieces, *others], axis=1)
    near = [
        along_z(own, -1),
        along_z(own, 1),
        along_z(own[:4], -2),
        along_z(own[4:], 2),
    ]
    arrived_other = lax.ppermute(arrived, "core", [(0, 1), (1, 0)])
    own_lists, rest_lists = active_lists(token_pos, block_mask)

    def part(many):
        return shape((many, 4, 2, *message), BF16)

    piece = (PIECE, HEAD_WIDTH)
    query_shape = (16, 256, HEAD_WIDTH)
    dqt_shape = (16, HEAD_WIDTH, 256)

    def key_scratch(many):
        return [VMEM((many, *piece), BF16)] * 2, [VMEM((many, *piece), F32)] * 2

    inputs, sums = key_scratch(OWN)
    grad_own, *state = vmem_call(
        own_kernel,
        [
            part(8),
            shape(dqt_shape, F32),
            shape(query_shape, BF16),
            shape(query_shape, BF16),
            shape((16, 8, 256), F32),
        ],
        [SCALARS] * 3 + [WHOLE] * 3,
        scratch_shapes=[
            *inputs,
            VMEM((3, PIECE, 256), F32),
            *sums,
            pltpu.SMEM((64,), jnp.int32),
        ],
        cost_estimate=pl.CostEstimate(
            flops=4_000_000_000, bytes_accessed=8 << 20, transcendentals=0
        ),
    )(*own_lists, place, arrived, arrived_other, own)
    inputs, sums = key_scratch(REST)
    grad_query, *grad_near = vmem_call(
        rest_kernel,
        [shape((16, 2, GROUP * ROWS, HEAD_WIDTH), BF16)] + [part(m) for m in (8, 8, 4, 4)],
        [SCALARS] * 3 + [WHOLE] * 8,
        scratch_shapes=[
            *inputs,
            *sums,
            VMEM(dqt_shape, F32),
            pltpu.SMEM((64,), jnp.int32),
        ],
    )(*rest_lists, place, *state, *near)

    back = [
        along_z(grad, step) for grad, step in zip(grad_near, (1, -1, 2, -2), strict=True)
    ]
    back_query = exchange(
        grad_query.reshape(32, GROUP * ROWS, HEAD_WIDTH), PLANE + ("core",)
    )
    query_out = vmem_call(
        sum_queries_kernel, shape((ROWS, QUERY_HEADS * HEAD_WIDTH), BF16), [WHOLE]
    )(back_query)
    total = vmem_call(total_kernel, part(8), [SCALARS] + [WHOLE] * 5)(place, grad_own, *back)
    back_keys = exchange(total.reshape(32, 2, *message), KEY_AXES)
    key_shape = shape((ROWS, KEY_HEADS * HEAD_WIDTH), BF16)
    key_out, value_out = vmem_call(sum_keys_kernel, [key_shape, key_shape], [WHOLE])(back_keys)
    return query_out, key_out, value_out


def solution(mesh):
    parts = Mesh(
        mesh.devices.reshape(4, 2, 4, 2, 2, 4), ("zhi", "core", "x", "yh", "yl", "zlo")
    )
    rows = P(TOKEN_AXES, None)
    return jax.shard_map(
        local,
        mesh=parts,
        in_specs=(rows,) * 7 + (P(), P()),
        out_specs=(rows,) * 3,
        check_vma=False,
    )
```

time: 156 us -> 164 us (1.051)
  waiting for transfers between devices: 52 us -> 34.3 us
  starting transfers between devices: 70.8 us -> 87.5 us
  Pallas kernels: 22.5 us -> 28.6 us
    ppermute x8 -> x11, starting transfers between devices: 28.6 us -> 51.6 us  [along_z(): return lax.ppermute(value, ('zhi', 'zlo'), pairs)]
    all_to_all x4, waiting for transfers between devices: 40.1 us -> 20.3 us  [exchange(): return lax.all_to_all(value, axes, split_axis=0, concat_axis=0, tiled=True)]
    all_to_all x4, starting transfers between devices: 40.3 us -> 34 us  [exchange(): return lax.all_to_all(value, axes, split_axis=0, concat_axis=0, tiled=True)]
    pallas_call x3 -> x4, Pallas kernels: 19.7 us -> 25.8 us  [the longest x1 16.5 us: local(): vmem_call(rest_kernel, [shape((16, 2, GROUP * ROWS, HEAD_WIDTH), BF16)] +...]
    ppermute x8 -> x11, waiting for transfers between devices: 10.6 us -> 14 us  [along_z(): return lax.ppermute(value, ('zhi', 'zlo'), pairs)]
    unnamed x30 -> x10, local copies, waits for them, and re-layouts: 4.31 us -> 4.36 us
  transfers between devices with their start and end apart: 13 -> 16, of which waited for: 7 -> 4; matrix products, arithmetic and copies ran while one was open for 3% -> 4% of each run, Pallas kernels for 2% -> 7%
where the time goes in v4:
time: 164 us; the launch traced here: 163 us
  starting transfers between devices  87.5 us (53%)
  waiting for transfers between devices  34.3 us (21%)
  Pallas kernels  28.6 us (17%)
  local copies, waits for them, and re-layouts  6.99 us (4%)
  other arithmetic  3.23 us (2%)
    ppermute x11, starting transfers between devices, along_z(): return lax.ppermute(value, ('zhi', 'zlo'), pairs)  51.6 us
    all_to_all x4, starting transfers between devices, exchange(): return lax.all_to_all(value, axes, split_axis=0, concat_axis=0, tiled=True)  34 us
    all_to_all x4, waiting for transfers between devices, exchange(): return lax.all_to_all(value, axes, split_axis=0, concat_axis=0, tiled=True)  20.3 us
    pallas_call x1, Pallas kernels, local(): vmem_call(rest_kernel, [shape((16, 2, GROUP * ROWS, HEAD_WIDTH), BF16)] +...  16.5 us
    ppermute x11, waiting for transfers between devices, along_z(): return lax.ppermute(value, ('zhi', 'zlo'), pairs)  14 us
    pallas_call x1, Pallas kernels, local(): vmem_call(own_kernel, [part(8), shape(dqt_shape, F32), shape(query_shape,...  7.3 us
    unnamed x10, local copies, waits for them, and re-layouts  4.36 us
  transfers between devices with their start and end apart: 16, of which 4 were waited for; matrix products, arithmetic and copies ran while one was open for 4% of the time, Pallas kernels for 7%

profile of v4, /device:TPU:64, one launch (start us, length us, event | category | flops | bytes accessed | tf_op | source)
XLA Modules:
  0.0 162.6 jit_solution(5637689921502337243)
XLA Ops:
  0.6 0.7 copy-done.3
  1.4 0.8 copy-done.4
  2.1 0.6 shard_map.113
  2.8 5.3 %all-to-all-start = ((bf16[8,2,16,128]{3,2,1,0:T(8,128)(2,1)}), bf16[8,2,16,128]{3,2,1,0:T(8,128)(2,1)S(1)}, u32[]{:S(2)}, u32[]{:S(2)}) async-start(bf16[8,2,16,128]{3,2,1,0:T(8,128)(2,1)} %shard_map.113), calls=%async_computation | async-start | bytes 131072 | tf_op jit(solution)/shard_map/all_to_all | solution.py:287
  8.1 0.9 slice_reduce_fusion
  9.0 0.1 squeeze.15
  9.1 0.1 squeeze.14
  9.3 0.4 dynamic-slice_reduce_fusion.3
  9.7 0.1 reshape.110
  9.8 0.1 reshape.111
  9.9 0.1 reshape.112
  9.9 0.1 reshape.113
  10.0 0.2 fusion.8
  10.2 0.1 pad_add_fusion
  10.3 0.1 broadcast_compare_fusion
  10.4 1.1 fusion
  11.4 0.7 convert_bitcast_fusion.1
  12.1 0.7 convert_bitcast_fusion
  12.8 0.1 copy.31
  12.9 0.1 reshape.121.thr_ref
  13.0 0.1 copy.32
  13.1 0.1 reshape.123.sums_ref
  13.2 1.0 copy-done
  14.1 0.9 copy-done.1
  15.1 0.9 copy-done.2
  16.0 1.2 shard_map.112
  17.3 7.2 %all-to-all-start.1 = ((bf16[16,17,16,128]{3,2,1,0:T(8,128)(2,1)}), bf16[16,17,16,128]{3,2,1,0:T(8,128)(2,1)S(1)}, u32[]{:S(2)}, u32[]{:S(2)}) async-start(bf16[16,17,16,128]{3,2,1,0:T(8,128)(2,1)} %shard_map.112), calls=%async_computation.1 | async-start | bytes 2228224 | tf_op jit(solution)/shard_map/all_to_all | solution.py:287
  24.5 0.1 copy.28
  24.6 0.1 copy.27
  24.7 0.1 convert_reduce_fusion.count_ref
  24.9 0.1 select_reduce_fusion.3
  25.0 0.1 copy.30
  25.1 0.1 select_n.115
  25.2 0.1 fusion.20
  25.3 10.9 %collective-permute-start = (bf16[8,2,16,128]{3,2,1,0:T(8,128)(2,1)S(1)}, bf16[8,2,16,128]{3,2,1,0:T(8,128)(2,1)S(1)}, u32[]{:S(2)}, u32[]{:S(2)}) collective-permute-start(bf16[8,2,16,128]{3,2,1,0:T(8,128)(2,1)S(1)} %all-to-all-done), channel_id=1, source_target_pairs={{0,384},{1,385},{2,386},{3,387},{128,0},{129,1},{130,2},{131,3},{2... | collective-permute-start | bytes 196616 | tf_op jit(solution)/shard_map/ppermute | solution.py:292
  36.2 1.9 %collective-permute-start.1 = (bf16[8,2,16,128]{3,2,1,0:T(8,128)(2,1)S(1)}, bf16[8,2,16,128]{3,2,1,0:T(8,128)(2,1)S(1)}, u32[]{:S(2)}, u32[]{:S(2)}) collective-permute-start(bf16[8,2,16,128]{3,2,1,0:T(8,128)(2,1)S(1)} %all-to-all-done), channel_id=1, source_target_pairs={{0,128},{1,129},{2,130},{3,131},{128,256},{129,257},{130,258},{131... | collective-permute-start | bytes 196616 | tf_op jit(solution)/shard_map/ppermute | solution.py:292
  38.1 10.8 %collective-permute-start.2 = (bf16[8,2,16,128]{3,2,1,0:T(8,128)(2,1)S(1)}, bf16[8,2,16,128]{3,2,1,0:T(8,128)(2,1)S(1)}, u32[]{:S(2)}, u32[]{:S(2)}) collective-permute-start(bf16[8,2,16,128]{3,2,1,0:T(8,128)(2,1)S(1)} %all-to-all-done), channel_id=1, source_target_pairs={{0,256},{1,257},{2,258},{3,259},{128,384},{129,385},{130,386},{131... | collective-permute-start | bytes 196616 | tf_op jit(solution)/shard_map/ppermute | solution.py:292
  48.9 0.3 select_reduce_fusion.1
  49.3 5.4 %collective-permute-done.2 = bf16[8,2,16,128]{3,2,1,0:T(8,128)(2,1)S(1)} collective-permute-done((bf16[8,2,16,128]{3,2,1,0:T(8,128)(2,1)S(1)}, bf16[8,2,16,128]{3,2,1,0:T(8,128)(2,1)S(1)}, u32[]{:S(2)}, u32[]{:S(2)}) %collective-permute-start.2) | collective-permute-done | bytes 65568 | tf_op jit(solution)/shard_map/ppermute | solution.py:292
  54.7 1.9 %collective-permute-start.3 = (bf16[16,17,16,128]{3,2,1,0:T(8,128)(2,1)S(1)}, bf16[16,17,16,128]{3,2,1,0:T(8,128)(2,1)S(1)}, u32[]{:S(2)}, u32[]{:S(2)}) collective-permute-start(bf16[16,17,16,128]{3,2,1,0:T(8,128)(2,1)S(1)} %all-to-all-done.1.qa_ref), channel_id=1, source_target_pairs={{0,64},{64,0},{1,65},{65,1},{2,66},{66,2},{3,67},{67,3},{4,68},{68... | collective-permute-start | bytes 3342344 | tf_op jit(solution)/shard_map/ppermute | solution.py:376
  56.6 0.2 convert_reduce_fusion.1.count_ref
  56.8 0.1 select_add_fusion.1
  56.9 0.3 select_reduce_fusion
  57.2 0.1 fusion.11
  57.3 0.1 select_n.111
  57.4 0.1 pad_add_fusion.1.place_ref
  57.6 1.9 %collective-permute-start.4 = (bf16[8,4,2,16,128]{4,3,2,1,0:T(8,128)(2,1)S(1)}, bf16[8,4,2,16,128]{4,3,2,1,0:T(8,128)(2,1)S(1)}, u32[]{:S(2)}, u32[]{:S(2)}) collective-permute-start(bf16[8,4,2,16,128]{4,3,2,1,0:T(8,128)(2,1)S(1)} %pad_maximum_fusion.own_ref), channel_id=1, source_target_pairs={{0,387},{1,0},{2,1},{3,2},{128,3},{129,128},{130,129},{131,130},{2... | collective-permute-start | bytes 786440 | tf_op jit(solution)/shard_map/ppermute | solution.py:292
  59.5 3.9 %collective-permute-start.5 = (bf16[8,4,2,16,128]{4,3,2,1,0:T(8,128)(2,1)S(1)}, bf16[8,4,2,16,128]{4,3,2,1,0:T(8,128)(2,1)S(1)}, u32[]{:S(2)}, u32[]{:S(2)}) collective-permute-start(bf16[8,4,2,16,128]{4,3,2,1,0:T(8,128)(2,1)S(1)} %pad_maximum_fusion.own_ref), channel_id=1, source_target_pairs={{0,1},{1,2},{2,3},{3,128},{128,129},{129,130},{130,131},{131,256},... | collective-permute-start | bytes 786440 | tf_op jit(solution)/shard_map/ppermute | solution.py:292
  63.4 4.9 %collective-permute-start.6 = (bf16[4,4,2,16,128]{4,3,2,1,0:T(8,128)(2,1)S(1)}, bf16[4,4,2,16,128]{4,3,2,1,0:T(8,128)(2,1)S(1)}, u32[]{:S(2)}, u32[]{:S(2)}) collective-permute-start(bf16[4,4,2,16,128]{4,3,2,1,0:T(8,128)(2,1)S(1)} %get-tuple-element.44), channel_id=1, source_target_pairs={{0,386},{1,387},{2,0},{3,1},{128,2},{129,3},{130,128},{131,129},{2... | collective-permute-start | bytes 393224 | tf_op jit(solution)/shard_map/ppermute | solution.py:292
  68.4 3.0 %collective-permute-start.7 = (bf16[4,4,2,16,128]{4,3,2,1,0:T(8,128)(2,1)S(1)}, bf16[4,4,2,16,128]{4,3,2,1,0:T(8,128)(2,1)S(1)}, u32[]{:S(2)}, u32[]{:S(2)}) collective-permute-start(bf16[4,4,2,16,128]{4,3,2,1,0:T(8,128)(2,1)S(1)} %get-tuple-element.43), channel_id=1, source_target_pairs={{0,2},{1,3},{2,128},{3,129},{128,130},{129,131},{130,256},{131,257... | collective-permute-start | bytes 393224 | tf_op jit(solution)/shard_map/ppermute | solution.py:292
  71.4 7.3 %shard_map.114 = (bf16[8,4,2,16,128]{4,3,2,1,0:T(8,128)(2,1)S(1)}, f32[16,128,256]{2,1,0:T(8,128)S(1)}, bf16[16,256,128]{2,1,0:T(8,128)(2,1)S(1)}, bf16[16,256,128]{2,1,0:T(8,128)(2,1)S(1)}, f32[16,8,256]{2,1,0:T(8,128)S(1)}) custom-call(s32[160]{0:T(256)S(1)} %concatenate.11.list_ref, s32[16]{0:T(128)S(1)} %convert_reduce_fusion.count_ref, ...), custom_call_target="tpu_custom_call" | custom-call | flops 4000000000 | bytes 8388608 | tf_op jit(solution)/shard_map/pallas_call | solution.py:390
  78.8 16.5 %shard_map.115 = (bf16[16,2,128,128]{3,2,1,0:T(8,128)(2,1)}, bf16[8,4,2,16,128]{4,3,2,1,0:T(8,128)(2,1)S(1)}, bf16[8,4,2,16,128]{4,3,2,1,0:T(8,128)(2,1)S(1)}, b...) custom-call(s32[416]{0:T(512)S(1)} %concatenate.10.list_ref, s32[16]{0:T(128)S(1)} %convert_reduce_fusion.1.count_ref, ...), custom_call_target="tpu_custom_call" | custom-call | tf_op jit(solution)/shard_map/pallas_call | solution.py:411
  95.3 8.5 %all-to-all-start.2 = ((bf16[32,128,128]{2,1,0:T(8,128)(2,1)}), bf16[32,128,128]{2,1,0:T(8,128)(2,1)S(1)}, u32[]{:S(2)}, u32[]{:S(2)}) async-start(bf16[32,128,128]{2,1,0:T(8,128)(2,1)} %bitcast.12), calls=%async_computation.2 | async-start | bytes 2097152 | tf_op jit(solution)/shard_map/all_to_all | solution.py:287
  103.8 4.3 %collective-permute-start.8 = (bf16[8,4,2,16,128]{4,3,2,1,0:T(8,128)(2,1)S(1)}, bf16[8,4,2,16,128]{4,3,2,1,0:T(8,128)(2,1)S(1)}, u32[]{:S(2)}, u32[]{:S(2)}) collective-permute-start(bf16[8,4,2,16,128]{4,3,2,1,0:T(8,128)(2,1)S(1)} %get-tuple-element.33), channel_id=1, source_target_pairs={{0,1},{1,2},{2,3},{3,128},{128,129},{129,130},{130,131},{131,256},... | collective-permute-start | bytes 786440 | tf_op jit(solution)/shard_map/ppermute | solution.py:292
  108.0 1.9 %collective-permute-start.9 = (bf16[8,4,2,16,128]{4,3,2,1,0:T(8,128)(2,1)S(1)}, bf16[8,4,2,16,128]{4,3,2,1,0:T(8,128)(2,1)S(1)}, u32[]{:S(2)}, u32[]{:S(2)}) collective-permute-start(bf16[8,4,2,16,128]{4,3,2,1,0:T(8,128)(2,1)S(1)} %get-tuple-element.34), channel_id=1, source_target_pairs={{0,387},{1,0},{2,1},{3,2},{128,3},{129,128},{130,129},{131,130},{2... | collective-permute-start | bytes 786440 | tf_op jit(solution)/shard_map/ppermute | solution.py:292
  110.0 4.6 %collective-permute-start.10 = (bf16[4,4,2,16,128]{4,3,2,1,0:T(8,128)(2,1)S(1)}, bf16[4,4,2,16,128]{4,3,2,1,0:T(8,128)(2,1)S(1)}, u32[]{:S(2)}, u32[]{:S(2)}) collective-permute-start(bf16[4,4,2,16,128]{4,3,2,1,0:T(8,128)(2,1)S(1)} %get-tuple-element.35), channel_id=1, source_target_pairs={{0,2},{1,3},{2,128},{3,129},{128,130},{129,131},{130,256},{131,257... | collective-permute-start | bytes 393224 | tf_op jit(solution)/shard_map/ppermute | solution.py:292
  114.6 3.3 %collective-permute-start.11 = (bf16[4,4,2,16,128]{4,3,2,1,0:T(8,128)(2,1)S(1)}, bf16[4,4,2,16,128]{4,3,2,1,0:T(8,128)(2,1)S(1)}, u32[]{:S(2)}, u32[]{:S(2)}) collective-permute-start(bf16[4,4,2,16,128]{4,3,2,1,0:T(8,128)(2,1)S(1)} %get-tuple-element.36), channel_id=1, source_target_pairs={{0,386},{1,387},{2,0},{3,1},{128,2},{129,3},{130,128},{131,129},{2... | collective-permute-start | bytes 393224 | tf_op jit(solution)/shard_map/ppermute | solution.py:292
  117.9 4.6 %collective-permute-done.10.far_a_ref = bf16[4,4,2,16,128]{4,3,2,1,0:T(8,128)(2,1)S(1)} collective-permute-done((bf16[4,4,2,16,128]{4,3,2,1,0:T(8,128)(2,1)S(1)}, bf16[4,4,2,16,128]{4,3,2,1,0:T(8,128)(2,1)S(1)}, u32[]{:S(2)}, u32[]{:S(2)}) %collective-permute-start.10) | collective-permute-done | bytes 131104 | tf_op jit(solution)/shard_map/ppermute | solution.py:292
  122.5 4.0 %collective-permute-done.11.far_b_ref = bf16[4,4,2,16,128]{4,3,2,1,0:T(8,128)(2,1)S(1)} collective-permute-done((bf16[4,4,2,16,128]{4,3,2,1,0:T(8,128)(2,1)S(1)}, bf16[4,4,2,16,128]{4,3,2,1,0:T(8,128)(2,1)S(1)}, u32[]{:S(2)}, u32[]{:S(2)}) %collective-permute-start.11) | collective-permute-done | bytes 131104 | tf_op jit(solution)/shard_map/ppermute | solution.py:292
  126.5 1.4 shard_map.117
  127.9 13.0 %all-to-all-start.3 = ((bf16[32,2,16,128]{3,2,1,0:T(8,128)(2,1)}), bf16[32,2,16,128]{3,2,1,0:T(8,128)(2,1)S(1)}, u32[]{:S(2)}, u32[]{:S(2)}) async-start(bf16[32,2,16,128]{3,2,1,0:T(8,128)(2,1)} %bitcast.13), calls=%async_computation.3 | async-start | bytes 524288 | tf_op jit(solution)/shard_map/all_to_all | solution.py:287
  140.9 0.8 shard_map.116
  141.7 20.2 %all-to-all-done.3.in_ref = bf16[32,2,16,128]{3,2,1,0:T(8,128)(2,1)S(1)} async-done(((bf16[32,2,16,128]{3,2,1,0:T(8,128)(2,1)}), bf16[32,2,16,128]{3,2,1,0:T(8,128)(2,1)S(1)}, u32[]{:S(2)}, u32[]{:S(2)}) %all-to-all-start.3) | async-done | bytes 262176 | tf_op jit(solution)/shard_map/all_to_all | solution.py:287
  161.9 0.7 shard_map.118
  (31 shorter events, 0.3 us)
Async XLA Ops:
  0.6 0.8 copy-start.3
  1.4 0.8 copy-start.4
  2.8 14.5 %all-to-all-start = ((bf16[8,2,16,128]{3,2,1,0:T(8,128)(2,1)}), bf16[8,2,16,128]{3,2,1,0:T(8,128)(2,1)S(1)}, u32[]{:S(2)}, u32[]{:S(2)}) async-start(bf16[8,2,16,128]{3,2,1,0:T(8,128)(2,1)} %shard_map.113), calls=%async_computation | async-start | bytes 131072 | tf_op jit(solution)/shard_map/all_to_all | solution.py:287
  13.2 1.0 copy-start
  14.1 0.9 copy-start.1
  15.1 0.9 copy-start.2
  17.3 37.5 %all-to-all-start.1 = ((bf16[16,17,16,128]{3,2,1,0:T(8,128)(2,1)}), bf16[16,17,16,128]{3,2,1,0:T(8,128)(2,1)S(1)}, u32[]{:S(2)}, u32[]{:S(2)}) async-start(bf16[16,17,16,128]{3,2,1,0:T(8,128)(2,1)} %shard_map.112), calls=%async_computation.1 | async-start | bytes 2228224 | tf_op jit(solution)/shard_map/all_to_all | solution.py:287
  25.3 24.0 %collective-permute-start = (bf16[8,2,16,128]{3,2,1,0:T(8,128)(2,1)S(1)}, bf16[8,2,16,128]{3,2,1,0:T(8,128)(2,1)S(1)}, u32[]{:S(2)}, u32[]{:S(2)}) collective-permute-start(bf16[8,2,16,128]{3,2,1,0:T(8,128)(2,1)S(1)} %all-to-all-done), channel_id=1, source_target_pairs={{0,384},{1,385},{2,386},{3,387},{128,0},{129,1},{130,2},{131,3},{2... | collective-permute-start | bytes 196616 | tf_op jit(solution)/shard_map/ppermute | solution.py:292
  36.2 13.1 %collective-permute-start.1 = (bf16[8,2,16,128]{3,2,1,0:T(8,128)(2,1)S(1)}, bf16[8,2,16,128]{3,2,1,0:T(8,128)(2,1)S(1)}, u32[]{:S(2)}, u32[]{:S(2)}) collective-permute-start(bf16[8,2,16,128]{3,2,1,0:T(8,128)(2,1)S(1)} %all-to-all-done), channel_id=1, source_target_pairs={{0,128},{1,129},{2,130},{3,131},{128,256},{129,257},{130,258},{131... | collective-permute-start | bytes 196616 | tf_op jit(solution)/shard_map/ppermute | solution.py:292
  38.1 16.6 %collective-permute-start.2 = (bf16[8,2,16,128]{3,2,1,0:T(8,128)(2,1)S(1)}, bf16[8,2,16,128]{3,2,1,0:T(8,128)(2,1)S(1)}, u32[]{:S(2)}, u32[]{:S(2)}) collective-permute-start(bf16[8,2,16,128]{3,2,1,0:T(8,128)(2,1)S(1)} %all-to-all-done), channel_id=1, source_target_pairs={{0,256},{1,257},{2,258},{3,259},{128,384},{129,385},{130,386},{131... | collective-permute-start | bytes 196616 | tf_op jit(solution)/shard_map/ppermute | solution.py:292
  54.7 16.7 %collective-permute-start.3 = (bf16[16,17,16,128]{3,2,1,0:T(8,128)(2,1)S(1)}, bf16[16,17,16,128]{3,2,1,0:T(8,128)(2,1)S(1)}, u32[]{:S(2)}, u32[]{:S(2)}) collective-permute-start(bf16[16,17,16,128]{3,2,1,0:T(8,128)(2,1)S(1)} %all-to-all-done.1.qa_ref), channel_id=1, source_target_pairs={{0,64},{64,0},{1,65},{65,1},{2,66},{66,2},{3,67},{67,3},{4,68},{68... | collective-permute-start | bytes 3342344 | tf_op jit(solution)/shard_map/ppermute | solution.py:376
  57.6 21.2 %collective-permute-start.4 = (bf16[8,4,2,16,128]{4,3,2,1,0:T(8,128)(2,1)S(1)}, bf16[8,4,2,16,128]{4,3,2,1,0:T(8,128)(2,1)S(1)}, u32[]{:S(2)}, u32[]{:S(2)}) collective-permute-start(bf16[8,4,2,16,128]{4,3,2,1,0:T(8,128)(2,1)S(1)} %pad_maximum_fusion.own_ref), channel_id=1, source_target_pairs={{0,387},{1,0},{2,1},{3,2},{128,3},{129,128},{130,129},{131,130},{2... | collective-permute-start | bytes 786440 | tf_op jit(solution)/shard_map/ppermute | solution.py:292
  59.5 19.3 %collective-permute-start.5 = (bf16[8,4,2,16,128]{4,3,2,1,0:T(8,128)(2,1)S(1)}, bf16[8,4,2,16,128]{4,3,2,1,0:T(8,128)(2,1)S(1)}, u32[]{:S(2)}, u32[]{:S(2)}) collective-permute-start(bf16[8,4,2,16,128]{4,3,2,1,0:T(8,128)(2,1)S(1)} %pad_maximum_fusion.own_ref), channel_id=1, source_target_pairs={{0,1},{1,2},{2,3},{3,128},{128,129},{129,130},{130,131},{131,256},... | collective-permute-start | bytes 786440 | tf_op jit(solution)/shard_map/ppermute | solution.py:292
  63.4 15.3 %collective-permute-start.6 = (bf16[4,4,2,16,128]{4,3,2,1,0:T(8,128)(2,1)S(1)}, bf16[4,4,2,16,128]{4,3,2,1,0:T(8,128)(2,1)S(1)}, u32[]{:S(2)}, u32[]{:S(2)}) collective-permute-start(bf16[4,4,2,16,128]{4,3,2,1,0:T(8,128)(2,1)S(1)} %get-tuple-element.44), channel_id=1, source_target_pairs={{0,386},{1,387},{2,0},{3,1},{128,2},{129,3},{130,128},{131,129},{2... | collective-permute-start | bytes 393224 | tf_op jit(solution)/shard_map/ppermute | solution.py:292
  68.4 10.4 %collective-permute-start.7 = (bf16[4,4,2,16,128]{4,3,2,1,0:T(8,128)(2,1)S(1)}, bf16[4,4,2,16,128]{4,3,2,1,0:T(8,128)(2,1)S(1)}, u32[]{:S(2)}, u32[]{:S(2)}) collective-permute-start(bf16[4,4,2,16,128]{4,3,2,1,0:T(8,128)(2,1)S(1)} %get-tuple-element.43), channel_id=1, source_target_pairs={{0,2},{1,3},{2,128},{3,129},{128,130},{129,131},{130,256},{131,257... | collective-permute-start | bytes 393224 | tf_op jit(solution)/shard_map/ppermute | solution.py:292
  95.3 32.6 %all-to-all-start.2 = ((bf16[32,128,128]{2,1,0:T(8,128)(2,1)}), bf16[32,128,128]{2,1,0:T(8,128)(2,1)S(1)}, u32[]{:S(2)}, u32[]{:S(2)}) async-start(bf16[32,128,128]{2,1,0:T(8,128)(2,1)} %bitcast.12), calls=%async_computation.2 | async-start | bytes 2097152 | tf_op jit(solution)/shard_map/all_to_all | solution.py:287
  103.8 22.7 %collective-permute-start.8 = (bf16[8,4,2,16,128]{4,3,2,1,0:T(8,128)(2,1)S(1)}, bf16[8,4,2,16,128]{4,3,2,1,0:T(8,128)(2,1)S(1)}, u32[]{:S(2)}, u32[]{:S(2)}) collective-permute-start(bf16[8,4,2,16,128]{4,3,2,1,0:T(8,128)(2,1)S(1)} %get-tuple-element.33), channel_id=1, source_target_pairs={{0,1},{1,2},{2,3},{3,128},{128,129},{129,130},{130,131},{131,256},... | collective-permute-start | bytes 786440 | tf_op jit(solution)/shard_map/ppermute | solution.py:292
  108.0 18.5 %collective-permute-start.9 = (bf16[8,4,2,16,128]{4,3,2,1,0:T(8,128)(2,1)S(1)}, bf16[8,4,2,16,128]{4,3,2,1,0:T(8,128)(2,1)S(1)}, u32[]{:S(2)}, u32[]{:S(2)}) collective-permute-start(bf16[8,4,2,16,128]{4,3,2,1,0:T(8,128)(2,1)S(1)} %get-tuple-element.34), channel_id=1, source_target_pairs={{0,387},{1,0},{2,1},{3,2},{128,3},{129,128},{130,129},{131,130},{2... | collective-permute-start | bytes 786440 | tf_op jit(solution)/shard_map/ppermute | solution.py:292
  110.0 12.5 %collective-permute-start.10 = (bf16[4,4,2,16,128]{4,3,2,1,0:T(8,128)(2,1)S(1)}, bf16[4,4,2,16,128]{4,3,2,1,0:T(8,128)(2,1)S(1)}, u32[]{:S(2)}, u32[]{:S(2)}) collective-permute-start(bf16[4,4,2,16,128]{4,3,2,1,0:T(8,128)(2,1)S(1)} %get-tuple-element.35), channel_id=1, source_target_pairs={{0,2},{1,3},{2,128},{3,129},{128,130},{129,131},{130,256},{131,257... | collective-permute-start | bytes 393224 | tf_op jit(solution)/shard_map/ppermute | solution.py:292
  114.6 11.9 %collective-permute-start.11 = (bf16[4,4,2,16,128]{4,3,2,1,0:T(8,128)(2,1)S(1)}, bf16[4,4,2,16,128]{4,3,2,1,0:T(8,128)(2,1)S(1)}, u32[]{:S(2)}, u32[]{:S(2)}) collective-permute-start(bf16[4,4,2,16,128]{4,3,2,1,0:T(8,128)(2,1)S(1)} %get-tuple-element.36), channel_id=1, source_target_pairs={{0,386},{1,387},{2,0},{3,1},{128,2},{129,3},{130,128},{131,129},{2... | collective-permute-start | bytes 393224 | tf_op jit(solution)/shard_map/ppermute | solution.py:292
  127.9 34.0 %all-to-all-start.3 = ((bf16[32,2,16,128]{3,2,1,0:T(8,128)(2,1)}), bf16[32,2,16,128]{3,2,1,0:T(8,128)(2,1)S(1)}, u32[]{:S(2)}, u32[]{:S(2)}) async-start(bf16[32,2,16,128]{3,2,1,0:T(8,128)(2,1)} %bitcast.13), calls=%async_computation.3 | async-start | bytes 524288 | tf_op jit(solution)/shard_map/all_to_all | solution.py:287

commit v5 on v3

--- a/solution.py
+++ b/solution.py
@@ -28,13 +28,13 @@
 BF16 = jnp.bfloat16
 
 
-def vmem_call(kernel, out_shape, ins, **kw):
+def vmem_call(kernel, out_shape, ins, mib=20, **kw):
     return pl.pallas_call(
         kernel,
         out_shape=out_shape,
         in_specs=ins,
         out_specs=jax.tree.map(lambda _: pl.BlockSpec(memory_space=VMEM), out_shape),
-        compiler_params=pltpu.CompilerParams(vmem_limit_bytes=48 << 20),
+        compiler_params=pltpu.CompilerParams(vmem_limit_bytes=mib << 20),
         **kw,
     )
 
@@ -98,8 +98,6 @@
     dk_s,
     dv_s,
     dqt_s,
-    q_s,
-    do_s,
     stat_s,
     work_s,
 ):
@@ -124,13 +122,9 @@
     bias_s[2] = jnp.full((PIECE, 256), FAR, F32)
 
     def prepare(j, total):
-        pair = (qa_ref, qb_ref)
-        tile = (GROUP * ROWS, HEAD_WIDTH)
-        q_s[j] = jnp.concatenate([ref[j, :GROUP].reshape(tile) for ref in pair], axis=0)
-        do_s[j] = jnp.concatenate(
-            [ref[j, GROUP : 2 * GROUP].reshape(tile) for ref in pair], axis=0
+        stats = jnp.concatenate(
+            [ref[j, 2 * GROUP].astype(F32) for ref in (qa_ref, qb_ref)], axis=1
         )
-        stats = jnp.concatenate([ref[j, 2 * GROUP].astype(F32) for ref in pair], axis=1)
         stat_s[j, 0:1] = stats[0:1]
         stat_s[j, 1:2] = stats[1:2] + stats[2:3]
 
@@ -147,6 +141,15 @@
     def contract(a, b, a_dim, b_dim):
         return lax.dot_general(
             a, b, (((a_dim,), (b_dim,)), ((), ())), preferred_element_type=F32
+        )
+
+    def rows(j, first):
+        return jnp.concatenate(
+            [
+                ref[j, first : first + GROUP].reshape(GROUP * ROWS, HEAD_WIDTH)
+                for ref in (qa_ref, qb_ref)
+            ],
+            axis=0,
         )
 
     def one_step(step, _):
@@ -159,7 +162,7 @@
             keys = jnp.concatenate([k_s[i] for i in ids], axis=0)
             values = jnp.concatenate([v_s[i] for i in ids], axis=0)
             bias = jnp.concatenate([bias_s[entry >> 5] for entry in entries], axis=0)
-            query, grad = q_s[j], do_s[j]
+            query, grad = rows(j, 0), rows(j, GROUP)
             scores = contract(keys, query, 1, 1)
             dprob = contract(values, grad, 1, 1)
             gate = jnp.maximum(scores * (0.5 * SCALE) - stat_s[j, 0:1] - bias, 0.0)
@@ -284,7 +287,7 @@
 
     place = jnp.stack([lax.axis_index(name) for name in ("core", "zhi")]).astype(jnp.int32)
     message = (ROWS, HEAD_WIDTH)
-    send_keys = vmem_call(pack_keys_kernel, shape((32, 2, *message), BF16), [WHOLE] * 2)(
+    send_keys = vmem_call(pack_keys_kernel, shape((32, 2, *message), BF16), [WHOLE] * 2, 60)(
         key_head_rows, value_head_rows
     )
     own = exchange(send_keys, KEY_AXES).reshape(8, 4, 2, *message)
@@ -315,6 +318,7 @@
         attention_kernel,
         [shape((16, 2, GROUP * ROWS, HEAD_WIDTH), BF16)] + [part(m) for m in (8, 8, 8, 4, 4)],
         [SCALARS] * 3 + [WHOLE] * 7,
+        60,
         scratch_shapes=[
             VMEM((32, *piece), BF16),
             VMEM((32, *piece), BF16),
@@ -322,8 +326,6 @@
             VMEM((32, *piece), F32),
             VMEM((32, *piece), F32),
             VMEM((16, HEAD_WIDTH, 256), F32),
-            VMEM((16, 256, HEAD_WIDTH), BF16),
-            VMEM((16, 256, HEAD_WIDTH), BF16),
             VMEM((16, 8, 256), F32),
             pltpu.SMEM((80,), jnp.int32),
         ],

time: 156 us -> 155 us (level); the launches traced: 155 us -> 156 us
  Pallas kernels: 22.5 us -> 27 us
  local copies, waits for them, and re-layouts: 6.56 us -> 3.91 us
  starting transfers between devices: 70.8 us -> 68.7 us
    pallas_call x1, Pallas kernels: 18.2 us -> 21.9 us  [local(): vmem_call(attention_kernel, [shape((16, 2, GROUP * ROWS, HEAD_WIDTH), BF1...]
    unnamed x30 -> x36, local copies, waits for them, and re-layouts: 4.31 us -> 1.06 us
    ppermute x8, starting transfers between devices: 28.6 us -> 25.6 us  [along_z(): return lax.ppermute(value, ('zhi', 'zlo'), pairs)]
  transfers between devices with their start and end apart: 13 -> 13, of which waited for: 7 -> 7; matrix products, arithmetic and copies ran while one was open for 3% -> 4% of each run, Pallas kernels for 2% -> 2%
where the time goes in v5:
time: 155 us; the launch traced here: 156 us
  starting transfers between devices  68.7 us (44%)
  waiting for transfers between devices  52.2 us (34%)
  Pallas kernels  27 us (17%)
  local copies, waits for them, and re-layouts  3.91 us (3%)
  other arithmetic  2.55 us (2%)
    all_to_all x4, starting transfers between devices, exchange(): return lax.all_to_all(value, axes, split_axis=0, concat_axis=0, tiled=True)  41.2 us
    all_to_all x4, waiting for transfers between devices, exchange(): return lax.all_to_all(value, axes, split_axis=0, concat_axis=0, tiled=True)  40.8 us
    ppermute x8, starting transfers between devices, along_z(): return lax.ppermute(value, ('zhi', 'zlo'), pairs)  25.6 us
    pallas_call x1, Pallas kernels, local(): vmem_call(attention_kernel, [shape((16, 2, GROUP * ROWS, HEAD_WIDTH), BF1...  21.9 us
    ppermute x8, waiting for transfers between devices, along_z(): return lax.ppermute(value, ('zhi', 'zlo'), pairs)  11.2 us
  transfers between devices with their start and end apart: 13, of which 7 were waited for; matrix products, arithmetic and copies ran while one was open for 4% of the time, Pallas kernels for 2%

profile of v5, /device:TPU:64, one launch (start us, length us, event | category | flops | bytes accessed | tf_op | source)
XLA Modules:
  0.0 155.9 jit_solution(1048244924524222740)
XLA Ops:
  0.7 1.6 %shard_map.113 = bf16[32,2,16,128]{3,2,1,0:T(8,128)(2,1)} custom-call(bf16[16,1024]{1,0:T(8,128)(2,1)} %k_ref.1, bf16[16,1024]{1,0:T(8,128)(2,1)} %v_ref.1), custom_call_target="tpu_custom_call" | custom-call | tf_op jit(solution)/shard_map/pallas_call | solution.py:290
  2.3 17.2 %all-to-all-start = ((bf16[32,2,16,128]{3,2,1,0:T(8,128)(2,1)}), bf16[32,2,16,128]{3,2,1,0:T(8,128)(2,1)S(1)}, u32[]{:S(2)}, u32[]{:S(2)}) async-start(bf16[32,2,16,128]{3,2,1,0:T(8,128)(2,1)} %shard_map.113), calls=%async_computation | async-start | bytes 524288 | tf_op jit(solution)/shard_map/all_to_all | solution.py:227
  19.5 0.9 slice_reduce_fusion
  20.3 0.1 squeeze.14
  20.4 0.1 squeeze.15
  20.6 0.7 convert_bitcast_fusion
  21.3 0.1 copy.19
  21.4 0.1 reshape.128.sums_ref
  21.4 0.0 copy-done.12
  21.4 0.1 copy.18
  21.5 0.1 reshape.126.thr_ref
  21.6 0.0 copy-done.1
  21.6 1.3 shard_map.112
  22.9 20.6 %all-to-all-done = bf16[32,2,16,128]{3,2,1,0:T(8,128)(2,1)S(1)} async-done(((bf16[32,2,16,128]{3,2,1,0:T(8,128)(2,1)}), bf16[32,2,16,128]{3,2,1,0:T(8,128)(2,1)S(1)}, u32[]{:S(2)}, u32[]{:S(2)}) %all-to-all-start) | async-done | bytes 262176 | tf_op jit(solution)/shard_map/all_to_all | solution.py:227
  43.5 5.4 %all-to-all-start.1 = ((bf16[16,17,16,128]{3,2,1,0:T(8,128)(2,1)}), bf16[16,17,16,128]{3,2,1,0:T(8,128)(2,1)S(1)}, u32[]{:S(2)}, u32[]{:S(2)}) async-start(bf16[16,17,16,128]{3,2,1,0:T(8,128)(2,1)} %shard_map.112), calls=%async_computation.1 | async-start | bytes 2228224 | tf_op jit(solution)/shard_map/all_to_all | solution.py:227
  48.9 0.4 dynamic-slice_reduce_fusion.3
  49.4 0.1 reshape.114
  49.5 0.1 reshape.117
  49.5 0.1 reshape.116
  49.6 0.1 reshape.115
  49.7 1.9 %collective-permute-start.1 = (bf16[8,4,2,16,128]{4,3,2,1,0:T(8,128)(2,1)S(1)}, bf16[8,4,2,16,128]{4,3,2,1,0:T(8,128)(2,1)S(1)}, u32[]{:S(2)}, u32[]{:S(2)}) collective-permute-start(bf16[8,4,2,16,128]{4,3,2,1,0:T(8,128)(2,1)S(1)} %bitcast.10), channel_id=1, source_target_pairs={{0,1},{1,2},{2,3},{3,128},{128,129},{129,130},{130,131},{131,256},... | collective-permute-start | bytes 786440 | tf_op jit(solution)/shard_map/ppermute | solution.py:232
  51.7 3.9 %collective-permute-start = (bf16[8,4,2,16,128]{4,3,2,1,0:T(8,128)(2,1)S(1)}, bf16[8,4,2,16,128]{4,3,2,1,0:T(8,128)(2,1)S(1)}, u32[]{:S(2)}, u32[]{:S(2)}) collective-permute-start(bf16[8,4,2,16,128]{4,3,2,1,0:T(8,128)(2,1)S(1)} %bitcast.11), channel_id=1, source_target_pairs={{0,387},{1,0},{2,1},{3,2},{128,3},{129,128},{130,129},{131,130},{2... | collective-permute-start | bytes 786440 | tf_op jit(solution)/shard_map/ppermute | solution.py:232
  55.6 1.9 %collective-permute-start.3 = (bf16[4,4,2,16,128]{4,3,2,1,0:T(8,128)(2,1)S(1)}, bf16[4,4,2,16,128]{4,3,2,1,0:T(8,128)(2,1)S(1)}, u32[]{:S(2)}, u32[]{:S(2)}) collective-permute-start(bf16[4,4,2,16,128]{4,3,2,1,0:T(8,128)(2,1)S(1)} %get-tuple-element.37), channel_id=1, source_target_pairs={{0,2},{1,3},{2,128},{3,129},{128,130},{129,131},{130,256},{131,257... | collective-permute-start | bytes 393224 | tf_op jit(solution)/shard_map/ppermute | solution.py:232
  57.5 4.8 %collective-permute-start.2 = (bf16[4,4,2,16,128]{4,3,2,1,0:T(8,128)(2,1)S(1)}, bf16[4,4,2,16,128]{4,3,2,1,0:T(8,128)(2,1)S(1)}, u32[]{:S(2)}, u32[]{:S(2)}) collective-permute-start(bf16[4,4,2,16,128]{4,3,2,1,0:T(8,128)(2,1)S(1)} %get-tuple-element.38), channel_id=1, source_target_pairs={{0,386},{1,387},{2,0},{3,1},{128,2},{129,3},{130,128},{131,129},{2... | collective-permute-start | bytes 393224 | tf_op jit(solution)/shard_map/ppermute | solution.py:232
  62.4 0.1 pad_add_fusion
  62.5 0.2 fusion.7
  62.7 1.7 %collective-permute-done.3.far_b_ref = bf16[4,4,2,16,128]{4,3,2,1,0:T(8,128)(2,1)S(1)} collective-permute-done((bf16[4,4,2,16,128]{4,3,2,1,0:T(8,128)(2,1)S(1)}, bf16[4,4,2,16,128]{4,3,2,1,0:T(8,128)(2,1)S(1)}, u32[]{:S(2)}, u32[]{:S(2)}) %collective-permute-start.3) | collective-permute-done | bytes 131104 | tf_op jit(solution)/shard_map/ppermute | solution.py:232
  64.3 2.5 %collective-permute-done.2.far_a_ref = bf16[4,4,2,16,128]{4,3,2,1,0:T(8,128)(2,1)S(1)} collective-permute-done((bf16[4,4,2,16,128]{4,3,2,1,0:T(8,128)(2,1)S(1)}, bf16[4,4,2,16,128]{4,3,2,1,0:T(8,128)(2,1)S(1)}, u32[]{:S(2)}, u32[]{:S(2)}) %collective-permute-start.2) | collective-permute-done | bytes 131104 | tf_op jit(solution)/shard_map/ppermute | solution.py:232
  66.8 0.0 collective-permute-done.1.down_ref
  66.8 0.0 collective-permute-done.up_ref
  66.8 0.0 all-to-all-done.1.qa_ref
  66.9 1.9 %collective-permute-start.4 = (bf16[16,17,16,128]{3,2,1,0:T(8,128)(2,1)S(1)}, bf16[16,17,16,128]{3,2,1,0:T(8,128)(2,1)S(1)}, u32[]{:S(2)}, u32[]{:S(2)}) collective-permute-start(bf16[16,17,16,128]{3,2,1,0:T(8,128)(2,1)S(1)} %all-to-all-done.1.qa_ref), channel_id=1, source_target_pairs={{0,64},{64,0},{1,65},{65,1},{2,66},{66,2},{3,67},{67,3},{4,68},{68... | collective-permute-start | bytes 3342344 | tf_op jit(solution)/shard_map/ppermute | solution.py:310
  68.8 0.3 fusion.17
  69.1 0.1 convert_reduce_fusion.count_ref
  69.2 0.0 copy-start.11
  69.2 0.3 select_reduce_fusion.1
  69.6 0.1 select_add_fusion
  69.6 0.4 select_reduce_fusion
  70.0 0.1 fusion.10
  70.1 0.1 select_n.95
  70.2 0.6 concatenate.7.list_ref
  70.8 0.6 pad_add_fusion.1.place_ref
  71.4 0.2 collective-permute-done.4.qb_ref
  71.5 0.0 copy-done.7
  71.5 0.0 copy-done.8
  71.5 0.0 copy-done.4
  71.5 0.0 copy-done.11
  71.6 1.0 copy-done.6
  72.5 21.9 %shard_map.114 = (bf16[16,2,128,128]{3,2,1,0:T(8,128)(2,1)}, bf16[8,4,2,16,128]{4,3,2,1,0:T(8,128)(2,1)}, bf16[8,4,2,16,128]{4,3,2,1,0:T(8,128)(2,1)}, bf16[8,4,...) custom-call(s32[544]{0:T(1024)} %concatenate.7.list_ref, ...), custom_call_target="tpu_custom_call" | custom-call | tf_op jit(solution)/shard_map/pallas_call | solution.py:317
  94.5 7.5 %all-to-all-start.2 = ((bf16[32,128,128]{2,1,0:T(8,128)(2,1)}), bf16[32,128,128]{2,1,0:T(8,128)(2,1)S(1)}, u32[]{:S(2)}, u32[]{:S(2)}) async-start(bf16[32,128,128]{2,1,0:T(8,128)(2,1)} %bitcast.14), calls=%async_computation.2 | async-start | bytes 2097152 | tf_op jit(solution)/shard_map/all_to_all | solution.py:227
  101.9 1.9 %collective-permute-start.5 = (bf16[8,4,2,16,128]{4,3,2,1,0:T(8,128)(2,1)S(1)}, bf16[8,4,2,16,128]{4,3,2,1,0:T(8,128)(2,1)S(1)}, u32[]{:S(2)}, u32[]{:S(2)}) collective-permute-start(bf16[8,4,2,16,128]{4,3,2,1,0:T(8,128)(2,1)S(1)} %copy-done.14), channel_id=1, source_target_pairs={{0,1},{1,2},{2,3},{3,128},{128,129},{129,130},{130,131},{131,256},... | collective-permute-start | bytes 786440 | tf_op jit(solution)/shard_map/ppermute | solution.py:232
  103.9 3.9 %collective-permute-start.6 = (bf16[8,4,2,16,128]{4,3,2,1,0:T(8,128)(2,1)S(1)}, bf16[8,4,2,16,128]{4,3,2,1,0:T(8,128)(2,1)S(1)}, u32[]{:S(2)}, u32[]{:S(2)}) collective-permute-start(bf16[8,4,2,16,128]{4,3,2,1,0:T(8,128)(2,1)S(1)} %copy-done.13), channel_id=1, source_target_pairs={{0,387},{1,0},{2,1},{3,2},{128,3},{129,128},{130,129},{131,130},{2... | collective-permute-start | bytes 786440 | tf_op jit(solution)/shard_map/ppermute | solution.py:232
  107.8 3.4 %collective-permute-start.7 = (bf16[4,4,2,16,128]{4,3,2,1,0:T(8,128)(2,1)S(1)}, bf16[4,4,2,16,128]{4,3,2,1,0:T(8,128)(2,1)S(1)}, u32[]{:S(2)}, u32[]{:S(2)}) collective-permute-start(bf16[4,4,2,16,128]{4,3,2,1,0:T(8,128)(2,1)S(1)} %copy-done.16), channel_id=1, source_target_pairs={{0,2},{1,3},{2,128},{3,129},{128,130},{129,131},{130,256},{131,257... | collective-permute-start | bytes 393224 | tf_op jit(solution)/shard_map/ppermute | solution.py:232
  111.2 3.8 %collective-permute-start.8 = (bf16[4,4,2,16,128]{4,3,2,1,0:T(8,128)(2,1)S(1)}, bf16[4,4,2,16,128]{4,3,2,1,0:T(8,128)(2,1)S(1)}, u32[]{:S(2)}, u32[]{:S(2)}) collective-permute-start(bf16[4,4,2,16,128]{4,3,2,1,0:T(8,128)(2,1)S(1)} %copy-done.15), channel_id=1, source_target_pairs={{0,386},{1,387},{2,0},{3,1},{128,2},{129,3},{130,128},{131,129},{2... | collective-permute-start | bytes 393224 | tf_op jit(solution)/shard_map/ppermute | solution.py:232
  115.0 3.4 %collective-permute-done.7.far_a_ref = bf16[4,4,2,16,128]{4,3,2,1,0:T(8,128)(2,1)S(1)} collective-permute-done((bf16[4,4,2,16,128]{4,3,2,1,0:T(8,128)(2,1)S(1)}, bf16[4,4,2,16,128]{4,3,2,1,0:T(8,128)(2,1)S(1)}, u32[]{:S(2)}, u32[]{:S(2)}) %collective-permute-start.7) | collective-permute-done | bytes 131104 | tf_op jit(solution)/shard_map/ppermute | solution.py:232
  118.4 3.7 %collective-permute-done.8.far_b_ref = bf16[4,4,2,16,128]{4,3,2,1,0:T(8,128)(2,1)S(1)} collective-permute-done((bf16[4,4,2,16,128]{4,3,2,1,0:T(8,128)(2,1)S(1)}, bf16[4,4,2,16,128]{4,3,2,1,0:T(8,128)(2,1)S(1)}, u32[]{:S(2)}, u32[]{:S(2)}) %collective-permute-start.8) | collective-permute-done | bytes 131104 | tf_op jit(solution)/shard_map/ppermute | solution.py:232
  122.1 0.0 collective-permute-done.5.up_ref
  122.1 0.0 collective-permute-done.6.down_ref
  122.1 0.8 shard_map.116
  122.9 0.0 all-to-all-done.2.in_ref
  122.9 11.2 %all-to-all-start.3 = ((bf16[32,2,16,128]{3,2,1,0:T(8,128)(2,1)}), bf16[32,2,16,128]{3,2,1,0:T(8,128)(2,1)S(1)}, u32[]{:S(2)}, u32[]{:S(2)}) async-start(bf16[32,2,16,128]{3,2,1,0:T(8,128)(2,1)} %bitcast.7), calls=%async_computation.3 | async-start | bytes 524288 | tf_op jit(solution)/shard_map/all_to_all | solution.py:227
  134.1 0.8 shard_map.115
  134.9 20.3 %all-to-all-done.3.in_ref = bf16[32,2,16,128]{3,2,1,0:T(8,128)(2,1)S(1)} async-done(((bf16[32,2,16,128]{3,2,1,0:T(8,128)(2,1)}), bf16[32,2,16,128]{3,2,1,0:T(8,128)(2,1)S(1)}, u32[]{:S(2)}, u32[]{:S(2)}) %all-to-all-start.3) | async-done | bytes 262176 | tf_op jit(solution)/shard_map/all_to_all | solution.py:227
  155.2 0.7 shard_map.117
  (34 shorter events, 0.1 us)
Async XLA Ops:
  0.6 20.8 %copy-start.12 = (bf16[16,64]{1,0:T(8,128)(2,1)S(1)}, bf16[16,64]{1,0:T(8,128)(2,1)}, u32[]{:S(2)}) copy-start(bf16[16,64]{1,0:T(8,128)(2,1)} %param.14) | copy-start | bytes 6148
  0.6 21.0 %copy-start.3 = (bf16[16,8192]{1,0:T(8,128)(2,1)S(1)}, bf16[16,8192]{1,0:T(8,128)(2,1)}, u32[]{:S(2)}) copy-start(bf16[16,8192]{1,0:T(8,128)(2,1)} %sup_ref.1) | copy-start | bytes 786436
  0.7 21.0 %copy-start.2 = (bf16[16,8192]{1,0:T(8,128)(2,1)S(1)}, bf16[16,8192]{1,0:T(8,128)(2,1)}, u32[]{:S(2)}) copy-start(bf16[16,8192]{1,0:T(8,128)(2,1)} %do_ref.1) | copy-start | bytes 786436
  0.7 21.0 %copy-start.1 = (bf16[16,8192]{1,0:T(8,128)(2,1)S(1)}, bf16[16,8192]{1,0:T(8,128)(2,1)}, u32[]{:S(2)}) copy-start(bf16[16,8192]{1,0:T(8,128)(2,1)} %q_ref.1) | copy-start | bytes 786436
  2.3 41.2 %all-to-all-start = ((bf16[32,2,16,128]{3,2,1,0:T(8,128)(2,1)}), bf16[32,2,16,128]{3,2,1,0:T(8,128)(2,1)S(1)}, u32[]{:S(2)}, u32[]{:S(2)}) async-start(bf16[32,2,16,128]{3,2,1,0:T(8,128)(2,1)} %shard_map.113), calls=%async_computation | async-start | bytes 524288 | tf_op jit(solution)/shard_map/all_to_all | solution.py:227
  43.5 12.1 %copy-start.5 = (bf16[32,2,16,128]{3,2,1,0:T(8,128)(2,1)}, bf16[32,2,16,128]{3,2,1,0:T(8,128)(2,1)S(1)}, u32[]{:S(2)}) copy-start(bf16[32,2,16,128]{3,2,1,0:T(8,128)(2,1)S(1)} %all-to-all-done) | copy-start | bytes 786436
  43.5 25.3 %copy-start.17 = (s32[64,64]{1,0:T(8,128)S(1)}, s32[64,64]{1,0:T(8,128)}, u32[]{:S(2)}) copy-start(s32[64,64]{1,0:T(8,128)} %param.17) | copy-start | bytes 49156
  43.5 23.4 %all-to-all-start.1 = ((bf16[16,17,16,128]{3,2,1,0:T(8,128)(2,1)}), bf16[16,17,16,128]{3,2,1,0:T(8,128)(2,1)S(1)}, u32[]{:S(2)}, u32[]{:S(2)}) async-start(bf16[16,17,16,128]{3,2,1,0:T(8,128)(2,1)} %shard_map.112), calls=%async_computation.1 | async-start | bytes 2228224 | tf_op jit(solution)/shard_map/all_to_all | solution.py:227
  49.7 17.1 %collective-permute-start.1 = (bf16[8,4,2,16,128]{4,3,2,1,0:T(8,128)(2,1)S(1)}, bf16[8,4,2,16,128]{4,3,2,1,0:T(8,128)(2,1)S(1)}, u32[]{:S(2)}, u32[]{:S(2)}) collective-permute-start(bf16[8,4,2,16,128]{4,3,2,1,0:T(8,128)(2,1)S(1)} %bitcast.10), channel_id=1, source_target_pairs={{0,1},{1,2},{2,3},{3,128},{128,129},{129,130},{130,131},{131,256},... | collective-permute-start | bytes 786440 | tf_op jit(solution)/shard_map/ppermute | solution.py:232
  51.7 15.2 %collective-permute-start = (bf16[8,4,2,16,128]{4,3,2,1,0:T(8,128)(2,1)S(1)}, bf16[8,4,2,16,128]{4,3,2,1,0:T(8,128)(2,1)S(1)}, u32[]{:S(2)}, u32[]{:S(2)}) collective-permute-start(bf16[8,4,2,16,128]{4,3,2,1,0:T(8,128)(2,1)S(1)} %bitcast.11), channel_id=1, source_target_pairs={{0,387},{1,0},{2,1},{3,2},{128,3},{129,128},{130,129},{131,130},{2... | collective-permute-start | bytes 786440 | tf_op jit(solution)/shard_map/ppermute | solution.py:232
  55.6 8.7 %collective-permute-start.3 = (bf16[4,4,2,16,128]{4,3,2,1,0:T(8,128)(2,1)S(1)}, bf16[4,4,2,16,128]{4,3,2,1,0:T(8,128)(2,1)S(1)}, u32[]{:S(2)}, u32[]{:S(2)}) collective-permute-start(bf16[4,4,2,16,128]{4,3,2,1,0:T(8,128)(2,1)S(1)} %get-tuple-element.37), channel_id=1, source_target_pairs={{0,2},{1,3},{2,128},{3,129},{128,130},{129,131},{130,256},{131,257... | collective-permute-start | bytes 393224 | tf_op jit(solution)/shard_map/ppermute | solution.py:232
  57.5 9.3 %collective-permute-start.2 = (bf16[4,4,2,16,128]{4,3,2,1,0:T(8,128)(2,1)S(1)}, bf16[4,4,2,16,128]{4,3,2,1,0:T(8,128)(2,1)S(1)}, u32[]{:S(2)}, u32[]{:S(2)}) collective-permute-start(bf16[4,4,2,16,128]{4,3,2,1,0:T(8,128)(2,1)S(1)} %get-tuple-element.38), channel_id=1, source_target_pairs={{0,386},{1,387},{2,0},{3,1},{128,2},{129,3},{130,128},{131,129},{2... | collective-permute-start | bytes 393224 | tf_op jit(solution)/shard_map/ppermute | solution.py:232
  64.3 7.2 %copy-start.9 = (bf16[4,4,2,16,128]{4,3,2,1,0:T(8,128)(2,1)}, bf16[4,4,2,16,128]{4,3,2,1,0:T(8,128)(2,1)S(1)}, u32[]{:S(2)}) copy-start(bf16[4,4,2,16,128]{4,3,2,1,0:T(8,128)(2,1)S(1)} %collective-permute-done.3.far_b_ref) | copy-start | bytes 393220
  66.8 4.7 %copy-start.10 = (bf16[4,4,2,16,128]{4,3,2,1,0:T(8,128)(2,1)}, bf16[4,4,2,16,128]{4,3,2,1,0:T(8,128)(2,1)S(1)}, u32[]{:S(2)}) copy-start(bf16[4,4,2,16,128]{4,3,2,1,0:T(8,128)(2,1)S(1)} %collective-permute-done.2.far_a_ref) | copy-start | bytes 393220
  66.8 4.7 %copy-start.7 = (bf16[8,4,2,16,128]{4,3,2,1,0:T(8,128)(2,1)}, bf16[8,4,2,16,128]{4,3,2,1,0:T(8,128)(2,1)S(1)}, u32[]{:S(2)}) copy-start(bf16[8,4,2,16,128]{4,3,2,1,0:T(8,128)(2,1)S(1)} %collective-permute-done.1.down_ref) | copy-start | bytes 786436
  66.8 4.7 %copy-start.8 = (bf16[8,4,2,16,128]{4,3,2,1,0:T(8,128)(2,1)}, bf16[8,4,2,16,128]{4,3,2,1,0:T(8,128)(2,1)S(1)}, u32[]{:S(2)}) copy-start(bf16[8,4,2,16,128]{4,3,2,1,0:T(8,128)(2,1)S(1)} %collective-permute-done.up_ref) | copy-start | bytes 786436
  66.8 4.7 %copy-start.4 = (bf16[16,17,16,128]{3,2,1,0:T(8,128)(2,1)}, bf16[16,17,16,128]{3,2,1,0:T(8,128)(2,1)S(1)}, u32[]{:S(2)}) copy-start(bf16[16,17,16,128]{3,2,1,0:T(8,128)(2,1)S(1)} %all-to-all-done.1.qa_ref) | copy-start | bytes 3342340
  66.9 4.6 %collective-permute-start.4 = (bf16[16,17,16,128]{3,2,1,0:T(8,128)(2,1)S(1)}, bf16[16,17,16,128]{3,2,1,0:T(8,128)(2,1)S(1)}, u32[]{:S(2)}, u32[]{:S(2)}) collective-permute-start(bf16[16,17,16,128]{3,2,1,0:T(8,128)(2,1)S(1)} %all-to-all-done.1.qa_ref), channel_id=1, source_target_pairs={{0,64},{64,0},{1,65},{65,1},{2,66},{66,2},{3,67},{67,3},{4,68},{68... | collective-permute-start | bytes 3342344 | tf_op jit(solution)/shard_map/ppermute | solution.py:310
  69.2 2.3 %copy-start.11 = (s32[16]{0:T(128)}, s32[16]{0:T(128)S(1)}, u32[]{:S(2)}) copy-start(s32[16]{0:T(128)S(1)} %convert_reduce_fusion.count_ref) | copy-start | bytes 196
  71.5 1.0 copy-start.6
  94.4 7.5 %copy-start.14 = (bf16[8,4,2,16,128]{4,3,2,1,0:T(8,128)(2,1)S(1)}, bf16[8,4,2,16,128]{4,3,2,1,0:T(8,128)(2,1)}, u32[]{:S(2)}) copy-start(bf16[8,4,2,16,128]{4,3,2,1,0:T(8,128)(2,1)} %get-tuple-element.27) | copy-start | bytes 786436
  94.4 9.4 %copy-start.13 = (bf16[8,4,2,16,128]{4,3,2,1,0:T(8,128)(2,1)S(1)}, bf16[8,4,2,16,128]{4,3,2,1,0:T(8,128)(2,1)}, u32[]{:S(2)}) copy-start(bf16[8,4,2,16,128]{4,3,2,1,0:T(8,128)(2,1)} %get-tuple-element.28) | copy-start | bytes 786436
  94.4 13.4 %copy-start.16 = (bf16[4,4,2,16,128]{4,3,2,1,0:T(8,128)(2,1)S(1)}, bf16[4,4,2,16,128]{4,3,2,1,0:T(8,128)(2,1)}, u32[]{:S(2)}) copy-start(bf16[4,4,2,16,128]{4,3,2,1,0:T(8,128)(2,1)} %get-tuple-element.29) | copy-start | bytes 393220
  94.4 16.8 %copy-start.15 = (bf16[4,4,2,16,128]{4,3,2,1,0:T(8,128)(2,1)S(1)}, bf16[4,4,2,16,128]{4,3,2,1,0:T(8,128)(2,1)}, u32[]{:S(2)}) copy-start(bf16[4,4,2,16,128]{4,3,2,1,0:T(8,128)(2,1)} %get-tuple-element.30) | copy-start | bytes 393220
  94.5 27.6 %copy-start = (bf16[8,4,2,16,128]{4,3,2,1,0:T(8,128)(2,1)S(1)}, bf16[8,4,2,16,128]{4,3,2,1,0:T(8,128)(2,1)}, u32[]{:S(2)}) copy-start(bf16[8,4,2,16,128]{4,3,2,1,0:T(8,128)(2,1)} %get-tuple-element.26.own_ref) | copy-start | bytes 786436
  94.5 28.5 %all-to-all-start.2 = ((bf16[32,128,128]{2,1,0:T(8,128)(2,1)}), bf16[32,128,128]{2,1,0:T(8,128)(2,1)S(1)}, u32[]{:S(2)}, u32[]{:S(2)}) async-start(bf16[32,128,128]{2,1,0:T(8,128)(2,1)} %bitcast.14), calls=%async_computation.2 | async-start | bytes 2097152 | tf_op jit(solution)/shard_map/all_to_all | solution.py:227
  101.9 20.1 %collective-permute-start.5 = (bf16[8,4,2,16,128]{4,3,2,1,0:T(8,128)(2,1)S(1)}, bf16[8,4,2,16,128]{4,3,2,1,0:T(8,128)(2,1)S(1)}, u32[]{:S(2)}, u32[]{:S(2)}) collective-permute-start(bf16[8,4,2,16,128]{4,3,2,1,0:T(8,128)(2,1)S(1)} %copy-done.14), channel_id=1, source_target_pairs={{0,1},{1,2},{2,3},{3,128},{128,129},{129,130},{130,131},{131,256},... | collective-permute-start | bytes 786440 | tf_op jit(solution)/shard_map/ppermute | solution.py:232
  103.9 18.2 %collective-permute-start.6 = (bf16[8,4,2,16,128]{4,3,2,1,0:T(8,128)(2,1)S(1)}, bf16[8,4,2,16,128]{4,3,2,1,0:T(8,128)(2,1)S(1)}, u32[]{:S(2)}, u32[]{:S(2)}) collective-permute-start(bf16[8,4,2,16,128]{4,3,2,1,0:T(8,128)(2,1)S(1)} %copy-done.13), channel_id=1, source_target_pairs={{0,387},{1,0},{2,1},{3,2},{128,3},{129,128},{130,129},{131,130},{2... | collective-permute-start | bytes 786440 | tf_op jit(solution)/shard_map/ppermute | solution.py:232
  107.8 10.5 %collective-permute-start.7 = (bf16[4,4,2,16,128]{4,3,2,1,0:T(8,128)(2,1)S(1)}, bf16[4,4,2,16,128]{4,3,2,1,0:T(8,128)(2,1)S(1)}, u32[]{:S(2)}, u32[]{:S(2)}) collective-permute-start(bf16[4,4,2,16,128]{4,3,2,1,0:T(8,128)(2,1)S(1)} %copy-done.16), channel_id=1, source_target_pairs={{0,2},{1,3},{2,128},{3,129},{128,130},{129,131},{130,256},{131,257... | collective-permute-start | bytes 393224 | tf_op jit(solution)/shard_map/ppermute | solution.py:232
  111.2 10.9 %collective-permute-start.8 = (bf16[4,4,2,16,128]{4,3,2,1,0:T(8,128)(2,1)S(1)}, bf16[4,4,2,16,128]{4,3,2,1,0:T(8,128)(2,1)S(1)}, u32[]{:S(2)}, u32[]{:S(2)}) collective-permute-start(bf16[4,4,2,16,128]{4,3,2,1,0:T(8,128)(2,1)S(1)} %copy-done.15), channel_id=1, source_target_pairs={{0,386},{1,387},{2,0},{3,1},{128,2},{129,3},{130,128},{131,129},{2... | collective-permute-start | bytes 393224 | tf_op jit(solution)/shard_map/ppermute | solution.py:232
  122.9 32.3 %all-to-all-start.3 = ((bf16[32,2,16,128]{3,2,1,0:T(8,128)(2,1)}), bf16[32,2,16,128]{3,2,1,0:T(8,128)(2,1)S(1)}, u32[]{:S(2)}, u32[]{:S(2)}) async-start(bf16[32,2,16,128]{3,2,1,0:T(8,128)(2,1)} %bitcast.7), calls=%async_computation.3 | async-start | bytes 524288 | tf_op jit(solution)/shard_map/all_to_all | solution.py:227

commit v6 on v5

--- a/solution.py
+++ b/solution.py
@@ -22,7 +22,8 @@
 STEPS = (0, 1, -1, 2)
 TOKEN_AXES = ("x", "yh", "yl", "zlo", "zhi", "core")
 PLANE = ("x", "yh", "yl")
-KEY_AXES = ("x", "yl", "zhi")
+HEAD_AXES = ("x", "yl")
+KEY_AXES = ("zhi", "x", "yl")
 VMEM = pltpu.VMEM
 F32 = jnp.float32
 BF16 = jnp.bfloat16
@@ -46,13 +47,24 @@
 def pack_keys_kernel(k_ref, v_ref, out_ref):
     for head in range(KEY_HEADS):
         cols = slice(head * HEAD_WIDTH, (head + 1) * HEAD_WIDTH)
-        key, value = k_ref[:, cols], v_ref[:, cols]
-        for copy in range(4):
-            out_ref[head * 4 + copy, 0] = key
-            out_ref[head * 4 + copy, 1] = value
+        out_ref[head, 0] = k_ref[:, cols]
+        out_ref[head, 1] = v_ref[:, cols]
 
 
 def pack_queries_kernel(q_ref, do_ref, sup_ref, thr_ref, sums_ref, out_ref):
+    wide = (QUERY_HEADS, GROUP * ROWS)
+    column = lax.broadcasted_iota(jnp.int32, wide, 0)
+    lane_head = lax.broadcasted_iota(jnp.int32, wide, 1) >> 4
+    tall = (ROWS, GROUP * ROWS)
+    own_row = lax.broadcasted_iota(jnp.int32, tall, 0) == (
+        lax.broadcasted_iota(jnp.int32, tall, 1) & (ROWS - 1)
+    )
+
+    def to_lanes(ref, head):
+        pick = (column == head * GROUP + lane_head).astype(BF16)
+        spread = jnp.dot(ref[...], pick, preferred_element_type=F32)
+        return jnp.sum(jnp.where(own_row, spread, 0.0), axis=0, keepdims=True)
+
     for head in range(KEY_HEADS):
         dests = [(head // 2) * 4 + yh * 2 + head % 2 for yh in range(2)]
         products = []
@@ -65,11 +77,11 @@
                 out_ref[dest, GROUP + g] = grad
             products.append(grad.astype(F32) * sup_ref[:, cols].astype(F32))
         row_dot = jnp.sum(jnp.concatenate(products, axis=0).T, axis=0, keepdims=True)
-        mean = row_dot / sums_ref[head : head + 1, :]
+        mean = row_dot / to_lanes(sums_ref, head)
         high = mean.astype(BF16).astype(F32)
         low = mean - high
         stats = jnp.concatenate(
-            [thr_ref[head : head + 1, :], high, low, jnp.zeros((13, 128), F32)], axis=0
+            [to_lanes(thr_ref, head), high, low, jnp.zeros((13, 128), F32)], axis=0
         ).astype(BF16)
         for dest in dests:
             out_ref[dest, 2 * GROUP] = stats
@@ -199,7 +211,7 @@
         total = (own_ref[b].astype(F32) + up_ref[b].astype(F32)) + (
             down_ref[b].astype(F32) + far.astype(F32)
         )
-        out_ref[b] = total.astype(BF16)
+        out_ref[:, b] = total.astype(BF16)
 
 
 def sum_queries_kernel(in_ref, out_ref):
@@ -219,7 +231,7 @@
     for head in range(KEY_HEADS):
         cols = slice(head * HEAD_WIDTH, (head + 1) * HEAD_WIDTH)
         for kind, ref in enumerate((dk_ref, dv_ref)):
-            parts = [in_ref[head * 4 + zhi, kind].astype(F32) for zhi in range(4)]
+            parts = [in_ref[zhi * 8 + head, kind].astype(F32) for zhi in range(4)]
             ref[:, cols] = ((parts[0] + parts[1]) + (parts[2] + parts[3])).astype(BF16)
 
 
@@ -282,21 +294,18 @@
 ):
     shape = jax.ShapeDtypeStruct
 
-    def by_head(stat):
-        return stat.astype(F32).T.reshape(KEY_HEADS, GROUP * ROWS)
-
     place = jnp.stack([lax.axis_index(name) for name in ("core", "zhi")]).astype(jnp.int32)
     message = (ROWS, HEAD_WIDTH)
-    send_keys = vmem_call(pack_keys_kernel, shape((32, 2, *message), BF16), [WHOLE] * 2, 60)(
+    send_keys = vmem_call(pack_keys_kernel, shape((8, 2, *message), BF16), [WHOLE] * 2, 60)(
         key_head_rows, value_head_rows
     )
-    own = exchange(send_keys, KEY_AXES).reshape(8, 4, 2, *message)
-    send = vmem_call(pack_queries_kernel, shape((16, SLOTS, *message), BF16), [WHOLE] * 5)(
+    own = jnp.swapaxes(lax.all_gather(exchange(send_keys, HEAD_AXES), "zhi", axis=0), 0, 1)
+    send = vmem_call(pack_queries_kernel, shape((16, SLOTS, *message), BF16), [WHOLE] * 5, 60)(
         queries,
         output_gradient,
         support_values,
-        by_head(thresholds),
-        by_head(gate_row_sums),
+        thresholds,
+        gate_row_sums,
     )
     send, own = lax.optimization_barrier((send, own))
     near = [
@@ -308,6 +317,7 @@
     arrived = exchange(send, PLANE)
     arrived, *near = lax.optimization_barrier((arrived, *near))
     arrived_other = lax.ppermute(arrived, "core", [(0, 1), (1, 0)])
+    token_pos, _ = lax.optimization_barrier((token_pos, own[0, 0, 0, 0, 0]))
     lists, count = active_lists(token_pos, block_mask)
 
     def part(many):
@@ -340,7 +350,9 @@
     query_out = vmem_call(
         sum_queries_kernel, shape((ROWS, QUERY_HEADS * HEAD_WIDTH), BF16), [WHOLE]
     )(back_query)
-    total = vmem_call(total_kernel, part(8), [WHOLE] * 5)(grad_own, *back)
+    total = vmem_call(total_kernel, shape((4, 8, 2, *message), BF16), [WHOLE] * 5)(
+        grad_own, *back
+    )
     back_keys = exchange(total.reshape(32, 2, *message), KEY_AXES)
     key_shape = shape((ROWS, KEY_HEADS * HEAD_WIDTH), BF16)
     key_out, value_out = vmem_call(sum_keys_kernel, [key_shape, key_shape], [WHOLE])(back_keys)

time: 155 us -> 152 us (0.981)
  the two profiles are of different devices: /device:TPU:64 before, /device:TPU:8 now
where the time goes in v6:
time: 152 us; the launch traced here: 151 us
  starting transfers between devices  67.2 us (44%)
  waiting for transfers between devices  29.4 us (19%)
  Pallas kernels  24.5 us (16%)
  blocking collectives  23.4 us (15%)
  local copies, waits for them, and re-layouts  3.61 us (2%)
  other arithmetic  1.92 us (1%)
    all_to_all x4, starting transfers between devices, exchange(): return lax.all_to_all(value, axes, split_axis=0, concat_axis=0, tiled=True)  35 us
    ppermute x8, starting transfers between devices, along_z(): return lax.ppermute(value, ('zhi', 'zlo'), pairs)  30.3 us
    all_gather x1, blocking collectives, local(): lax.all_gather(exchange(send_keys, HEAD_AXES), 'zhi', axis=0)  23.4 us
    all_to_all x4, waiting for transfers between devices, exchange(): return lax.all_to_all(value, axes, split_axis=0, concat_axis=0, tiled=True)  20.2 us
    pallas_call x1, Pallas kernels, local(): vmem_call(attention_kernel, [shape((16, 2, GROUP * ROWS, HEAD_WIDTH), BF1...  18.4 us
    ppermute x8, waiting for transfers between devices, along_z(): return lax.ppermute(value, ('zhi', 'zlo'), pairs)  9.17 us
  transfers between devices with their start and end apart: 13, of which 7 were waited for; matrix products, arithmetic and copies ran while one was open for 3% of the time, Pallas kernels for 3%

profile of v6, /device:TPU:8, one launch (start us, length us, event | category | flops | bytes accessed | tf_op | source)
XLA Modules:
  0.0 151.3 jit_solution(6629404343861196008)
XLA Ops:
  0.6 1.4 shard_map.113
  2.0 9.1 %all-to-all-start = ((bf16[8,2,16,128]{3,2,1,0:T(8,128)(2,1)}), bf16[8,2,16,128]{3,2,1,0:T(8,128)(2,1)S(1)}, u32[]{:S(2)}, u32[]{:S(2)}) async-start(bf16[8,2,16,128]{3,2,1,0:T(8,128)(2,1)} %shard_map.113), calls=%async_computation | async-start | bytes 131072 | tf_op jit(solution)/shard_map/all_to_all | solution.py:239
  11.1 0.9 slice_reduce_fusion
  12.1 0.1 squeeze.15
  12.1 0.1 squeeze.16
  12.3 2.4 %shard_map.112 = bf16[16,17,16,128]{3,2,1,0:T(8,128)(2,1)} custom-call(bf16[16,8192]{1,0:T(8,128)(2,1)} %q_ref.1, bf16[16,8192]{1,0:T(8,128)(2,1)} %do_ref.1, bf16[16,8192]{1,0:T(8,128)(2,1)} %sup_ref.1, bf16[16,64]{1,0:T(8,128)(2,1)} %thr_ref.1, bf16[16,64]{1,0:T(8,128)(2,1)} %sums_ref.1), custom_call_target="tpu_custom_call" | custom-call | tf_op jit(solution)/shard_map/pallas_call | solution.py:303
  14.7 1.5 %all-to-all-done = bf16[8,2,16,128]{3,2,1,0:T(8,128)(2,1)S(1)} async-done(((bf16[8,2,16,128]{3,2,1,0:T(8,128)(2,1)}), bf16[8,2,16,128]{3,2,1,0:T(8,128)(2,1)S(1)}, u32[]{:S(2)}, u32[]{:S(2)}) %all-to-all-start) | async-done | bytes 65568 | tf_op jit(solution)/shard_map/all_to_all | solution.py:239
  16.2 23.4 %all-gather = bf16[32,2,16,128]{3,2,1,0:T(8,128)(2,1)S(1)} all-gather(bf16[8,2,16,128]{3,2,1,0:T(8,128)(2,1)S(1)} %all-to-all-done), channel_id=2, replica_groups=mesh['zhi'=4,'core'=2,'x'=4,'yh'=2,'yl'=2,'zlo'=4] {'zhi'}, dimensions={0}, use_global_device_ids=true | all-gather | bytes 327680 | tf_op jit(solution)/shard_map/all_gather | solution.py:302
  39.6 0.0 copy-start.2
  39.6 0.0 copy-start.13
  39.6 7.7 %all-to-all-start.1 = ((bf16[16,17,16,128]{3,2,1,0:T(8,128)(2,1)}), bf16[16,17,16,128]{3,2,1,0:T(8,128)(2,1)S(1)}, u32[]{:S(2)}, u32[]{:S(2)}) async-start(bf16[16,17,16,128]{3,2,1,0:T(8,128)(2,1)} %shard_map.112), calls=%async_computation.1 | async-start | bytes 2228224 | tf_op jit(solution)/shard_map/all_to_all | solution.py:239
  47.4 0.4 dynamic-slice_reduce_fusion.3
  47.8 0.1 reshape.101
  47.9 0.1 reshape.104
  48.0 0.1 reshape.103
  48.0 0.1 reshape.102
  48.2 1.9 %collective-permute-start.1 = (bf16[8,4,2,16,128]{4,3,2,1,0:T(8,128)(2,1)S(1)}, bf16[8,4,2,16,128]{4,3,2,1,0:T(8,128)(2,1)S(1)}, u32[]{:S(2)}, u32[]{:S(2)}) collective-permute-start(bf16[8,4,2,16,128]{4,3,2,1,0:T(8,128)(2,1)S(1)} %bitcast.9), channel_id=1, source_target_pairs={{0,1},{1,2},{2,3},{3,128},{128,129},{129,130},{130,131},{131,256},... | collective-permute-start | bytes 786440 | tf_op jit(solution)/shard_map/ppermute | solution.py:244
  50.1 5.1 %collective-permute-start = (bf16[8,4,2,16,128]{4,3,2,1,0:T(8,128)(2,1)S(1)}, bf16[8,4,2,16,128]{4,3,2,1,0:T(8,128)(2,1)S(1)}, u32[]{:S(2)}, u32[]{:S(2)}) collective-permute-start(bf16[8,4,2,16,128]{4,3,2,1,0:T(8,128)(2,1)S(1)} %bitcast.10), channel_id=1, source_target_pairs={{0,387},{1,0},{2,1},{3,2},{128,3},{129,128},{130,129},{131,130},{2... | collective-permute-start | bytes 786440 | tf_op jit(solution)/shard_map/ppermute | solution.py:244
  55.2 0.0 copy-done.2
  55.3 1.9 %collective-permute-start.3 = (bf16[4,4,2,16,128]{4,3,2,1,0:T(8,128)(2,1)S(1)}, bf16[4,4,2,16,128]{4,3,2,1,0:T(8,128)(2,1)S(1)}, u32[]{:S(2)}, u32[]{:S(2)}) collective-permute-start(bf16[4,4,2,16,128]{4,3,2,1,0:T(8,128)(2,1)S(1)} %get-tuple-element.37), channel_id=1, source_target_pairs={{0,2},{1,3},{2,128},{3,129},{128,130},{129,131},{130,256},{131,257... | collective-permute-start | bytes 393224 | tf_op jit(solution)/shard_map/ppermute | solution.py:244
  57.2 6.0 %collective-permute-start.2 = (bf16[4,4,2,16,128]{4,3,2,1,0:T(8,128)(2,1)S(1)}, bf16[4,4,2,16,128]{4,3,2,1,0:T(8,128)(2,1)S(1)}, u32[]{:S(2)}, u32[]{:S(2)}) collective-permute-start(bf16[4,4,2,16,128]{4,3,2,1,0:T(8,128)(2,1)S(1)} %get-tuple-element.38), channel_id=1, source_target_pairs={{0,386},{1,387},{2,0},{3,1},{128,2},{129,3},{130,128},{131,129},{2... | collective-permute-start | bytes 393224 | tf_op jit(solution)/shard_map/ppermute | solution.py:244
  63.2 0.1 pad_add_fusion
  63.3 0.2 fusion.7
  63.5 0.9 collective-permute-done.3.far_b_ref
  64.4 1.9 %collective-permute-done.2.far_a_ref = bf16[4,4,2,16,128]{4,3,2,1,0:T(8,128)(2,1)S(1)} collective-permute-done((bf16[4,4,2,16,128]{4,3,2,1,0:T(8,128)(2,1)S(1)}, bf16[4,4,2,16,128]{4,3,2,1,0:T(8,128)(2,1)S(1)}, u32[]{:S(2)}, u32[]{:S(2)}) %collective-permute-start.2) | collective-permute-done | bytes 131104 | tf_op jit(solution)/shard_map/ppermute | solution.py:244
  66.4 0.0 collective-permute-done.1.down_ref
  66.4 0.0 collective-permute-done.up_ref
  66.4 0.0 copy-start.5
  66.4 0.0 all-to-all-done.1.qa_ref
  66.4 0.0 copy-start.1
  66.4 1.9 %collective-permute-start.4 = (bf16[16,17,16,128]{3,2,1,0:T(8,128)(2,1)S(1)}, bf16[16,17,16,128]{3,2,1,0:T(8,128)(2,1)S(1)}, u32[]{:S(2)}, u32[]{:S(2)}) collective-permute-start(bf16[16,17,16,128]{3,2,1,0:T(8,128)(2,1)S(1)} %all-to-all-done.1.qa_ref), channel_id=1, source_target_pairs={{0,64},{64,0},{1,65},{65,1},{2,66},{66,2},{3,67},{67,3},{4,68},{68... | collective-permute-start | bytes 3342344 | tf_op jit(solution)/shard_map/ppermute | solution.py:319
  68.3 0.0 copy-done.13
  68.3 0.3 fusion.17
  68.6 0.1 convert_reduce_fusion.count_ref
  68.8 0.0 copy-start.8
  68.8 0.3 select_reduce_fusion.1
  69.1 0.1 select_add_fusion
  69.2 0.4 select_reduce_fusion
  69.5 0.1 fusion.10
  69.6 0.1 select_n.95
  69.7 0.6 concatenate.7.list_ref
  70.3 0.7 pad_add_fusion.1.place_ref
  71.0 0.1 collective-permute-done.4.qb_ref
  71.0 0.0 copy-done.6
  71.0 0.0 copy-done.7
  71.0 0.0 copy-done.4
  71.1 1.0 copy-done.3
  72.1 18.4 %shard_map.114 = (bf16[16,2,128,128]{3,2,1,0:T(8,128)(2,1)}, bf16[8,4,2,16,128]{4,3,2,1,0:T(8,128)(2,1)}, bf16[8,4,2,16,128]{4,3,2,1,0:T(8,128)(2,1)}, bf16[8,4,...) custom-call(s32[544]{0:T(1024)} %concatenate.7.list_ref, ...), custom_call_target="tpu_custom_call" | custom-call | tf_op jit(solution)/shard_map/pallas_call | solution.py:327
  90.5 7.6 %all-to-all-start.2 = ((bf16[32,128,128]{2,1,0:T(8,128)(2,1)}), bf16[32,128,128]{2,1,0:T(8,128)(2,1)S(1)}, u32[]{:S(2)}, u32[]{:S(2)}) async-start(bf16[32,128,128]{2,1,0:T(8,128)(2,1)} %bitcast.14), calls=%async_computation.2 | async-start | bytes 2097152 | tf_op jit(solution)/shard_map/all_to_all | solution.py:239
  98.1 4.3 %collective-permute-start.5 = (bf16[8,4,2,16,128]{4,3,2,1,0:T(8,128)(2,1)S(1)}, bf16[8,4,2,16,128]{4,3,2,1,0:T(8,128)(2,1)S(1)}, u32[]{:S(2)}, u32[]{:S(2)}) collective-permute-start(bf16[8,4,2,16,128]{4,3,2,1,0:T(8,128)(2,1)S(1)} %copy-done.10), channel_id=1, source_target_pairs={{0,1},{1,2},{2,3},{3,128},{128,129},{129,130},{130,131},{131,256},... | collective-permute-start | bytes 786440 | tf_op jit(solution)/shard_map/ppermute | solution.py:244
  102.4 2.8 %collective-permute-start.6 = (bf16[8,4,2,16,128]{4,3,2,1,0:T(8,128)(2,1)S(1)}, bf16[8,4,2,16,128]{4,3,2,1,0:T(8,128)(2,1)S(1)}, u32[]{:S(2)}, u32[]{:S(2)}) collective-permute-start(bf16[8,4,2,16,128]{4,3,2,1,0:T(8,128)(2,1)S(1)} %copy-done.9), channel_id=1, source_target_pairs={{0,387},{1,0},{2,1},{3,2},{128,3},{129,128},{130,129},{131,130},{2... | collective-permute-start | bytes 786440 | tf_op jit(solution)/shard_map/ppermute | solution.py:244
  105.2 0.0 copy-done.12
  105.2 4.1 %collective-permute-start.7 = (bf16[4,4,2,16,128]{4,3,2,1,0:T(8,128)(2,1)S(1)}, bf16[4,4,2,16,128]{4,3,2,1,0:T(8,128)(2,1)S(1)}, u32[]{:S(2)}, u32[]{:S(2)}) collective-permute-start(bf16[4,4,2,16,128]{4,3,2,1,0:T(8,128)(2,1)S(1)} %copy-done.12), channel_id=1, source_target_pairs={{0,2},{1,3},{2,128},{3,129},{128,130},{129,131},{130,256},{131,257... | collective-permute-start | bytes 393224 | tf_op jit(solution)/shard_map/ppermute | solution.py:244
  109.3 4.1 %collective-permute-start.8 = (bf16[4,4,2,16,128]{4,3,2,1,0:T(8,128)(2,1)S(1)}, bf16[4,4,2,16,128]{4,3,2,1,0:T(8,128)(2,1)S(1)}, u32[]{:S(2)}, u32[]{:S(2)}) collective-permute-start(bf16[4,4,2,16,128]{4,3,2,1,0:T(8,128)(2,1)S(1)} %copy-done.11), channel_id=1, source_target_pairs={{0,386},{1,387},{2,0},{3,1},{128,2},{129,3},{130,128},{131,129},{2... | collective-permute-start | bytes 393224 | tf_op jit(solution)/shard_map/ppermute | solution.py:244
  113.4 2.4 %collective-permute-done.7.far_a_ref = bf16[4,4,2,16,128]{4,3,2,1,0:T(8,128)(2,1)S(1)} collective-permute-done((bf16[4,4,2,16,128]{4,3,2,1,0:T(8,128)(2,1)S(1)}, bf16[4,4,2,16,128]{4,3,2,1,0:T(8,128)(2,1)S(1)}, u32[]{:S(2)}, u32[]{:S(2)}) %collective-permute-start.7) | collective-permute-done | bytes 131104 | tf_op jit(solution)/shard_map/ppermute | solution.py:244
  115.8 3.9 %collective-permute-done.8.far_b_ref = bf16[4,4,2,16,128]{4,3,2,1,0:T(8,128)(2,1)S(1)} collective-permute-done((bf16[4,4,2,16,128]{4,3,2,1,0:T(8,128)(2,1)S(1)}, bf16[4,4,2,16,128]{4,3,2,1,0:T(8,128)(2,1)S(1)}, u32[]{:S(2)}, u32[]{:S(2)}) %collective-permute-start.8) | collective-permute-done | bytes 131104 | tf_op jit(solution)/shard_map/ppermute | solution.py:244
  119.7 0.0 collective-permute-done.5.up_ref
  119.7 0.0 collective-permute-done.6.down_ref
  119.7 0.8 shard_map.116
  120.6 0.0 all-to-all-done.2.in_ref
  120.6 10.7 %all-to-all-start.3 = ((bf16[32,2,16,128]{3,2,1,0:T(8,128)(2,1)}), bf16[32,2,16,128]{3,2,1,0:T(8,128)(2,1)S(1)}, u32[]{:S(2)}, u32[]{:S(2)}) async-start(bf16[32,2,16,128]{3,2,1,0:T(8,128)(2,1)} %bitcast.6), calls=%async_computation.3 | async-start | bytes 524288 | tf_op jit(solution)/shard_map/all_to_all | solution.py:239
  131.2 0.8 shard_map.115
  132.1 18.6 %all-to-all-done.3.in_ref = bf16[32,2,16,128]{3,2,1,0:T(8,128)(2,1)S(1)} async-done(((bf16[32,2,16,128]{3,2,1,0:T(8,128)(2,1)}), bf16[32,2,16,128]{3,2,1,0:T(8,128)(2,1)S(1)}, u32[]{:S(2)}, u32[]{:S(2)}) %all-to-all-start.3) | async-done | bytes 262176 | tf_op jit(solution)/shard_map/all_to_all | solution.py:239
  150.7 0.7 shard_map.117
  (22 shorter events, 0.1 us)
Async XLA Ops:
  2.0 14.2 %all-to-all-start = ((bf16[8,2,16,128]{3,2,1,0:T(8,128)(2,1)}), bf16[8,2,16,128]{3,2,1,0:T(8,128)(2,1)S(1)}, u32[]{:S(2)}, u32[]{:S(2)}) async-start(bf16[8,2,16,128]{3,2,1,0:T(8,128)(2,1)} %shard_map.113), calls=%async_computation | async-start | bytes 131072 | tf_op jit(solution)/shard_map/all_to_all | solution.py:239
  39.6 15.6 %copy-start.2 = (bf16[4,8,2,16,128]{4,3,2,0,1:T(8,128)(2,1)}, bf16[4,8,2,16,128]{4,3,2,0,1:T(8,128)(2,1)S(1)}, u32[]{:S(2)}) copy-start(bf16[4,8,2,16,128]{4,3,2,0,1:T(8,128)(2,1)S(1)} %copy.17) | copy-start | bytes 786436
  39.6 28.7 %copy-start.13 = (s32[64,64]{1,0:T(8,128)S(1)}, s32[64,64]{1,0:T(8,128)}, u32[]{:S(2)}) copy-start(s32[64,64]{1,0:T(8,128)} %param.17) | copy-start | bytes 49156
  39.6 26.7 %all-to-all-start.1 = ((bf16[16,17,16,128]{3,2,1,0:T(8,128)(2,1)}), bf16[16,17,16,128]{3,2,1,0:T(8,128)(2,1)S(1)}, u32[]{:S(2)}, u32[]{:S(2)}) async-start(bf16[16,17,16,128]{3,2,1,0:T(8,128)(2,1)} %shard_map.112), calls=%async_computation.1 | async-start | bytes 2228224 | tf_op jit(solution)/shard_map/all_to_all | solution.py:239
  48.2 18.2 %collective-permute-start.1 = (bf16[8,4,2,16,128]{4,3,2,1,0:T(8,128)(2,1)S(1)}, bf16[8,4,2,16,128]{4,3,2,1,0:T(8,128)(2,1)S(1)}, u32[]{:S(2)}, u32[]{:S(2)}) collective-permute-start(bf16[8,4,2,16,128]{4,3,2,1,0:T(8,128)(2,1)S(1)} %bitcast.9), channel_id=1, source_target_pairs={{0,1},{1,2},{2,3},{3,128},{128,129},{129,130},{130,131},{131,256},... | collective-permute-start | bytes 786440 | tf_op jit(solution)/shard_map/ppermute | solution.py:244
  50.1 16.3 %collective-permute-start = (bf16[8,4,2,16,128]{4,3,2,1,0:T(8,128)(2,1)S(1)}, bf16[8,4,2,16,128]{4,3,2,1,0:T(8,128)(2,1)S(1)}, u32[]{:S(2)}, u32[]{:S(2)}) collective-permute-start(bf16[8,4,2,16,128]{4,3,2,1,0:T(8,128)(2,1)S(1)} %bitcast.10), channel_id=1, source_target_pairs={{0,387},{1,0},{2,1},{3,2},{128,3},{129,128},{130,129},{131,130},{2... | collective-permute-start | bytes 786440 | tf_op jit(solution)/shard_map/ppermute | solution.py:244
  55.3 9.1 %collective-permute-start.3 = (bf16[4,4,2,16,128]{4,3,2,1,0:T(8,128)(2,1)S(1)}, bf16[4,4,2,16,128]{4,3,2,1,0:T(8,128)(2,1)S(1)}, u32[]{:S(2)}, u32[]{:S(2)}) collective-permute-start(bf16[4,4,2,16,128]{4,3,2,1,0:T(8,128)(2,1)S(1)} %get-tuple-element.37), channel_id=1, source_target_pairs={{0,2},{1,3},{2,128},{3,129},{128,130},{129,131},{130,256},{131,257... | collective-permute-start | bytes 393224 | tf_op jit(solution)/shard_map/ppermute | solution.py:244
  57.2 9.2 %collective-permute-start.2 = (bf16[4,4,2,16,128]{4,3,2,1,0:T(8,128)(2,1)S(1)}, bf16[4,4,2,16,128]{4,3,2,1,0:T(8,128)(2,1)S(1)}, u32[]{:S(2)}, u32[]{:S(2)}) collective-permute-start(bf16[4,4,2,16,128]{4,3,2,1,0:T(8,128)(2,1)S(1)} %get-tuple-element.38), channel_id=1, source_target_pairs={{0,386},{1,387},{2,0},{3,1},{128,2},{129,3},{130,128},{131,129},{2... | collective-permute-start | bytes 393224 | tf_op jit(solution)/shard_map/ppermute | solution.py:244
  64.4 6.6 %copy-start.6 = (bf16[4,4,2,16,128]{4,3,2,1,0:T(8,128)(2,1)}, bf16[4,4,2,16,128]{4,3,2,1,0:T(8,128)(2,1)S(1)}, u32[]{:S(2)}) copy-start(bf16[4,4,2,16,128]{4,3,2,1,0:T(8,128)(2,1)S(1)} %collective-permute-done.3.far_b_ref) | copy-start | bytes 393220
  66.4 4.7 %copy-start.7 = (bf16[4,4,2,16,128]{4,3,2,1,0:T(8,128)(2,1)}, bf16[4,4,2,16,128]{4,3,2,1,0:T(8,128)(2,1)S(1)}, u32[]{:S(2)}) copy-start(bf16[4,4,2,16,128]{4,3,2,1,0:T(8,128)(2,1)S(1)} %collective-permute-done.2.far_a_ref) | copy-start | bytes 393220
  66.4 4.7 %copy-start.4 = (bf16[8,4,2,16,128]{4,3,2,1,0:T(8,128)(2,1)}, bf16[8,4,2,16,128]{4,3,2,1,0:T(8,128)(2,1)S(1)}, u32[]{:S(2)}) copy-start(bf16[8,4,2,16,128]{4,3,2,1,0:T(8,128)(2,1)S(1)} %collective-permute-done.1.down_ref) | copy-start | bytes 786436
  66.4 4.7 %copy-start.5 = (bf16[8,4,2,16,128]{4,3,2,1,0:T(8,128)(2,1)}, bf16[8,4,2,16,128]{4,3,2,1,0:T(8,128)(2,1)S(1)}, u32[]{:S(2)}) copy-start(bf16[8,4,2,16,128]{4,3,2,1,0:T(8,128)(2,1)S(1)} %collective-permute-done.up_ref) | copy-start | bytes 786436
  66.4 4.7 %copy-start.1 = (bf16[16,17,16,128]{3,2,1,0:T(8,128)(2,1)}, bf16[16,17,16,128]{3,2,1,0:T(8,128)(2,1)S(1)}, u32[]{:S(2)}) copy-start(bf16[16,17,16,128]{3,2,1,0:T(8,128)(2,1)S(1)} %all-to-all-done.1.qa_ref) | copy-start | bytes 3342340
  66.4 4.6 %collective-permute-start.4 = (bf16[16,17,16,128]{3,2,1,0:T(8,128)(2,1)S(1)}, bf16[16,17,16,128]{3,2,1,0:T(8,128)(2,1)S(1)}, u32[]{:S(2)}, u32[]{:S(2)}) collective-permute-start(bf16[16,17,16,128]{3,2,1,0:T(8,128)(2,1)S(1)} %all-to-all-done.1.qa_ref), channel_id=1, source_target_pairs={{0,64},{64,0},{1,65},{65,1},{2,66},{66,2},{3,67},{67,3},{4,68},{68... | collective-permute-start | bytes 3342344 | tf_op jit(solution)/shard_map/ppermute | solution.py:319
  68.8 2.3 %copy-start.8 = (s32[16]{0:T(128)}, s32[16]{0:T(128)S(1)}, u32[]{:S(2)}) copy-start(s32[16]{0:T(128)S(1)} %convert_reduce_fusion.count_ref) | copy-start | bytes 196
  71.1 1.0 copy-start.3
  90.5 7.6 %copy-start.10 = (bf16[8,4,2,16,128]{4,3,2,1,0:T(8,128)(2,1)S(1)}, bf16[8,4,2,16,128]{4,3,2,1,0:T(8,128)(2,1)}, u32[]{:S(2)}) copy-start(bf16[8,4,2,16,128]{4,3,2,1,0:T(8,128)(2,1)} %get-tuple-element.27) | copy-start | bytes 786436
  90.5 11.9 %copy-start.9 = (bf16[8,4,2,16,128]{4,3,2,1,0:T(8,128)(2,1)S(1)}, bf16[8,4,2,16,128]{4,3,2,1,0:T(8,128)(2,1)}, u32[]{:S(2)}) copy-start(bf16[8,4,2,16,128]{4,3,2,1,0:T(8,128)(2,1)} %get-tuple-element.28) | copy-start | bytes 786436
  90.5 14.7 %copy-start.12 = (bf16[4,4,2,16,128]{4,3,2,1,0:T(8,128)(2,1)S(1)}, bf16[4,4,2,16,128]{4,3,2,1,0:T(8,128)(2,1)}, u32[]{:S(2)}) copy-start(bf16[4,4,2,16,128]{4,3,2,1,0:T(8,128)(2,1)} %get-tuple-element.29) | copy-start | bytes 393220
  90.5 18.8 %copy-start.11 = (bf16[4,4,2,16,128]{4,3,2,1,0:T(8,128)(2,1)S(1)}, bf16[4,4,2,16,128]{4,3,2,1,0:T(8,128)(2,1)}, u32[]{:S(2)}) copy-start(bf16[4,4,2,16,128]{4,3,2,1,0:T(8,128)(2,1)} %get-tuple-element.30) | copy-start | bytes 393220
  90.5 29.2 %copy-start = (bf16[8,4,2,16,128]{4,3,2,1,0:T(8,128)(2,1)S(1)}, bf16[8,4,2,16,128]{4,3,2,1,0:T(8,128)(2,1)}, u32[]{:S(2)}) copy-start(bf16[8,4,2,16,128]{4,3,2,1,0:T(8,128)(2,1)} %get-tuple-element.26.own_ref) | copy-start | bytes 786436
  90.5 30.0 %all-to-all-start.2 = ((bf16[32,128,128]{2,1,0:T(8,128)(2,1)}), bf16[32,128,128]{2,1,0:T(8,128)(2,1)S(1)}, u32[]{:S(2)}, u32[]{:S(2)}) async-start(bf16[32,128,128]{2,1,0:T(8,128)(2,1)} %bitcast.14), calls=%async_computation.2 | async-start | bytes 2097152 | tf_op jit(solution)/shard_map/all_to_all | solution.py:239
  98.1 21.6 %collective-permute-start.5 = (bf16[8,4,2,16,128]{4,3,2,1,0:T(8,128)(2,1)S(1)}, bf16[8,4,2,16,128]{4,3,2,1,0:T(8,128)(2,1)S(1)}, u32[]{:S(2)}, u32[]{:S(2)}) collective-permute-start(bf16[8,4,2,16,128]{4,3,2,1,0:T(8,128)(2,1)S(1)} %copy-done.10), channel_id=1, source_target_pairs={{0,1},{1,2},{2,3},{3,128},{128,129},{129,130},{130,131},{131,256},... | collective-permute-start | bytes 786440 | tf_op jit(solution)/shard_map/ppermute | solution.py:244
  102.4 17.4 %collective-permute-start.6 = (bf16[8,4,2,16,128]{4,3,2,1,0:T(8,128)(2,1)S(1)}, bf16[8,4,2,16,128]{4,3,2,1,0:T(8,128)(2,1)S(1)}, u32[]{:S(2)}, u32[]{:S(2)}) collective-permute-start(bf16[8,4,2,16,128]{4,3,2,1,0:T(8,128)(2,1)S(1)} %copy-done.9), channel_id=1, source_target_pairs={{0,387},{1,0},{2,1},{3,2},{128,3},{129,128},{130,129},{131,130},{2... | collective-permute-start | bytes 786440 | tf_op jit(solution)/shard_map/ppermute | solution.py:244
  105.2 10.6 %collective-permute-start.7 = (bf16[4,4,2,16,128]{4,3,2,1,0:T(8,128)(2,1)S(1)}, bf16[4,4,2,16,128]{4,3,2,1,0:T(8,128)(2,1)S(1)}, u32[]{:S(2)}, u32[]{:S(2)}) collective-permute-start(bf16[4,4,2,16,128]{4,3,2,1,0:T(8,128)(2,1)S(1)} %copy-done.12), channel_id=1, source_target_pairs={{0,2},{1,3},{2,128},{3,129},{128,130},{129,131},{130,256},{131,257... | collective-permute-start | bytes 393224 | tf_op jit(solution)/shard_map/ppermute | solution.py:244
  109.3 10.4 %collective-permute-start.8 = (bf16[4,4,2,16,128]{4,3,2,1,0:T(8,128)(2,1)S(1)}, bf16[4,4,2,16,128]{4,3,2,1,0:T(8,128)(2,1)S(1)}, u32[]{:S(2)}, u32[]{:S(2)}) collective-permute-start(bf16[4,4,2,16,128]{4,3,2,1,0:T(8,128)(2,1)S(1)} %copy-done.11), channel_id=1, source_target_pairs={{0,386},{1,387},{2,0},{3,1},{128,2},{129,3},{130,128},{131,129},{2... | collective-permute-start | bytes 393224 | tf_op jit(solution)/shard_map/ppermute | solution.py:244
  120.6 30.1 %all-to-all-start.3 = ((bf16[32,2,16,128]{3,2,1,0:T(8,128)(2,1)}), bf16[32,2,16,128]{3,2,1,0:T(8,128)(2,1)S(1)}, u32[]{:S(2)}, u32[]{:S(2)}) async-start(bf16[32,2,16,128]{3,2,1,0:T(8,128)(2,1)} %bitcast.6), calls=%async_computation.3 | async-start | bytes 524288 | tf_op jit(solution)/shard_map/all_to_all | solution.py:239

commit v7 on v6

--- a/solution.py
+++ b/solution.py
@@ -90,7 +90,6 @@
 def attention_kernel(
     list_ref,
     count_ref,
-    place_ref,
     qa_ref,
     qb_ref,
     own_ref,
@@ -113,7 +112,7 @@
     stat_s,
     work_s,
 ):
-    core, zhi = place_ref[0], place_ref[1]
+    core, zhi = lax.axis_index("core"), lax.axis_index("zhi")
     ins = [own_ref, up_ref, down_ref, far_a_ref, far_b_ref]
     outs = [own_out, up_out, down_out, far_a_out, far_b_out]
     places = [(0, 8), (8, 8), (16, 8), (24, 4), (28, 4)]
@@ -169,7 +168,9 @@
         for way in range(UNROLL):
             base = work_s[step * UNROLL + way]
             j = jnp.minimum(base >> 5, 15)
-            entries = [list_ref[base + u] for u in range(BATCH)]
+            entries = [
+                jnp.where(base >= 512, 64, list_ref[j, (base & 31) + u]) for u in range(BATCH)
+            ]
             ids = [entry & 31 for entry in entries]
             keys = jnp.concatenate([k_s[i] for i in ids], axis=0)
             values = jnp.concatenate([v_s[i] for i in ids], axis=0)
@@ -278,7 +279,7 @@
         axis=2,
     )
     lists = jnp.where(number[None, :] < count[:, None], lists, 64)
-    return jnp.concatenate([lists.reshape(512), jnp.full((32,), 64, jnp.int32)]), count
+    return lists, count
 
 
 def local(
@@ -294,7 +295,6 @@
 ):
     shape = jax.ShapeDtypeStruct
 
-    place = jnp.stack([lax.axis_index(name) for name in ("core", "zhi")]).astype(jnp.int32)
     message = (ROWS, HEAD_WIDTH)
     send_keys = vmem_call(pack_keys_kernel, shape((8, 2, *message), BF16), [WHOLE] * 2, 60)(
         key_head_rows, value_head_rows
@@ -327,7 +327,7 @@
     grad_query, grad_own, *grad_near = vmem_call(
         attention_kernel,
         [shape((16, 2, GROUP * ROWS, HEAD_WIDTH), BF16)] + [part(m) for m in (8, 8, 8, 4, 4)],
-        [SCALARS] * 3 + [WHOLE] * 7,
+        [SCALARS] * 2 + [WHOLE] * 7,
         60,
         scratch_shapes=[
             VMEM((32, *piece), BF16),
@@ -339,7 +339,7 @@
             VMEM((16, 8, 256), F32),
             pltpu.SMEM((80,), jnp.int32),
         ],
-    )(lists, count, place, arrived, arrived_other, own, *near)
+    )(lists, count, arrived, arrived_other, own, *near)
 
     back = [
         along_z(grad, step) for grad, step in zip(grad_near, (1, -1, 2, -2), strict=True)

time: 152 us -> 153 us (level)
  starting transfers between devices: 67.2 us -> 64 us
  waiting for transfers between devices: 29.4 us -> 32.2 us
  Pallas kernels: 24.5 us -> 26.9 us
    all_to_all x4, starting transfers between devices: 35 us -> 32.1 us  [exchange(): return lax.all_to_all(value, axes, split_axis=0, concat_axis=0, tiled=True)]
    all_to_all x4, waiting for transfers between devices: 20.2 us -> 22.6 us  [exchange(): return lax.all_to_all(value, axes, split_axis=0, concat_axis=0, tiled=True)]
    pallas_call x1, Pallas kernels: 18.4 us -> 20.7 us  [local(): vmem_call(attention_kernel, [shape((16, 2, GROUP * ROWS, HEAD_WIDTH), BF1...]
  transfers between devices with their start and end apart: 13 -> 13, of which waited for: 7 -> 7; matrix products, arithmetic and copies ran while one was open for 3% -> 2% of each run, Pallas kernels for 3% -> 3%
where the time goes in v7:
time: 153 us; the launch traced here: 152 us
  starting transfers between devices  64 us (42%)
  waiting for transfers between devices  32.2 us (21%)
  Pallas kernels  26.9 us (18%)
  blocking collectives  23.4 us (15%)
  local copies, waits for them, and re-layouts  2.17 us (1%)
  other arithmetic  1.88 us (1%)
    all_to_all x4, starting transfers between devices, exchange(): return lax.all_to_all(value, axes, split_axis=0, concat_axis=0, tiled=True)  32.1 us
    ppermute x8, starting transfers between devices, along_z(): return lax.ppermute(value, ('zhi', 'zlo'), pairs)  30 us
    all_gather x1, blocking collectives, local(): lax.all_gather(exchange(send_keys, HEAD_AXES), 'zhi', axis=0)  23.4 us
    all_to_all x4, waiting for transfers between devices, exchange(): return lax.all_to_all(value, axes, split_axis=0, concat_axis=0, tiled=True)  22.6 us
    pallas_call x1, Pallas kernels, local(): vmem_call(attention_kernel, [shape((16, 2, GROUP * ROWS, HEAD_WIDTH), BF1...  20.7 us
    ppermute x8, waiting for transfers between devices, along_z(): return lax.ppermute(value, ('zhi', 'zlo'), pairs)  8.88 us
  transfers between devices with their start and end apart: 13, of which 7 were waited for; matrix products, arithmetic and copies ran while one was open for 2% of the time, Pallas kernels for 3%

profile of v7, /device:TPU:8, one launch (start us, length us, event | category | flops | bytes accessed | tf_op | source)
XLA Modules:
  0.0 151.9 jit_solution(6085855314328291671)
XLA Ops:
  0.6 1.4 shard_map.113
  2.0 9.1 %all-to-all-start = ((bf16[8,2,16,128]{3,2,1,0:T(8,128)(2,1)}), bf16[8,2,16,128]{3,2,1,0:T(8,128)(2,1)S(1)}, u32[]{:S(2)}, u32[]{:S(2)}) async-start(bf16[8,2,16,128]{3,2,1,0:T(8,128)(2,1)} %shard_map.113), calls=%async_computation | async-start | bytes 131072 | tf_op jit(solution)/shard_map/all_to_all | solution.py:240
  11.1 2.4 %shard_map.112 = bf16[16,17,16,128]{3,2,1,0:T(8,128)(2,1)} custom-call(bf16[16,8192]{1,0:T(8,128)(2,1)} %q_ref.1, bf16[16,8192]{1,0:T(8,128)(2,1)} %do_ref.1, bf16[16,8192]{1,0:T(8,128)(2,1)} %sup_ref.1, bf16[16,64]{1,0:T(8,128)(2,1)} %thr_ref.1, bf16[16,64]{1,0:T(8,128)(2,1)} %sums_ref.1), custom_call_target="tpu_custom_call" | custom-call | tf_op jit(solution)/shard_map/pallas_call | solution.py:303
  13.5 2.7 %all-to-all-done = bf16[8,2,16,128]{3,2,1,0:T(8,128)(2,1)S(1)} async-done(((bf16[8,2,16,128]{3,2,1,0:T(8,128)(2,1)}), bf16[8,2,16,128]{3,2,1,0:T(8,128)(2,1)S(1)}, u32[]{:S(2)}, u32[]{:S(2)}) %all-to-all-start) | async-done | bytes 65568 | tf_op jit(solution)/shard_map/all_to_all | solution.py:240
  16.2 23.4 %all-gather = bf16[32,2,16,128]{3,2,1,0:T(8,128)(2,1)S(1)} all-gather(bf16[8,2,16,128]{3,2,1,0:T(8,128)(2,1)S(1)} %all-to-all-done), channel_id=2, replica_groups=mesh['zhi'=4,'core'=2,'x'=4,'yh'=2,'yl'=2,'zlo'=4] {'zhi'}, dimensions={0}, use_global_device_ids=true | all-gather | bytes 327680 | tf_op jit(solution)/shard_map/all_gather | solution.py:302
  39.6 0.0 copy-start.2
  39.6 0.0 copy-start.8
  39.6 0.0 copy-start.14
  39.7 6.3 %all-to-all-start.1 = ((bf16[16,17,16,128]{3,2,1,0:T(8,128)(2,1)}), bf16[16,17,16,128]{3,2,1,0:T(8,128)(2,1)S(1)}, u32[]{:S(2)}, u32[]{:S(2)}) async-start(bf16[16,17,16,128]{3,2,1,0:T(8,128)(2,1)} %shard_map.112), calls=%async_computation.1 | async-start | bytes 2228224 | tf_op jit(solution)/shard_map/all_to_all | solution.py:240
  46.0 0.0 copy-done.8
  46.0 0.1 slice_reduce_fusion
  46.1 0.1 squeeze.15
  46.2 0.1 squeeze.16
  46.3 2.4 %collective-permute-start.1 = (bf16[8,4,2,16,128]{4,3,2,1,0:T(8,128)(2,1)S(1)}, bf16[8,4,2,16,128]{4,3,2,1,0:T(8,128)(2,1)S(1)}, u32[]{:S(2)}, u32[]{:S(2)}) collective-permute-start(bf16[8,4,2,16,128]{4,3,2,1,0:T(8,128)(2,1)S(1)} %bitcast.7), channel_id=1, source_target_pairs={{0,1},{1,2},{2,3},{3,128},{128,129},{129,130},{130,131},{131,256},... | collective-permute-start | bytes 786440 | tf_op jit(solution)/shard_map/ppermute | solution.py:245
  48.8 4.6 %collective-permute-start = (bf16[8,4,2,16,128]{4,3,2,1,0:T(8,128)(2,1)S(1)}, bf16[8,4,2,16,128]{4,3,2,1,0:T(8,128)(2,1)S(1)}, u32[]{:S(2)}, u32[]{:S(2)}) collective-permute-start(bf16[8,4,2,16,128]{4,3,2,1,0:T(8,128)(2,1)S(1)} %bitcast.8), channel_id=1, source_target_pairs={{0,387},{1,0},{2,1},{3,2},{128,3},{129,128},{130,129},{131,130},{2... | collective-permute-start | bytes 786440 | tf_op jit(solution)/shard_map/ppermute | solution.py:245
  53.4 0.0 copy-done.2
  53.4 1.9 %collective-permute-start.3 = (bf16[4,4,2,16,128]{4,3,2,1,0:T(8,128)(2,1)S(1)}, bf16[4,4,2,16,128]{4,3,2,1,0:T(8,128)(2,1)S(1)}, u32[]{:S(2)}, u32[]{:S(2)}) collective-permute-start(bf16[4,4,2,16,128]{4,3,2,1,0:T(8,128)(2,1)S(1)} %get-tuple-element.37), channel_id=1, source_target_pairs={{0,2},{1,3},{2,128},{3,129},{128,130},{129,131},{130,256},{131,257... | collective-permute-start | bytes 393224 | tf_op jit(solution)/shard_map/ppermute | solution.py:245
  55.4 6.0 %collective-permute-start.2 = (bf16[4,4,2,16,128]{4,3,2,1,0:T(8,128)(2,1)S(1)}, bf16[4,4,2,16,128]{4,3,2,1,0:T(8,128)(2,1)S(1)}, u32[]{:S(2)}, u32[]{:S(2)}) collective-permute-start(bf16[4,4,2,16,128]{4,3,2,1,0:T(8,128)(2,1)S(1)} %get-tuple-element.38), channel_id=1, source_target_pairs={{0,386},{1,387},{2,0},{3,1},{128,2},{129,3},{130,128},{131,129},{2... | collective-permute-start | bytes 393224 | tf_op jit(solution)/shard_map/ppermute | solution.py:245
  61.5 0.4 dynamic-slice_reduce_fusion.3
  61.9 0.1 reshape.94
  62.0 0.1 reshape.97
  62.1 0.1 reshape.96
  62.2 0.1 reshape.95
  62.3 0.2 fusion.7
  62.5 1.0 collective-permute-done.3.far_b_ref
  63.5 1.2 collective-permute-done.2.far_a_ref
  64.6 0.0 collective-permute-done.1.down_ref
  64.7 0.0 collective-permute-done.up_ref
  64.7 0.0 copy-start.5
  64.7 0.0 all-to-all-done.1.qa_ref
  64.7 0.0 copy-start.1
  64.7 1.9 %collective-permute-start.4 = (bf16[16,17,16,128]{3,2,1,0:T(8,128)(2,1)S(1)}, bf16[16,17,16,128]{3,2,1,0:T(8,128)(2,1)S(1)}, u32[]{:S(2)}, u32[]{:S(2)}) collective-permute-start(bf16[16,17,16,128]{3,2,1,0:T(8,128)(2,1)S(1)} %all-to-all-done.1.qa_ref), channel_id=1, source_target_pairs={{0,64},{64,0},{1,65},{65,1},{2,66},{66,2},{3,67},{67,3},{4,68},{68... | collective-permute-start | bytes 3342344 | tf_op jit(solution)/shard_map/ppermute | solution.py:319
  66.6 0.1 pad_add_fusion
  66.7 0.0 copy-done.14
  66.7 0.3 fusion.17
  67.0 0.1 convert_reduce_fusion.count_ref
  67.1 0.0 copy-start.9
  67.1 0.3 select_reduce_fusion.1
  67.5 0.1 select_add_fusion
  67.6 0.4 select_reduce_fusion
  67.9 0.7 fusion.10.list_ref
  68.6 0.8 collective-permute-done.4.qb_ref
  69.3 0.0 copy-done.6
  69.3 0.0 copy-done.7
  69.3 0.0 copy-done.4
  69.3 0.0 copy-done.5
  69.4 1.0 copy-done.3
  70.4 20.7 %shard_map.114 = (bf16[16,2,128,128]{3,2,1,0:T(8,128)(2,1)}, bf16[8,4,2,16,128]{4,3,2,1,0:T(8,128)(2,1)}, bf16[8,4,2,16,128]{4,3,2,1,0:T(8,128)(2,1)}, bf16[8,4,...) custom-call(s32[16,32]{1,0:T(8,128)} %fusion.10.list_ref, ...), custom_call_target="tpu_custom_call" | custom-call | tf_op jit(solution)/shard_map/pallas_call | solution.py:327
  91.2 6.0 %all-to-all-start.2 = ((bf16[32,128,128]{2,1,0:T(8,128)(2,1)}), bf16[32,128,128]{2,1,0:T(8,128)(2,1)S(1)}, u32[]{:S(2)}, u32[]{:S(2)}) async-start(bf16[32,128,128]{2,1,0:T(8,128)(2,1)} %bitcast.12), calls=%async_computation.2 | async-start | bytes 2097152 | tf_op jit(solution)/shard_map/all_to_all | solution.py:240
  97.2 0.0 copy-done.11
  97.2 2.1 %collective-permute-start.5 = (bf16[8,4,2,16,128]{4,3,2,1,0:T(8,128)(2,1)S(1)}, bf16[8,4,2,16,128]{4,3,2,1,0:T(8,128)(2,1)S(1)}, u32[]{:S(2)}, u32[]{:S(2)}) collective-permute-start(bf16[8,4,2,16,128]{4,3,2,1,0:T(8,128)(2,1)S(1)} %copy-done.11), channel_id=1, source_target_pairs={{0,1},{1,2},{2,3},{3,128},{128,129},{129,130},{130,131},{131,256},... | collective-permute-start | bytes 786440 | tf_op jit(solution)/shard_map/ppermute | solution.py:245
  99.3 4.9 %collective-permute-start.6 = (bf16[8,4,2,16,128]{4,3,2,1,0:T(8,128)(2,1)S(1)}, bf16[8,4,2,16,128]{4,3,2,1,0:T(8,128)(2,1)S(1)}, u32[]{:S(2)}, u32[]{:S(2)}) collective-permute-start(bf16[8,4,2,16,128]{4,3,2,1,0:T(8,128)(2,1)S(1)} %copy-done.10), channel_id=1, source_target_pairs={{0,387},{1,0},{2,1},{3,2},{128,3},{129,128},{130,129},{131,130},{2... | collective-permute-start | bytes 786440 | tf_op jit(solution)/shard_map/ppermute | solution.py:245
  104.3 4.4 %collective-permute-start.7 = (bf16[4,4,2,16,128]{4,3,2,1,0:T(8,128)(2,1)S(1)}, bf16[4,4,2,16,128]{4,3,2,1,0:T(8,128)(2,1)S(1)}, u32[]{:S(2)}, u32[]{:S(2)}) collective-permute-start(bf16[4,4,2,16,128]{4,3,2,1,0:T(8,128)(2,1)S(1)} %copy-done.13), channel_id=1, source_target_pairs={{0,2},{1,3},{2,128},{3,129},{128,130},{129,131},{130,256},{131,257... | collective-permute-start | bytes 393224 | tf_op jit(solution)/shard_map/ppermute | solution.py:245
  108.7 3.6 %collective-permute-start.8 = (bf16[4,4,2,16,128]{4,3,2,1,0:T(8,128)(2,1)S(1)}, bf16[4,4,2,16,128]{4,3,2,1,0:T(8,128)(2,1)S(1)}, u32[]{:S(2)}, u32[]{:S(2)}) collective-permute-start(bf16[4,4,2,16,128]{4,3,2,1,0:T(8,128)(2,1)S(1)} %copy-done.12), channel_id=1, source_target_pairs={{0,386},{1,387},{2,0},{3,1},{128,2},{129,3},{130,128},{131,129},{2... | collective-permute-start | bytes 393224 | tf_op jit(solution)/shard_map/ppermute | solution.py:245
  112.3 2.4 %collective-permute-done.7.far_a_ref = bf16[4,4,2,16,128]{4,3,2,1,0:T(8,128)(2,1)S(1)} collective-permute-done((bf16[4,4,2,16,128]{4,3,2,1,0:T(8,128)(2,1)S(1)}, bf16[4,4,2,16,128]{4,3,2,1,0:T(8,128)(2,1)S(1)}, u32[]{:S(2)}, u32[]{:S(2)}) %collective-permute-start.7) | collective-permute-done | bytes 131104 | tf_op jit(solution)/shard_map/ppermute | solution.py:245
  114.6 4.3 %collective-permute-done.8.far_b_ref = bf16[4,4,2,16,128]{4,3,2,1,0:T(8,128)(2,1)S(1)} collective-permute-done((bf16[4,4,2,16,128]{4,3,2,1,0:T(8,128)(2,1)S(1)}, bf16[4,4,2,16,128]{4,3,2,1,0:T(8,128)(2,1)S(1)}, u32[]{:S(2)}, u32[]{:S(2)}) %collective-permute-start.8) | collective-permute-done | bytes 131104 | tf_op jit(solution)/shard_map/ppermute | solution.py:245
  119.0 0.0 collective-permute-done.5.up_ref
  119.0 0.0 collective-permute-done.6.down_ref
  119.0 0.8 shard_map.116
  119.8 0.0 all-to-all-done.2.in_ref
  119.8 10.7 %all-to-all-start.3 = ((bf16[32,2,16,128]{3,2,1,0:T(8,128)(2,1)}), bf16[32,2,16,128]{3,2,1,0:T(8,128)(2,1)S(1)}, u32[]{:S(2)}, u32[]{:S(2)}) async-start(bf16[32,2,16,128]{3,2,1,0:T(8,128)(2,1)} %bitcast.4), calls=%async_computation.3 | async-start | bytes 524288 | tf_op jit(solution)/shard_map/all_to_all | solution.py:240
  130.5 0.8 shard_map.115
  131.3 19.9 %all-to-all-done.3.in_ref = bf16[32,2,16,128]{3,2,1,0:T(8,128)(2,1)S(1)} async-done(((bf16[32,2,16,128]{3,2,1,0:T(8,128)(2,1)}), bf16[32,2,16,128]{3,2,1,0:T(8,128)(2,1)S(1)}, u32[]{:S(2)}, u32[]{:S(2)}) %all-to-all-start.3) | async-done | bytes 262176 | tf_op jit(solution)/shard_map/all_to_all | solution.py:240
  151.3 0.7 shard_map.117
  (21 shorter events, 0.1 us)
Async XLA Ops:
  2.0 14.2 %all-to-all-start = ((bf16[8,2,16,128]{3,2,1,0:T(8,128)(2,1)}), bf16[8,2,16,128]{3,2,1,0:T(8,128)(2,1)S(1)}, u32[]{:S(2)}, u32[]{:S(2)}) async-start(bf16[8,2,16,128]{3,2,1,0:T(8,128)(2,1)} %shard_map.113), calls=%async_computation | async-start | bytes 131072 | tf_op jit(solution)/shard_map/all_to_all | solution.py:240
  39.6 13.8 %copy-start.2 = (bf16[4,8,2,16,128]{4,3,2,0,1:T(8,128)(2,1)}, bf16[4,8,2,16,128]{4,3,2,0,1:T(8,128)(2,1)S(1)}, u32[]{:S(2)}) copy-start(bf16[4,8,2,16,128]{4,3,2,0,1:T(8,128)(2,1)S(1)} %copy.17) | copy-start | bytes 786436
  39.6 6.3 %copy-start.8 = (s32[8192]{0:T(1024)S(1)}, s32[8192]{0:T(1024)}, u32[]{:S(2)}) copy-start(s32[8192]{0:T(1024)} %param.16) | copy-start | bytes 98308
  39.6 27.1 %copy-start.14 = (s32[64,64]{1,0:T(8,128)S(1)}, s32[64,64]{1,0:T(8,128)}, u32[]{:S(2)}) copy-start(s32[64,64]{1,0:T(8,128)} %param.17) | copy-start | bytes 49156
  39.7 25.0 %all-to-all-start.1 = ((bf16[16,17,16,128]{3,2,1,0:T(8,128)(2,1)}), bf16[16,17,16,128]{3,2,1,0:T(8,128)(2,1)S(1)}, u32[]{:S(2)}, u32[]{:S(2)}) async-start(bf16[16,17,16,128]{3,2,1,0:T(8,128)(2,1)} %shard_map.112), calls=%async_computation.1 | async-start | bytes 2228224 | tf_op jit(solution)/shard_map/all_to_all | solution.py:240
  46.3 18.3 %collective-permute-start.1 = (bf16[8,4,2,16,128]{4,3,2,1,0:T(8,128)(2,1)S(1)}, bf16[8,4,2,16,128]{4,3,2,1,0:T(8,128)(2,1)S(1)}, u32[]{:S(2)}, u32[]{:S(2)}) collective-permute-start(bf16[8,4,2,16,128]{4,3,2,1,0:T(8,128)(2,1)S(1)} %bitcast.7), channel_id=1, source_target_pairs={{0,1},{1,2},{2,3},{3,128},{128,129},{129,130},{130,131},{131,256},... | collective-permute-start | bytes 786440 | tf_op jit(solution)/shard_map/ppermute | solution.py:245
  48.8 15.9 %collective-permute-start = (bf16[8,4,2,16,128]{4,3,2,1,0:T(8,128)(2,1)S(1)}, bf16[8,4,2,16,128]{4,3,2,1,0:T(8,128)(2,1)S(1)}, u32[]{:S(2)}, u32[]{:S(2)}) collective-permute-start(bf16[8,4,2,16,128]{4,3,2,1,0:T(8,128)(2,1)S(1)} %bitcast.8), channel_id=1, source_target_pairs={{0,387},{1,0},{2,1},{3,2},{128,3},{129,128},{130,129},{131,130},{2... | collective-permute-start | bytes 786440 | tf_op jit(solution)/shard_map/ppermute | solution.py:245
  53.4 10.0 %collective-permute-start.3 = (bf16[4,4,2,16,128]{4,3,2,1,0:T(8,128)(2,1)S(1)}, bf16[4,4,2,16,128]{4,3,2,1,0:T(8,128)(2,1)S(1)}, u32[]{:S(2)}, u32[]{:S(2)}) collective-permute-start(bf16[4,4,2,16,128]{4,3,2,1,0:T(8,128)(2,1)S(1)} %get-tuple-element.37), channel_id=1, source_target_pairs={{0,2},{1,3},{2,128},{3,129},{128,130},{129,131},{130,256},{131,257... | collective-permute-start | bytes 393224 | tf_op jit(solution)/shard_map/ppermute | solution.py:245
  55.4 9.3 %collective-permute-start.2 = (bf16[4,4,2,16,128]{4,3,2,1,0:T(8,128)(2,1)S(1)}, bf16[4,4,2,16,128]{4,3,2,1,0:T(8,128)(2,1)S(1)}, u32[]{:S(2)}, u32[]{:S(2)}) collective-permute-start(bf16[4,4,2,16,128]{4,3,2,1,0:T(8,128)(2,1)S(1)} %get-tuple-element.38), channel_id=1, source_target_pairs={{0,386},{1,387},{2,0},{3,1},{128,2},{129,3},{130,128},{131,129},{2... | collective-permute-start | bytes 393224 | tf_op jit(solution)/shard_map/ppermute | solution.py:245
  63.5 5.9 %copy-start.6 = (bf16[4,4,2,16,128]{4,3,2,1,0:T(8,128)(2,1)}, bf16[4,4,2,16,128]{4,3,2,1,0:T(8,128)(2,1)S(1)}, u32[]{:S(2)}) copy-start(bf16[4,4,2,16,128]{4,3,2,1,0:T(8,128)(2,1)S(1)} %collective-permute-done.3.far_b_ref) | copy-start | bytes 393220
  64.6 4.7 %copy-start.7 = (bf16[4,4,2,16,128]{4,3,2,1,0:T(8,128)(2,1)}, bf16[4,4,2,16,128]{4,3,2,1,0:T(8,128)(2,1)S(1)}, u32[]{:S(2)}) copy-start(bf16[4,4,2,16,128]{4,3,2,1,0:T(8,128)(2,1)S(1)} %collective-permute-done.2.far_a_ref) | copy-start | bytes 393220
  64.7 4.7 %copy-start.4 = (bf16[8,4,2,16,128]{4,3,2,1,0:T(8,128)(2,1)}, bf16[8,4,2,16,128]{4,3,2,1,0:T(8,128)(2,1)S(1)}, u32[]{:S(2)}) copy-start(bf16[8,4,2,16,128]{4,3,2,1,0:T(8,128)(2,1)S(1)} %collective-permute-done.1.down_ref) | copy-start | bytes 786436
  64.7 4.7 %copy-start.5 = (bf16[8,4,2,16,128]{4,3,2,1,0:T(8,128)(2,1)}, bf16[8,4,2,16,128]{4,3,2,1,0:T(8,128)(2,1)S(1)}, u32[]{:S(2)}) copy-start(bf16[8,4,2,16,128]{4,3,2,1,0:T(8,128)(2,1)S(1)} %collective-permute-done.up_ref) | copy-start | bytes 786436
  64.7 4.7 %copy-start.1 = (bf16[16,17,16,128]{3,2,1,0:T(8,128)(2,1)}, bf16[16,17,16,128]{3,2,1,0:T(8,128)(2,1)S(1)}, u32[]{:S(2)}) copy-start(bf16[16,17,16,128]{3,2,1,0:T(8,128)(2,1)S(1)} %all-to-all-done.1.qa_ref) | copy-start | bytes 3342340
  64.7 4.6 %collective-permute-start.4 = (bf16[16,17,16,128]{3,2,1,0:T(8,128)(2,1)S(1)}, bf16[16,17,16,128]{3,2,1,0:T(8,128)(2,1)S(1)}, u32[]{:S(2)}, u32[]{:S(2)}) collective-permute-start(bf16[16,17,16,128]{3,2,1,0:T(8,128)(2,1)S(1)} %all-to-all-done.1.qa_ref), channel_id=1, source_target_pairs={{0,64},{64,0},{1,65},{65,1},{2,66},{66,2},{3,67},{67,3},{4,68},{68... | collective-permute-start | bytes 3342344 | tf_op jit(solution)/shard_map/ppermute | solution.py:319
  67.1 2.3 %copy-start.9 = (s32[16]{0:T(128)}, s32[16]{0:T(128)S(1)}, u32[]{:S(2)}) copy-start(s32[16]{0:T(128)S(1)} %convert_reduce_fusion.count_ref) | copy-start | bytes 196
  69.4 1.0 copy-start.3
  91.1 6.1 %copy-start.11 = (bf16[8,4,2,16,128]{4,3,2,1,0:T(8,128)(2,1)S(1)}, bf16[8,4,2,16,128]{4,3,2,1,0:T(8,128)(2,1)}, u32[]{:S(2)}) copy-start(bf16[8,4,2,16,128]{4,3,2,1,0:T(8,128)(2,1)} %get-tuple-element.27) | copy-start | bytes 786436
  91.1 8.2 %copy-start.10 = (bf16[8,4,2,16,128]{4,3,2,1,0:T(8,128)(2,1)S(1)}, bf16[8,4,2,16,128]{4,3,2,1,0:T(8,128)(2,1)}, u32[]{:S(2)}) copy-start(bf16[8,4,2,16,128]{4,3,2,1,0:T(8,128)(2,1)} %get-tuple-element.28) | copy-start | bytes 786436
  91.1 13.1 %copy-start.13 = (bf16[4,4,2,16,128]{4,3,2,1,0:T(8,128)(2,1)S(1)}, bf16[4,4,2,16,128]{4,3,2,1,0:T(8,128)(2,1)}, u32[]{:S(2)}) copy-start(bf16[4,4,2,16,128]{4,3,2,1,0:T(8,128)(2,1)} %get-tuple-element.29) | copy-start | bytes 393220
  91.1 17.5 %copy-start.12 = (bf16[4,4,2,16,128]{4,3,2,1,0:T(8,128)(2,1)S(1)}, bf16[4,4,2,16,128]{4,3,2,1,0:T(8,128)(2,1)}, u32[]{:S(2)}) copy-start(bf16[4,4,2,16,128]{4,3,2,1,0:T(8,128)(2,1)} %get-tuple-element.30) | copy-start | bytes 393220
  91.2 27.8 %copy-start = (bf16[8,4,2,16,128]{4,3,2,1,0:T(8,128)(2,1)S(1)}, bf16[8,4,2,16,128]{4,3,2,1,0:T(8,128)(2,1)}, u32[]{:S(2)}) copy-start(bf16[8,4,2,16,128]{4,3,2,1,0:T(8,128)(2,1)} %get-tuple-element.26.own_ref) | copy-start | bytes 786436
  91.2 28.7 %all-to-all-start.2 = ((bf16[32,128,128]{2,1,0:T(8,128)(2,1)}), bf16[32,128,128]{2,1,0:T(8,128)(2,1)S(1)}, u32[]{:S(2)}, u32[]{:S(2)}) async-start(bf16[32,128,128]{2,1,0:T(8,128)(2,1)} %bitcast.12), calls=%async_computation.2 | async-start | bytes 2097152 | tf_op jit(solution)/shard_map/all_to_all | solution.py:240
  97.2 21.8 %collective-permute-start.5 = (bf16[8,4,2,16,128]{4,3,2,1,0:T(8,128)(2,1)S(1)}, bf16[8,4,2,16,128]{4,3,2,1,0:T(8,128)(2,1)S(1)}, u32[]{:S(2)}, u32[]{:S(2)}) collective-permute-start(bf16[8,4,2,16,128]{4,3,2,1,0:T(8,128)(2,1)S(1)} %copy-done.11), channel_id=1, source_target_pairs={{0,1},{1,2},{2,3},{3,128},{128,129},{129,130},{130,131},{131,256},... | collective-permute-start | bytes 786440 | tf_op jit(solution)/shard_map/ppermute | solution.py:245
  99.3 19.6 %collective-permute-start.6 = (bf16[8,4,2,16,128]{4,3,2,1,0:T(8,128)(2,1)S(1)}, bf16[8,4,2,16,128]{4,3,2,1,0:T(8,128)(2,1)S(1)}, u32[]{:S(2)}, u32[]{:S(2)}) collective-permute-start(bf16[8,4,2,16,128]{4,3,2,1,0:T(8,128)(2,1)S(1)} %copy-done.10), channel_id=1, source_target_pairs={{0,387},{1,0},{2,1},{3,2},{128,3},{129,128},{130,129},{131,130},{2... | collective-permute-start | bytes 786440 | tf_op jit(solution)/shard_map/ppermute | solution.py:245
  104.3 10.3 %collective-permute-start.7 = (bf16[4,4,2,16,128]{4,3,2,1,0:T(8,128)(2,1)S(1)}, bf16[4,4,2,16,128]{4,3,2,1,0:T(8,128)(2,1)S(1)}, u32[]{:S(2)}, u32[]{:S(2)}) collective-permute-start(bf16[4,4,2,16,128]{4,3,2,1,0:T(8,128)(2,1)S(1)} %copy-done.13), channel_id=1, source_target_pairs={{0,2},{1,3},{2,128},{3,129},{128,130},{129,131},{130,256},{131,257... | collective-permute-start | bytes 393224 | tf_op jit(solution)/shard_map/ppermute | solution.py:245
  108.7 10.3 %collective-permute-start.8 = (bf16[4,4,2,16,128]{4,3,2,1,0:T(8,128)(2,1)S(1)}, bf16[4,4,2,16,128]{4,3,2,1,0:T(8,128)(2,1)S(1)}, u32[]{:S(2)}, u32[]{:S(2)}) collective-permute-start(bf16[4,4,2,16,128]{4,3,2,1,0:T(8,128)(2,1)S(1)} %copy-done.12), channel_id=1, source_target_pairs={{0,386},{1,387},{2,0},{3,1},{128,2},{129,3},{130,128},{131,129},{2... | collective-permute-start | bytes 393224 | tf_op jit(solution)/shard_map/ppermute | solution.py:245
  119.8 31.4 %all-to-all-start.3 = ((bf16[32,2,16,128]{3,2,1,0:T(8,128)(2,1)}), bf16[32,2,16,128]{3,2,1,0:T(8,128)(2,1)S(1)}, u32[]{:S(2)}, u32[]{:S(2)}) async-start(bf16[32,2,16,128]{3,2,1,0:T(8,128)(2,1)} %bitcast.4), calls=%async_computation.3 | async-start | bytes 524288 | tf_op jit(solution)/shard_map/all_to_all | solution.py:240
